TPU v7x, 32 devices: a whole 2x2x4 slice. The times are simulated.
32 devices in a mesh: gx: 16 (over z, y, core), gy: 2 (over x).
Axes of the slice: x: 2, y: 2, z: 4, core: 2. Of those that a mesh axis runs over, the one named last changes fastest.
Arguments:
- input_one: float32 [32, 2, 64, 256], P(None, None, 'gx', 'gy'), may hold values from -6 to 6
- input_two: float32 [32, 2, 64, 256], P(None, None, 'gx', 'gy'), may hold values from -6 to 6
- input_three: float32 [32, 2, 64, 256], P(None, None, 'gx', 'gy'), may hold values from -6 to 6
- cotangent: float32 [32, 2, 64, 256], P(None, None, 'gx', 'gy'), may hold values from -6 to 6
- kernel_one: float32 [27, 32, 32], replicated, may hold values from -0.21875 to 0.21875
- kernel_two: float32 [27, 32, 32], replicated, may hold values from -0.21875 to 0.21875
- kernel_three: float32 [27, 32, 32], replicated, may hold values from -0.21875 to 0.21875
Outputs:
- grad_input: float32 [32, 2, 64, 256], P(None, None, 'gx', 'gy')
- grad_kernel_one: float32 [27, 32, 32], replicated
- grad_kernel_two: float32 [27, 32, 32], replicated
- grad_kernel_three: float32 [27, 32, 32], replicated
All inputs are finite; a program needn't handle non-finite values.
Results may differ from a plain program's by a relative error of at most 0.00013.
Values sent between devices are 32-bit elements; how exact they have to be, the bound alone decides.
No kernel may reach another device: no remote copies, remote signals or barrier semaphores. Data moves between devices by JAX's collectives and lax.ppermute only.
A program may use at most 64 MiB of HBM per device.

v0:
```python
import math

import jax
import jax.numpy as jnp
from jax import lax
from jax.sharding import PartitionSpec as P

inv_root_two = 0.7071067811865476
inv_root_two_pi = 0.3989422804014327


def with_halo(value, sides, width):
    for axis, dim in sides:
        size, length = (lax.axis_size(axis), value.shape[dim])
        up = [(i, (i + 1) % size) for i in range(size - 1)]
        down = [(j, i) for i, j in up]
        last = lax.slice_in_dim(value, length - width, length, axis=dim)
        leading = lax.slice_in_dim(value, 0, width, axis=dim)
        before = lax.ppermute(last, axis, up)
        after = lax.ppermute(leading, axis, down)
        value = jnp.concatenate([before, value, after], axis=dim)
    return value


def gelu_slope(value):
    normal_cdf = 0.5 * (1.0 + jax.scipy.special.erf(value * inv_root_two))
    density = jnp.exp(-0.5 * value * value) * inv_root_two_pi
    return normal_cdf + value * density


def conv_taps(padded, kernel, depth, rows, cols):
    total = None
    for tap in range(27):
        a, b, c = (tap // 9, tap // 3 % 3, tap % 3)
        window = padded[:, a : a + depth, b : b + rows, c : c + cols]
        term = jnp.einsum("oi,izxy->ozxy", kernel[tap], window, precision=lax.Precision.HIGHEST)
        total = term if total is None else total + term
    return total


def back_taps(padded, kernel, depth, rows, cols):
    total = None
    for tap in range(27):
        a, b, c = (tap // 9, tap // 3 % 3, tap % 3)
        window = padded[:, 2 - a : 2 - a + depth, 2 - b : 2 - b + rows, 2 - c : 2 - c + cols]
        term = jnp.einsum("oi,ozxy->izxy", kernel[tap], window, precision=lax.Precision.HIGHEST)
        total = term if total is None else total + term
    return total


def kernel_terms(padded, slope_grad, depth, rows, cols):
    parts = []
    for tap in range(27):
        a, b, c = (tap // 9, tap // 3 % 3, tap % 3)
        window = padded[:, a : a + depth, b : b + rows, c : c + cols]
        parts.append(
            jnp.einsum("ozxy,izxy->oi", slope_grad, window, precision=lax.Precision.HIGHEST)
        )
    return jnp.stack(parts, axis=0)


def depth_pad(field):
    return jnp.pad(field, ((0, 0), (1, 1), (0, 0), (0, 0)))


def per_device(input_one, input_two, input_three, cotangent, kernel_one, kernel_two, kernel_three):
    depth, rows, cols = (input_one.shape[1], input_one.shape[2], input_one.shape[3])
    factor = 1.0 / math.sqrt(depth * rows * cols * lax.axis_size("gx") * lax.axis_size("gy"))
    fields = (input_three, input_two, input_one)
    kernels = (kernel_three, kernel_two, kernel_one)
    grad = cotangent
    results = []
    for layer in range(3):
        kernel = kernels[layer]
        padded = depth_pad(with_halo(fields[layer], (("gx", 2), ("gy", 3)), 1))
        pre = conv_taps(padded, kernel, depth, rows, cols)
        slope_grad = grad * gelu_slope(pre)
        terms = kernel_terms(padded, slope_grad, depth, rows, cols)
        results.append(lax.psum(terms, ("gx", "gy")) * factor)
        grad_padded = depth_pad(with_halo(slope_grad, (("gx", 2), ("gy", 3)), 1))
        grad = back_taps(grad_padded, kernel, depth, rows, cols)
    return (grad, results[2], results[1], results[0])


def solution(mesh):
    placed = (
        P(None, None, "gx", "gy"),
        P(None, None, "gx", "gy"),
        P(None, None, "gx", "gy"),
        P(None, None, "gx", "gy"),
        P(),
        P(),
        P(),
    )
    return jax.shard_map(
        per_device,
        mesh=mesh,
        in_specs=placed,
        out_specs=(P(None, None, "gx", "gy"), P(), P(), P()),
        check_vma=False,
    )
```

profile of v0, /device:TPU:0, one launch (start us, length us, event | category | flops | bytes accessed | tf_op | source)
XLA Modules:
  0.0 299.1 jit_solution(5990423751141898299)
XLA Ops:
  7.2 1.1 fusion.897
  8.3 2.4 collective-permute-start
  10.7 1.4 collective-permute-start.1
  12.2 5.2 %collective-permute-start.8 = (f32[32,2,1,128]{3,0,2,1:T(8,128)S(1)}, f32[32,2,1,128]{3,0,2,1:T(8,128)S(1)}, u32[]{:S(2)}, u32[]{:S(2)}) collective-permute-start(f32[32,2,1,128]{3,0,2,1:T(8,128)S(1)} %copy.940), channel_id=1, source_target_pairs={{0,2},{2,4},{4,6},{6,8},{8,10},{10,12},{12,14},{14,16},{16,18},{18... | collective-permute-start | bytes 98312 | tf_op jit(solution)/shard_map/ppermute | solution.py:19
  17.4 1.3 collective-permute-start.9
  18.8 4.4 %collective-permute-start.16 = (f32[32,2,1,128]{3,0,2,1:T(8,128)S(1)}, f32[32,2,1,128]{3,0,2,1:T(8,128)S(1)}, u32[]{:S(2)}, u32[]{:S(2)}) collective-permute-start(f32[32,2,1,128]{3,0,2,1:T(8,128)S(1)} %copy.942), channel_id=1, source_target_pairs={{0,2},{2,4},{4,6},{6,8},{8,10},{10,12},{12,14},{14,16},{16,18},{18... | collective-permute-start | bytes 98312 | tf_op jit(solution)/shard_map/ppermute | solution.py:19
  23.2 1.3 collective-permute-start.17
  24.7 3.4 %collective-permute-start.2 = (f32[32,2,6,1]{3,0,2,1:T(8,128)S(1)}, f32[32,2,6,1]{3,0,2,1:T(8,128)S(1)}, u32[]{:S(2)}, u32[]{:S(2)}) collective-permute-start(f32[32,2,6,1]{3,0,2,1:T(8,128)S(1)} %get-tuple-element.108), channel_id=1, source_target_pairs={{0,1},{2,3},{4,5},{6,7},{8,9},{10,11},{12,13},{14,15},{16,17},{18,... | collective-permute-start | bytes 4616 | tf_op jit(solution)/shard_map/ppermute | solution.py:19
  28.4 1.3 collective-permute-start.3
  30.2 4.6 %collective-permute-start.10 = (f32[32,2,6,1]{3,0,2,1:T(8,128)S(1)}, f32[32,2,6,1]{3,0,2,1:T(8,128)S(1)}, u32[]{:S(2)}, u32[]{:S(2)}) collective-permute-start(f32[32,2,6,1]{3,0,2,1:T(8,128)S(1)} %get-tuple-element.99), channel_id=1, source_target_pairs={{0,1},{2,3},{4,5},{6,7},{8,9},{10,11},{12,13},{14,15},{16,17},{18,... | collective-permute-start | bytes 4616 | tf_op jit(solution)/shard_map/ppermute | solution.py:19
  35.0 1.3 collective-permute-start.11
  36.8 4.6 %collective-permute-start.18 = (f32[32,2,6,1]{3,0,2,1:T(8,128)S(1)}, f32[32,2,6,1]{3,0,2,1:T(8,128)S(1)}, u32[]{:S(2)}, u32[]{:S(2)}) collective-permute-start(f32[32,2,6,1]{3,0,2,1:T(8,128)S(1)} %get-tuple-element.90), channel_id=1, source_target_pairs={{0,1},{2,3},{4,5},{6,7},{8,9},{10,11},{12,13},{14,15},{16,17},{18,... | collective-permute-start | bytes 4616 | tf_op jit(solution)/shard_map/ppermute | solution.py:19
  41.9 1.5 collective-permute-start.19
  44.0 0.5 fusion.883
  45.6 0.5 fusion.884
  48.6 0.4 pad_maximum_fusion.11
  53.1 0.5 copy-done.11
  53.6 0.4 fusion.214
  55.2 0.5 fusion.885
  62.8 0.4 pad_maximum_fusion.9
  63.7 0.5 fusion.76
  67.8 2.9 collective-permute-start.4
  70.7 1.3 collective-permute-start.5
  74.5 0.4 pad_maximum_fusion.7
  81.8 0.6 copy-done.6
  82.4 4.3 %collective-permute-start.6 = (f32[32,2,6,1]{3,0,2,1:T(8,128)S(1)}, f32[32,2,6,1]{3,0,2,1:T(8,128)S(1)}, u32[]{:S(2)}, u32[]{:S(2)}) collective-permute-start(f32[32,2,6,1]{3,0,2,1:T(8,128)S(1)} %get-tuple-element.104), channel_id=1, source_target_pairs={{0,1},{2,3},{4,5},{6,7},{8,9},{10,11},{12,13},{14,15},{16,17},{18,... | collective-permute-start | bytes 4616 | tf_op jit(solution)/shard_map/ppermute | solution.py:19
  86.7 1.7 collective-permute-start.7
  89.0 0.8 collective-permute-done.6
  89.8 4.4 %collective-permute-done.7 = f32[32,2,6,1]{3,0,2,1:T(8,128)S(1)} collective-permute-done((f32[32,2,6,1]{3,0,2,1:T(8,128)S(1)}, f32[32,2,6,1]{3,0,2,1:T(8,128)S(1)}, u32[]{:S(2)}, u32[]{:S(2)}) %collective-permute-start.7) | collective-permute-done | bytes 1568 | tf_op jit(solution)/shard_map/ppermute | solution.py:20
  96.4 0.4 convolution_add_fusion.49
  97.4 0.4 convolution_add_fusion.46
  98.1 0.4 convolution_add_fusion.44
  98.5 0.4 convolution_add_fusion.43
  99.2 0.4 fusion.67
  101.0 0.4 fusion.43
  101.3 0.4 fusion.42
  102.0 0.4 fusion.40
  108.0 4.5 %collective-permute-start.12 = (f32[32,2,1,128]{3,0,2,1:T(8,128)S(1)}, f32[32,2,1,128]{3,0,2,1:T(8,128)S(1)}, u32[]{:S(2)}, u32[]{:S(2)}) collective-permute-start(f32[32,2,1,128]{3,0,2,1:T(8,128)S(1)} %get-tuple-element.117), channel_id=1, source_target_pairs={{0,2},{2,4},{4,6},{6,8},{8,10},{10,12},{12,14},{14,16},{16,18},{18... | collective-permute-start | bytes 98312 | tf_op jit(solution)/shard_map/ppermute | solution.py:19
  112.5 1.3 collective-permute-start.13
  116.1 2.9 collective-permute-done.13
  119.1 1.5 collective-permute-start.14
  120.6 1.5 collective-permute-start.15
  122.7 1.3 collective-permute-done.14
  124.0 4.7 %collective-permute-done.15 = f32[32,2,6,1]{3,0,2,1:T(8,128)S(1)} collective-permute-done((f32[32,2,6,1]{3,0,2,1:T(8,128)S(1)}, f32[32,2,6,1]{3,0,2,1:T(8,128)S(1)}, u32[]{:S(2)}, u32[]{:S(2)}) %collective-permute-start.15) | collective-permute-done | bytes 1568 | tf_op jit(solution)/shard_map/ppermute | solution.py:20
  130.9 0.4 convolution_add_fusion.29
  131.6 0.4 convolution_add_fusion.27
  133.7 0.4 fusion.83
  136.5 0.4 fusion.21
  136.9 0.4 fusion.20
  142.4 3.3 %collective-permute-start.20 = (f32[32,2,1,128]{3,0,2,1:T(8,128)S(1)}, f32[32,2,1,128]{3,0,2,1:T(8,128)S(1)}, u32[]{:S(2)}, u32[]{:S(2)}) collective-permute-start(f32[32,2,1,128]{3,0,2,1:T(8,128)S(1)} %get-tuple-element.110), channel_id=1, source_target_pairs={{0,2},{2,4},{4,6},{6,8},{8,10},{10,12},{12,14},{14,16},{16,18},{18... | collective-permute-start | bytes 98312 | tf_op jit(solution)/shard_map/ppermute | solution.py:19
  145.8 1.3 collective-permute-start.21
  149.3 0.8 copy-done.8
  150.1 0.8 collective-permute-done.21
  151.1 1.5 collective-permute-start.22
  152.5 1.5 collective-permute-start.23
  154.7 1.0 collective-permute-done.22
  155.7 4.4 %collective-permute-done.23 = f32[32,2,6,1]{3,0,2,1:T(8,128)S(1)} collective-permute-done((f32[32,2,6,1]{3,0,2,1:T(8,128)S(1)}, f32[32,2,6,1]{3,0,2,1:T(8,128)S(1)}, u32[]{:S(2)}, u32[]{:S(2)}) %collective-permute-start.23) | collective-permute-done | bytes 1568 | tf_op jit(solution)/shard_map/ppermute | solution.py:20
  161.9 0.4 fusion.260
  165.1 0.4 fusion.99
  167.9 0.4 fusion.2
  168.9 0.7 copy.273
  169.7 119.4 %all-reduce.9.cloned.1.call-done = (f32[27,32,32]{2,1,0:T(8,128)}, f32[27,32,32]{2,1,0:T(8,128)}, f32[27,32,32]{2,1,0:T(8,128)}) async-done(((f32[27,32,32]{2,1,0:T(8,128)}, f32[27,32,32]{2,1,0:T(8,128)}, f32[27,32,32]{2,1,0:T(8,128)}), (f32[27,32,32]{2,1,0:T(8,128)}, f32[27,32,32]{2,1,0:T(8,128)}, f32[27,32,32]{2,1,0:T(8,128)})) %all-reduce.9.cloned.1.call-update) | async-done | bytes 331792 | tf_op jit(solution)/shard_map/psum | solution.py:79
  289.1 1.9 broadcast_multiply_fusion.2
  291.0 1.0 broadcast_multiply_fusion
  (302 shorter events, 67.4 us)
Async XLA Ops:
  7.2 5.0 %copy-start.4 = (f32[32,2,4,128]{3,2,1,0:T(4,128)S(1)}, f32[32,2,4,128]{3,2,1,0:T(4,128)}, u32[]{:S(2)}) copy-start(f32[32,2,4,128]{3,2,1,0:T(4,128)} %param.8) | copy-start | bytes 393220
  7.2 281.9 %all-reduce.9.cloned.1.call-start = ((), (), s32[]{:S(2)}) async-start(), calls=%async_computation | async-start | bytes 2654208 | tf_op jit(solution)/shard_map/psum | solution.py:79
  8.3 14.9 %collective-permute-start = (f32[32,2,1,128]{3,0,2,1:T(8,128)S(1)}, f32[32,2,1,128]{3,0,2,1:T(8,128)S(1)}, u32[]{:S(2)}, u32[]{:S(2)}) collective-permute-start(f32[32,2,1,128]{3,0,2,1:T(8,128)S(1)} %copy.938), channel_id=1, source_target_pairs={{0,2},{2,4},{4,6},{6,8},{8,10},{10,12},{12,14},{14,16},{16,18},{18... | collective-permute-start | bytes 98312 | tf_op jit(solution)/shard_map/ppermute | solution.py:19
  10.7 8.0 %copy-start.5 = (f32[32,2,4,128]{3,2,1,0:T(4,128)S(1)}, f32[32,2,4,128]{3,2,1,0:T(4,128)}, u32[]{:S(2)}) copy-start(f32[32,2,4,128]{3,2,1,0:T(4,128)} %param.7) | copy-start | bytes 393220
  10.7 13.9 %collective-permute-start.1 = (f32[32,2,1,128]{3,0,2,1:T(8,128)S(1)}, f32[32,2,1,128]{3,0,2,1:T(8,128)S(1)}, u32[]{:S(2)}, u32[]{:S(2)}) collective-permute-start(f32[32,2,1,128]{3,0,2,1:T(8,128)S(1)} %copy.939), channel_id=1, source_target_pairs={{2,0},{4,2},{6,4},{8,6},{10,8},{12,10},{14,12},{16,14},{18,16},{20... | collective-permute-start | bytes 98312 | tf_op jit(solution)/shard_map/ppermute | solution.py:20
  12.2 16.2 %collective-permute-start.8 = (f32[32,2,1,128]{3,0,2,1:T(8,128)S(1)}, f32[32,2,1,128]{3,0,2,1:T(8,128)S(1)}, u32[]{:S(2)}, u32[]{:S(2)}) collective-permute-start(f32[32,2,1,128]{3,0,2,1:T(8,128)S(1)} %copy.940), channel_id=1, source_target_pairs={{0,2},{2,4},{4,6},{6,8},{8,10},{10,12},{12,14},{14,16},{16,18},{18... | collective-permute-start | bytes 98312 | tf_op jit(solution)/shard_map/ppermute | solution.py:19
  17.4 12.7 %collective-permute-start.9 = (f32[32,2,1,128]{3,0,2,1:T(8,128)S(1)}, f32[32,2,1,128]{3,0,2,1:T(8,128)S(1)}, u32[]{:S(2)}, u32[]{:S(2)}) collective-permute-start(f32[32,2,1,128]{3,0,2,1:T(8,128)S(1)} %copy.941), channel_id=1, source_target_pairs={{2,0},{4,2},{6,4},{8,6},{10,8},{12,10},{14,12},{16,14},{18,16},{20... | collective-permute-start | bytes 98312 | tf_op jit(solution)/shard_map/ppermute | solution.py:20
  18.8 5.8 %copy-start.3 = (f32[32,2,4,128]{3,2,1,0:T(4,128)S(1)}, f32[32,2,4,128]{3,2,1,0:T(4,128)}, u32[]{:S(2)}) copy-start(f32[32,2,4,128]{3,2,1,0:T(4,128)} %param.9) | copy-start | bytes 393220
  18.8 16.3 %collective-permute-start.16 = (f32[32,2,1,128]{3,0,2,1:T(8,128)S(1)}, f32[32,2,1,128]{3,0,2,1:T(8,128)S(1)}, u32[]{:S(2)}, u32[]{:S(2)}) collective-permute-start(f32[32,2,1,128]{3,0,2,1:T(8,128)S(1)} %copy.942), channel_id=1, source_target_pairs={{0,2},{2,4},{4,6},{6,8},{8,10},{10,12},{12,14},{14,16},{16,18},{18... | collective-permute-start | bytes 98312 | tf_op jit(solution)/shard_map/ppermute | solution.py:19
  23.2 13.4 %collective-permute-start.17 = (f32[32,2,1,128]{3,0,2,1:T(8,128)S(1)}, f32[32,2,1,128]{3,0,2,1:T(8,128)S(1)}, u32[]{:S(2)}, u32[]{:S(2)}) collective-permute-start(f32[32,2,1,128]{3,0,2,1:T(8,128)S(1)} %copy.943), channel_id=1, source_target_pairs={{2,0},{4,2},{6,4},{8,6},{10,8},{12,10},{14,12},{16,14},{18,16},{20... | collective-permute-start | bytes 98312 | tf_op jit(solution)/shard_map/ppermute | solution.py:20
  24.6 3.6 %copy-start = (f32[27,32,32]{2,1,0:T(8,128)S(1)}, f32[27,32,32]{2,1,0:T(8,128)}, u32[]{:S(2)}) copy-start(f32[27,32,32]{2,1,0:T(8,128)} %param.13) | copy-start | bytes 331780
  24.7 17.2 %collective-permute-start.2 = (f32[32,2,6,1]{3,0,2,1:T(8,128)S(1)}, f32[32,2,6,1]{3,0,2,1:T(8,128)S(1)}, u32[]{:S(2)}, u32[]{:S(2)}) collective-permute-start(f32[32,2,6,1]{3,0,2,1:T(8,128)S(1)} %get-tuple-element.108), channel_id=1, source_target_pairs={{0,1},{2,3},{4,5},{6,7},{8,9},{10,11},{12,13},{14,15},{16,17},{18,... | collective-permute-start | bytes 4616 | tf_op jit(solution)/shard_map/ppermute | solution.py:19
  28.4 15.0 %collective-permute-start.3 = (f32[32,2,6,1]{3,0,2,1:T(8,128)S(1)}, f32[32,2,6,1]{3,0,2,1:T(8,128)S(1)}, u32[]{:S(2)}, u32[]{:S(2)}) collective-permute-start(f32[32,2,6,1]{3,0,2,1:T(8,128)S(1)} %get-tuple-element.109), channel_id=1, source_target_pairs={{1,0},{3,2},{5,4},{7,6},{9,8},{11,10},{13,12},{15,14},{17,16},{19,... | collective-permute-start | bytes 4616 | tf_op jit(solution)/shard_map/ppermute | solution.py:20
  30.1 4.7 %copy-start.1 = (f32[27,32,32]{2,1,0:T(8,128)S(1)}, f32[27,32,32]{2,1,0:T(8,128)}, u32[]{:S(2)}) copy-start(f32[27,32,32]{2,1,0:T(8,128)} %param.12) | copy-start | bytes 331780
  30.2 14.6 %collective-permute-start.10 = (f32[32,2,6,1]{3,0,2,1:T(8,128)S(1)}, f32[32,2,6,1]{3,0,2,1:T(8,128)S(1)}, u32[]{:S(2)}, u32[]{:S(2)}) collective-permute-start(f32[32,2,6,1]{3,0,2,1:T(8,128)S(1)} %get-tuple-element.99), channel_id=1, source_target_pairs={{0,1},{2,3},{4,5},{6,7},{8,9},{10,11},{12,13},{14,15},{16,17},{18,... | collective-permute-start | bytes 4616 | tf_op jit(solution)/shard_map/ppermute | solution.py:19
  35.0 9.7 %collective-permute-start.11 = (f32[32,2,6,1]{3,0,2,1:T(8,128)S(1)}, f32[32,2,6,1]{3,0,2,1:T(8,128)S(1)}, u32[]{:S(2)}, u32[]{:S(2)}) collective-permute-start(f32[32,2,6,1]{3,0,2,1:T(8,128)S(1)} %get-tuple-element.100), channel_id=1, source_target_pairs={{1,0},{3,2},{5,4},{7,6},{9,8},{11,10},{13,12},{15,14},{17,16},{19,... | collective-permute-start | bytes 4616 | tf_op jit(solution)/shard_map/ppermute | solution.py:20
  36.7 4.7 %copy-start.2 = (f32[27,32,32]{2,1,0:T(8,128)S(1)}, f32[27,32,32]{2,1,0:T(8,128)}, u32[]{:S(2)}) copy-start(f32[27,32,32]{2,1,0:T(8,128)} %param.11) | copy-start | bytes 331780
  36.8 17.6 %collective-permute-start.18 = (f32[32,2,6,1]{3,0,2,1:T(8,128)S(1)}, f32[32,2,6,1]{3,0,2,1:T(8,128)S(1)}, u32[]{:S(2)}, u32[]{:S(2)}) collective-permute-start(f32[32,2,6,1]{3,0,2,1:T(8,128)S(1)} %get-tuple-element.90), channel_id=1, source_target_pairs={{0,1},{2,3},{4,5},{6,7},{8,9},{10,11},{12,13},{14,15},{16,17},{18,... | collective-permute-start | bytes 4616 | tf_op jit(solution)/shard_map/ppermute | solution.py:19
  41.9 12.5 %collective-permute-start.19 = (f32[32,2,6,1]{3,0,2,1:T(8,128)S(1)}, f32[32,2,6,1]{3,0,2,1:T(8,128)S(1)}, u32[]{:S(2)}, u32[]{:S(2)}) collective-permute-start(f32[32,2,6,1]{3,0,2,1:T(8,128)S(1)} %get-tuple-element.91), channel_id=1, source_target_pairs={{1,0},{3,2},{5,4},{7,6},{9,8},{11,10},{13,12},{15,14},{17,16},{19,... | collective-permute-start | bytes 4616 | tf_op jit(solution)/shard_map/ppermute | solution.py:20
  52.7 0.9 copy-start.11
  67.8 13.8 %collective-permute-start.4 = (f32[32,2,1,128]{3,0,2,1:T(8,128)S(1)}, f32[32,2,1,128]{3,0,2,1:T(8,128)S(1)}, u32[]{:S(2)}, u32[]{:S(2)}) collective-permute-start(f32[32,2,1,128]{3,0,2,1:T(8,128)S(1)} %get-tuple-element.124), channel_id=1, source_target_pairs={{0,2},{2,4},{4,6},{6,8},{8,10},{10,12},{12,14},{14,16},{16,18},{18... | collective-permute-start | bytes 98312 | tf_op jit(solution)/shard_map/ppermute | solution.py:19
  70.7 10.9 %collective-permute-start.5 = (f32[32,2,1,128]{3,0,2,1:T(8,128)S(1)}, f32[32,2,1,128]{3,0,2,1:T(8,128)S(1)}, u32[]{:S(2)}, u32[]{:S(2)}) collective-permute-start(f32[32,2,1,128]{3,0,2,1:T(8,128)S(1)} %get-tuple-element.125), channel_id=1, source_target_pairs={{2,0},{4,2},{6,4},{8,6},{10,8},{12,10},{14,12},{16,14},{18,16},{20... | collective-permute-start | bytes 98312 | tf_op jit(solution)/shard_map/ppermute | solution.py:20
  81.6 0.8 copy-start.6
  82.4 7.4 %collective-permute-start.6 = (f32[32,2,6,1]{3,0,2,1:T(8,128)S(1)}, f32[32,2,6,1]{3,0,2,1:T(8,128)S(1)}, u32[]{:S(2)}, u32[]{:S(2)}) collective-permute-start(f32[32,2,6,1]{3,0,2,1:T(8,128)S(1)} %get-tuple-element.104), channel_id=1, source_target_pairs={{0,1},{2,3},{4,5},{6,7},{8,9},{10,11},{12,13},{14,15},{16,17},{18,... | collective-permute-start | bytes 4616 | tf_op jit(solution)/shard_map/ppermute | solution.py:19
  86.7 7.6 %collective-permute-start.7 = (f32[32,2,6,1]{3,0,2,1:T(8,128)S(1)}, f32[32,2,6,1]{3,0,2,1:T(8,128)S(1)}, u32[]{:S(2)}, u32[]{:S(2)}) collective-permute-start(f32[32,2,6,1]{3,0,2,1:T(8,128)S(1)} %get-tuple-element.103), channel_id=1, source_target_pairs={{1,0},{3,2},{5,4},{7,6},{9,8},{11,10},{13,12},{15,14},{17,16},{19,... | collective-permute-start | bytes 4616 | tf_op jit(solution)/shard_map/ppermute | solution.py:20
  108.0 8.1 %collective-permute-start.12 = (f32[32,2,1,128]{3,0,2,1:T(8,128)S(1)}, f32[32,2,1,128]{3,0,2,1:T(8,128)S(1)}, u32[]{:S(2)}, u32[]{:S(2)}) collective-permute-start(f32[32,2,1,128]{3,0,2,1:T(8,128)S(1)} %get-tuple-element.117), channel_id=1, source_target_pairs={{0,2},{2,4},{4,6},{6,8},{8,10},{10,12},{12,14},{14,16},{16,18},{18... | collective-permute-start | bytes 98312 | tf_op jit(solution)/shard_map/ppermute | solution.py:19
  112.5 6.5 %collective-permute-start.13 = (f32[32,2,1,128]{3,0,2,1:T(8,128)S(1)}, f32[32,2,1,128]{3,0,2,1:T(8,128)S(1)}, u32[]{:S(2)}, u32[]{:S(2)}) collective-permute-start(f32[32,2,1,128]{3,0,2,1:T(8,128)S(1)} %get-tuple-element.118), channel_id=1, source_target_pairs={{2,0},{4,2},{6,4},{8,6},{10,8},{12,10},{14,12},{16,14},{18,16},{20... | collective-permute-start | bytes 98312 | tf_op jit(solution)/shard_map/ppermute | solution.py:20
  116.0 3.1 %copy-start.7 = (f32[27,32,32]{2,1,0:T(8,128)}, f32[27,32,32]{2,1,0:T(8,128)S(1)}, u32[]{:S(2)}) copy-start(f32[27,32,32]{2,1,0:T(8,128)S(1)} %fusion.131) | copy-start | bytes 331780
  119.1 4.9 %collective-permute-start.14 = (f32[32,2,6,1]{3,0,2,1:T(8,128)S(1)}, f32[32,2,6,1]{3,0,2,1:T(8,128)S(1)}, u32[]{:S(2)}, u32[]{:S(2)}) collective-permute-start(f32[32,2,6,1]{3,0,2,1:T(8,128)S(1)} %get-tuple-element.95), channel_id=1, source_target_pairs={{0,1},{2,3},{4,5},{6,7},{8,9},{10,11},{12,13},{14,15},{16,17},{18,... | collective-permute-start | bytes 4616 | tf_op jit(solution)/shard_map/ppermute | solution.py:19
  120.6 8.1 %collective-permute-start.15 = (f32[32,2,6,1]{3,0,2,1:T(8,128)S(1)}, f32[32,2,6,1]{3,0,2,1:T(8,128)S(1)}, u32[]{:S(2)}, u32[]{:S(2)}) collective-permute-start(f32[32,2,6,1]{3,0,2,1:T(8,128)S(1)} %get-tuple-element.94), channel_id=1, source_target_pairs={{1,0},{3,2},{5,4},{7,6},{9,8},{11,10},{13,12},{15,14},{17,16},{19,... | collective-permute-start | bytes 4616 | tf_op jit(solution)/shard_map/ppermute | solution.py:20
  142.4 7.7 %collective-permute-start.20 = (f32[32,2,1,128]{3,0,2,1:T(8,128)S(1)}, f32[32,2,1,128]{3,0,2,1:T(8,128)S(1)}, u32[]{:S(2)}, u32[]{:S(2)}) collective-permute-start(f32[32,2,1,128]{3,0,2,1:T(8,128)S(1)} %get-tuple-element.110), channel_id=1, source_target_pairs={{0,2},{2,4},{4,6},{6,8},{8,10},{10,12},{12,14},{14,16},{16,18},{18... | collective-permute-start | bytes 98312 | tf_op jit(solution)/shard_map/ppermute | solution.py:19
  145.8 5.2 %collective-permute-start.21 = (f32[32,2,1,128]{3,0,2,1:T(8,128)S(1)}, f32[32,2,1,128]{3,0,2,1:T(8,128)S(1)}, u32[]{:S(2)}, u32[]{:S(2)}) collective-permute-start(f32[32,2,1,128]{3,0,2,1:T(8,128)S(1)} %get-tuple-element.111), channel_id=1, source_target_pairs={{2,0},{4,2},{6,4},{8,6},{10,8},{12,10},{14,12},{16,14},{18,16},{20... | collective-permute-start | bytes 98312 | tf_op jit(solution)/shard_map/ppermute | solution.py:20
  149.3 0.8 copy-start.8
  151.1 4.6 %collective-permute-start.22 = (f32[32,2,6,1]{3,0,2,1:T(8,128)S(1)}, f32[32,2,6,1]{3,0,2,1:T(8,128)S(1)}, u32[]{:S(2)}, u32[]{:S(2)}) collective-permute-start(f32[32,2,6,1]{3,0,2,1:T(8,128)S(1)} %get-tuple-element.86), channel_id=1, source_target_pairs={{0,1},{2,3},{4,5},{6,7},{8,9},{10,11},{12,13},{14,15},{16,17},{18,... | collective-permute-start | bytes 4616 | tf_op jit(solution)/shard_map/ppermute | solution.py:19
  152.5 7.6 %collective-permute-start.23 = (f32[32,2,6,1]{3,0,2,1:T(8,128)S(1)}, f32[32,2,6,1]{3,0,2,1:T(8,128)S(1)}, u32[]{:S(2)}, u32[]{:S(2)}) collective-permute-start(f32[32,2,6,1]{3,0,2,1:T(8,128)S(1)} %get-tuple-element.85), channel_id=1, source_target_pairs={{1,0},{3,2},{5,4},{7,6},{9,8},{11,10},{13,12},{15,14},{17,16},{19,... | collective-permute-start | bytes 4616 | tf_op jit(solution)/shard_map/ppermute | solution.py:20
  289.1 1.9 copy-start.9
  289.1 1.9 copy-start.10
Sparse Core Ops, SparseCore 0:
  150.2 138.7 all-reduce.8
where the time goes:
time: 303 us; the launch traced here: 299 us
  waiting for transfers between devices  140 us (46%)
  matrix products  71 us (23%)
  starting transfers between devices  59 us (19%)
  between operations  17 us (6%)
  local copies, waits for them, and re-layouts  6.29 us (2%)
  other arithmetic  5.93 us (2%)
    psum x1, waiting for transfers between devices, per_device(): results.append(lax.psum(terms, ('gx', 'gy')) * factor)  119 us
    ppermute x12, starting transfers between devices, with_halo(): before = lax.ppermute(last, axis, up)  42.4 us
    dot_general x81, matrix products, back_taps(): jnp.einsum('oi,ozxy->izxy', kernel[tap], window, precision=lax.Precision....  27.5 us
    dot_general x81, matrix products, conv_taps(): jnp.einsum('oi,izxy->ozxy', kernel[tap], window, precision=lax.Precision....  23.8 us
    dot_general x81, matrix products, kernel_terms(): jnp.einsum('ozxy,izxy->oi', slope_grad, window, precision=lax.Precision.H...  19.7 us
    ppermute x12, waiting for transfers between devices, with_halo(): after = lax.ppermute(leading, axis, down)  17.2 us
    ppermute x12, starting transfers between devices, with_halo(): after = lax.ppermute(leading, axis, down)  16.6 us
  transfers between devices with their start and end apart: 25, of which 9 were waited for; matrix products, arithmetic and copies ran while one was open for 12% of the time, Pallas kernels for 0%

commit v1 on v0

v1 whole, which is shorter than its diff:
```python
import functools
import math

import jax
import jax.numpy as jnp
from jax import lax
from jax.experimental import pallas as pl
from jax.experimental.pallas import tpu as pltpu
from jax.sharding import PartitionSpec as P

inv_root_two = 0.7071067811865476
inv_root_two_pi = 0.3989422804014327

LAYERS = 3
HALO = LAYERS + 1
SIDE = 2 * HALO
LANES = 128
F32 = jnp.float32
BF16 = jnp.bfloat16
NN = (((1,), (0,)), ((), ()))
NT = (((1,), (1,)), ((), ()))

WIDTHS = (HALO, HALO - 1, HALO - 1, HALO - 2)
STARTS = tuple(sum(WIDTHS[:f]) for f in range(4))
SLABS = sum(WIDTHS)


def gelu_slope(value):
    normal_cdf = 0.5 * (1.0 + lax.erf(value * inv_root_two))
    density = jnp.exp(-0.5 * value * value) * inv_root_two_pi
    return normal_cdf + value * density


def roll(value, shift):
    shift %= LANES
    return pltpu.roll(value, shift, 1) if shift else value


def lane_index(rows):
    return lax.broadcasted_iota(jnp.int32, (rows, LANES), 1)


def vmem(count):
    return [pl.BlockSpec(memory_space=pltpu.VMEM)] * count


def slab_at(ref, depth, rows, row):
    channels = ref.shape[0] // (depth * rows)
    parts = [ref[pl.ds(z * rows + row, channels, stride=depth * rows), :] for z in range(depth)]
    return jnp.concatenate(parts, axis=0)


def split(value):
    high = value.astype(BF16)
    low = (value - high.astype(F32)).astype(BF16)
    return high, low


def pack_kernel(depth, rows, *refs):
    fields, (inner, outer, strip) = refs[:4], refs[4:]
    odd = lax.rem(lax.axis_index("gx"), 2)
    planes = fields[0].shape[0] // rows
    lane = lane_index(planes)
    total = jnp.zeros((planes, LANES), F32)
    for f, ref in enumerate(fields):
        width = WIDTHS[f]
        for j in range(width):
            at = pl.ds((STARTS[f] + j) * planes, planes)
            inner[at, :] = slab_at(ref, depth, rows, (rows - width) * (1 - odd) + j)
            outer[at, :] = slab_at(ref, depth, rows, (rows - width) * odd + j)
        for r in range(rows):
            value = slab_at(ref, depth, rows, r)
            base = (f * rows + r) * SIDE
            first = (lane >= base) & (lane < base + HALO)
            last = (lane >= base + HALO) & (lane < base + SIDE)
            total = jnp.where(first, roll(value, base), total)
            total = jnp.where(last, roll(value, base + SIDE), total)
    strip[...] = total


def weight_kernel(channels, depth, *refs):
    kernels, (forward, backward) = refs[:LAYERS], refs[LAYERS:]
    planes = channels * depth
    in_low = lax.rem(lane_index(channels), planes) < channels
    for layer in range(LAYERS):
        for b in range(3):
            for c in range(3):
                tiles = []
                for a in range(3):
                    tap = kernels[layer][9 * a + 3 * b + c]
                    tiles.append(jnp.concatenate([tap] * (LANES // channels), axis=1))
                upper = jnp.where(in_low, tiles[1], tiles[2])
                lower = jnp.where(in_low, tiles[0], tiles[1])
                whole = jnp.concatenate([upper, lower], axis=0)
                turned = jnp.concatenate([whole, whole], axis=0).T[:planes]
                for ref, value, bb, cc in ((forward, whole, b, c), (backward, turned, 2 - b, 2 - c)):
                    base = (layer * 3 + bb) * 2 * planes
                    high, low = split(value)
                    ref[pl.ds(base, planes), pl.ds(cc * LANES, LANES)] = high
                    ref[pl.ds(base + planes, planes), pl.ds(cc * LANES, LANES)] = low


def main_kernel(depth, rows, channels, gy_rounds, factor, *refs):
    fields = refs[:4]
    inner, outer = refs[4:6]
    strips = refs[6 : 6 + 3 * gy_rounds]
    rest = refs[6 + 3 * gy_rounds :]
    forward, backward, grad_out, keep, send, xs, xside, hs, hside, gsum = rest
    planes = depth * channels
    gx, gy = lax.axis_index("gx"), lax.axis_index("gy")
    gx_size, gy_size = lax.axis_size("gx"), lax.axis_size("gy")
    x_odd, y_odd = lax.rem(gx, 2) == 1, lax.rem(gy, 2) == 1
    lane = lane_index(planes)
    place = lax.rem(lane, SIDE)
    right = place < HALO
    zero = jnp.zeros((planes, LANES), F32)

    def side_strip(group):
        got = [strips[group * gy_rounds + r][...] for r in range(gy_rounds)]
        if gy_rounds == 0:
            return zero
        if gy_rounds == 1:
            got.append(zero)
        from_right = jnp.where(y_odd, got[1], got[0])
        from_left = jnp.where(y_odd, got[0], got[1])
        return jnp.where(right, from_right, from_left)

    own_strip, inner_strip, outer_strip = (side_strip(g) for g in range(3))
    before_strip = jnp.where(x_odd, inner_strip, outer_strip)
    after_strip = jnp.where(x_odd, outer_strip, inner_strip)
    span = rows * SIDE

    def field_parts(f):
        width = WIDTHS[f]
        main = {}
        for j in range(width):
            at = pl.ds((STARTS[f] + j) * planes, planes)
            a, b = inner[at, :], outer[at, :]
            main[HALO - width + j] = jnp.where(x_odd, a, b)
            main[HALO + rows + j] = jnp.where(x_odd, b, a)
        for r in range(rows):
            main[HALO + r] = slab_at(fields[f], depth, rows, r)
        lead = HALO * SIDE
        before = roll(before_strip, lead - span - f * span)
        own = roll(own_strip, lead - f * span)
        after = roll(after_strip, lead + span - f * span)
        side = jnp.where(lane < lead, before, jnp.where(lane < lead + span, own, after))
        side = jnp.where(lane < lead + 2 * span, side, 0.0)
        side = jnp.where(lane >= lead - span, side, 0.0)
        return main, side

    def store_shifted(main, side, into, into_side):
        side_up, side_down = roll(side, -1), roll(side, 1)
        for e, value in main.items():
            base = e * SIDE
            down = jnp.where(lane == 0, roll(side, -(base + SIDE - 1)), roll(value, 1))
            up = jnp.where(lane == LANES - 1, roll(side, LANES - 1 - base), roll(value, -1))
            side_up = jnp.where(lane == base + SIDE - 1, roll(value, base + SIDE - 1), side_up)
            side_down = jnp.where(lane == base, roll(value, base + 1), side_down)
            for c, shifted in enumerate((down, value, up)):
                high, low = split(shifted)
                into[pl.ds(c * LANES, planes), pl.ds(e * LANES, LANES)] = high
                into[pl.ds(c * LANES + planes, planes), pl.ds(e * LANES, LANES)] = low
        for c, shifted in enumerate((side_down, side, side_up)):
            for b in range(3):
                high, low = split(roll(shifted, -(b - 1) * SIDE))
                base = (b * 3 + c) * LANES
                into_side[pl.ds(base, planes), :] = high
                into_side[pl.ds(base + planes, planes), :] = low

    def conv(weights, layer, source, lane_start, count):
        total = None
        for b in range(3):
            kernel = weights[pl.ds((layer * 3 + b) * 2 * planes, 2 * planes), :]
            window = source[:, pl.ds(lane_start + (b - 1) * LANES, count * LANES)]
            term = lax.dot_general(kernel, window, NN, preferred_element_type=F32)
            total = term if total is None else total + term
        return total[:planes] + total[planes:]

    def conv_side(weights, layer, source):
        total = None
        for b in range(3):
            kernel = weights[pl.ds((layer * 3 + b) * 2 * planes, 2 * planes), :]
            window = source[pl.ds(b * 3 * LANES, 3 * LANES), :]
            term = lax.dot_general(kernel, window, NN, preferred_element_type=F32)
            total = term if total is None else total + term
        return total[:planes] + total[planes:]

    def conv_rows(weights, layer, source, low, high):
        out = {}
        for e in range(low, high, 2):
            count = min(2, high - e)
            value = conv(weights, layer, source, e * LANES, count)
            for k in range(count):
                out[e + k] = value[:, k * LANES : (k + 1) * LANES]
        return out

    side_row = lane // SIDE
    row_low = jnp.where(gx > 0, 0, HALO)
    row_high = jnp.where(gx < gx_size - 1, 2 * HALO + rows, HALO + rows)
    col_ok = jnp.where(right, (gy < gy_size - 1).astype(jnp.int32), (gy > 0).astype(jnp.int32))
    side_ok = (side_row >= row_low) & (side_row < row_high) & (col_ok > 0)

    grad_main, grad_side = field_parts(1)
    half = lane_index(channels)
    for layer in range(LAYERS):
        x_main, x_side = field_parts((0, 2, 3)[layer])
        store_shifted(x_main, x_side, xs, xside)
        h_width = LAYERS - layer
        low, high = HALO - h_width, HALO + rows + h_width
        pre = conv_rows(forward, layer, xs, low, high)
        h_main = {}
        for e in range(low, high):
            value = grad_main[e] * gelu_slope(pre[e])
            if e < HALO:
                value = jnp.where(gx > 0, value, 0.0)
            if e >= HALO + rows:
                value = jnp.where(gx < gx_size - 1, value, 0.0)
            h_main[e] = value
        h_side = jnp.where(side_ok, grad_side * gelu_slope(conv_side(forward, layer, xside)), 0.0)
        store_shifted(h_main, h_side, hs, hside)

        own = hs[pl.ds(LANES, 2 * planes), pl.ds(HALO * LANES, rows * LANES)]
        tiles, extra = [], []
        for b in range(3):
            window = xs[:, pl.ds((HALO + b - 1) * LANES, rows * LANES)]
            product = lax.dot_general(own, window, NT, preferred_element_type=F32)
            product = product[:planes] + product[planes:]
            for c in range(3):
                tile = product[:, c * LANES : (c + 1) * LANES]
                tile = (tile + roll(tile, planes)) * factor
                upper, lower = tile[:channels], tile[channels:]
                middle = upper + roll(lower, -channels)
                tiles.append(jnp.where(half < channels, lower, jnp.where(half < 2 * channels, upper, middle)))
        for m in range(7):
            tile = tiles[m]
            if m < 6:
                source, part = tiles[7 + m // 3], m % 3
                tile = jnp.where(half < 3 * channels, tile, roll(source, (3 - part) * channels))
            gsum[pl.ds((layer * 7 + m) * channels, channels), :] = tile

        g_width = h_width - 1
        grad_main = conv_rows(backward, layer, hs, HALO - g_width, HALO + rows + g_width)
        if g_width:
            grad_side = conv_side(backward, layer, hside)

    for r in range(rows):
        for z in range(depth):
            at = pl.ds(z * rows + r, channels, stride=depth * rows)
            grad_out[at, :] = grad_main[HALO + r][z * channels : (z + 1) * channels]
    size = keep.shape[0]
    mine = pl.multiple_of(lax.rem(gx, 2) * size, 8)
    other = pl.multiple_of((1 - lax.rem(gx, 2)) * size, 8)
    keep[...] = gsum[pl.ds(mine, size), :]
    send[...] = gsum[pl.ds(other, size), :]


def unpack_kernel(channels, mine, other, *refs):
    outs, whole = refs[:LAYERS], refs[LAYERS]
    size = mine.shape[0]
    odd = lax.rem(lax.axis_index("gx"), 2)
    whole[pl.ds(pl.multiple_of(odd * size, 8), size), :] = mine[...]
    whole[pl.ds(pl.multiple_of((1 - odd) * size, 8), size), :] = other[...]
    order = (0, 2, 1)
    for layer in range(LAYERS):
        for m in range(7):
            tile = whole[pl.ds((layer * 7 + m) * channels, channels), :]
            for s in range(4):
                if s < 3:
                    tap = 9 * order[s] + m
                elif m < 6:
                    tap = 9 * order[m % 3] + 7 + m // 3
                else:
                    continue
                outs[layer][tap] = roll(tile, -s * channels)[:, :channels]


def pair_rounds(size):
    rounds = []
    for start in range(2):
        pairs = [(i, i + 1) for i in range(start, size - 1, 2)]
        if pairs:
            rounds.append(pairs + [(j, i) for i, j in pairs])
    return rounds


def reduce_halves(keep, send, gx_size, gy_size):
    axes = ("gx", "gy")
    total = gx_size * gy_size
    gx, gy = lax.axis_index("gx"), lax.axis_index("gy")

    def swap(value, bit):
        return lax.ppermute(value, axes, [(i, i ^ bit) for i in range(total)])

    value = keep + swap(send, gy_size)
    size = value.shape[0] // 2
    split_at = gy_size > 1
    bits = [1 << k for k in range(1, gy_size.bit_length() - 1)]
    bits += [gy_size << k for k in range(1, gx_size.bit_length() - 1)]
    if split_at:
        side = gy & 1
        mine = lax.dynamic_slice_in_dim(value, side * size, size, axis=0)
        other = lax.dynamic_slice_in_dim(value, (1 - side) * size, size, axis=0)
        value = mine + swap(other, 1)
    for bit in bits:
        value = value + swap(value, bit)
    if split_at:
        got = swap(value, 1)
        value = jnp.where(side == 0, jnp.concatenate([value, got]), jnp.concatenate([got, value]))
    return value, swap(value, gy_size)


def per_device(input_one, input_two, input_three, cotangent, kernel_one, kernel_two, kernel_three):
    channels, depth, rows, cols = input_one.shape
    gx_size, gy_size = lax.axis_size("gx"), lax.axis_size("gy")
    planes = channels * depth
    factor = 1.0 / math.sqrt(depth * rows * cols * gx_size * gy_size)
    fields = [v.reshape(planes * rows, cols) for v in (input_three, cotangent, input_two, input_one)]
    shape = jax.ShapeDtypeStruct

    inner, outer, strip = pl.pallas_call(
        functools.partial(pack_kernel, depth, rows),
        out_shape=[
            shape((SLABS * planes, cols), F32),
            shape((SLABS * planes, cols), F32),
            shape((planes, cols), F32),
        ],
        in_specs=vmem(4),
        out_specs=vmem(3),
        name="pack",
    )(*fields)

    x_rounds, y_rounds = pair_rounds(gx_size), pair_rounds(gy_size)
    both = ("gx", "gy")

    def diagonal(x_pairs, y_pairs):
        return [(i * gy_size + k, j * gy_size + m) for i, j in x_pairs for k, m in y_pairs]

    outer = lax.ppermute(outer, "gx", x_rounds[1])
    strips_own = [lax.ppermute(strip, "gy", pairs) for pairs in y_rounds]
    strips_outer = [lax.ppermute(strip, both, diagonal(x_rounds[1], pairs)) for pairs in y_rounds]
    inner = lax.ppermute(inner, "gx", x_rounds[0])
    strips_inner = [lax.ppermute(strip, both, diagonal(x_rounds[0], pairs)) for pairs in y_rounds]
    strips = strips_own + strips_inner + strips_outer

    weight_shape = shape((LAYERS * 3 * 2 * planes, 3 * LANES), BF16)
    forward, backward = pl.pallas_call(
        functools.partial(weight_kernel, channels, depth),
        out_shape=[weight_shape, weight_shape],
        in_specs=vmem(LAYERS),
        out_specs=vmem(2),
        cost_estimate=pl.CostEstimate(flops=20_000_000, bytes_accessed=4_000_000, transcendentals=0),
        name="weights",
    )(kernel_three, kernel_two, kernel_one)

    total_rows = LAYERS * 7 * channels
    span = (2 * HALO + rows) * LANES
    grad, keep, send = pl.pallas_call(
        functools.partial(main_kernel, depth, rows, channels, len(y_rounds), factor),
        out_shape=[
            shape((planes * rows, cols), F32),
            shape((total_rows // 2, LANES), F32),
            shape((total_rows // 2, LANES), F32),
        ],
        in_specs=vmem(8 + len(strips)),
        out_specs=vmem(3),
        scratch_shapes=[
            pltpu.VMEM((3 * LANES, span), BF16),
            pltpu.VMEM((9 * LANES, LANES), BF16),
            pltpu.VMEM((3 * LANES, span), BF16),
            pltpu.VMEM((9 * LANES, LANES), BF16),
            pltpu.VMEM((total_rows, LANES), F32),
        ],
        compiler_params=pltpu.CompilerParams(vmem_limit_bytes=40 * 1024 * 1024),
        name="layers",
    )(*fields, inner, outer, *strips, forward, backward)

    mine, other = reduce_halves(keep, send, gx_size, gy_size)
    results = pl.pallas_call(
        functools.partial(unpack_kernel, channels),
        out_shape=[shape(kernel_one.shape, F32)] * LAYERS,
        in_specs=vmem(2),
        out_specs=vmem(LAYERS),
        scratch_shapes=[pltpu.VMEM((total_rows, LANES), F32)],
        name="unpack",
    )(mine, other)
    return (grad.reshape(input_one.shape), results[2], results[1], results[0])


def solution(mesh):
    placed = (
        P(None, None, "gx", "gy"),
        P(None, None, "gx", "gy"),
        P(None, None, "gx", "gy"),
        P(None, None, "gx", "gy"),
        P(),
        P(),
        P(),
    )
    return jax.shard_map(
        per_device,
        mesh=mesh,
        in_specs=placed,
        out_specs=(P(None, None, "gx", "gy"), P(), P(), P()),
        check_vma=False,
    )
```

time: 303 us -> 58 us (0.19); the launches traced: 299 us -> 57.7 us
  waiting for transfers between devices: 140 us -> 16.2 us
  matrix products: 71 us -> 0 us
  starting transfers between devices: 59 us -> 22.2 us
  between operations: 17 us -> 0.78 us
  Pallas kernels: 0 us -> 15.4 us
  other arithmetic: 5.93 us -> 0.1 us
  local copies, waits for them, and re-layouts: 6.29 us -> 3.03 us
    psum x1 -> x0, waiting for transfers between devices: 119 us -> none  [per_device(): results.append(lax.psum(terms, ('gx', 'gy')) * factor)]
    dot_general x243 -> x0, matrix products: 71 us -> none  [the longest x81 27.5 us: back_taps(): jnp.einsum('oi,ozxy->izxy', kernel[tap], window, precision=lax.Precision....]
    ppermute x24 -> x12, starting transfers between devices: 59 us -> 22.2 us  [the longest x7 15.2 us: swap(): return lax.ppermute(value, axes, [(i, i ^ bit) for i in range(total)])]
    pallas_call x0 -> x4, Pallas kernels: none -> 15.4 us  [the longest x1 6.86 us: per_device(): pl.pallas_call(functools.partial(main_kernel, depth, rows, channels, len(...]
    ppermute x24 -> x12, waiting for transfers between devices: 20.4 us -> 16.2 us  [the longest x7 16.2 us: swap(): return lax.ppermute(value, axes, [(i, i ^ bit) for i in range(total)])]
    slice x15 -> x0, local copies, waits for them, and re-layouts: 3.34 us -> none  [the longest x3 1.5 us: conv_taps(): window = padded[:, a:a + depth, b:b + rows, c:c + cols]]
    concatenate x15 -> x0, other arithmetic: 3.04 us -> none  [with_halo(): value = jnp.concatenate([before, value, after], axis=dim)]
  transfers between devices with their start and end apart: 25 -> 12, of which waited for: 9 -> 7; matrix products, arithmetic and copies ran while one was open for 12% -> 0% of each run, Pallas kernels for 0% -> 7%
where the time goes in v1:
time: 58 us; the launch traced here: 57.7 us
  starting transfers between devices  22.2 us (38%)
  waiting for transfers between devices  16.2 us (28%)
  Pallas kernels  15.4 us (27%)
  local copies, waits for them, and re-layouts  3.03 us (5%)
  between operations  0.78 us (1%)
    ppermute x7, waiting for transfers between devices, swap(): return lax.ppermute(value, axes, [(i, i ^ bit) for i in range(total)])  16.2 us
    ppermute x7, starting transfers between devices, swap(): return lax.ppermute(value, axes, [(i, i ^ bit) for i in range(total)])  15.2 us
    pallas_call x1, Pallas kernels, per_device(): pl.pallas_call(functools.partial(main_kernel, depth, rows, channels, len(...  6.86 us
    pallas_call x1, Pallas kernels, per_device(): pl.pallas_call(functools.partial(weight_kernel, channels, depth), out_sha...  4.02 us
    unnamed x16, local copies, waits for them, and re-layouts  3.02 us
    ppermute x1, starting transfers between devices, per_device(): lax.ppermute(strip, both, diagonal(x_rounds[0], pairs))  2.72 us
    ppermute x1, starting transfers between devices, per_device(): strips_own = [lax.ppermute(strip, 'gy', pairs) for pairs in y_rounds]  2.55 us
    pallas_call x1, Pallas kernels, per_device(): pl.pallas_call(functools.partial(pack_kernel, depth, rows), out_shape=[sh...  2.3 us
  transfers between devices with their start and end apart: 12, of which 7 were waited for; matrix products, arithmetic and copies ran while one was open for 0% of the time, Pallas kernels for 7%

profile of v1, /device:TPU:0, one launch (start us, length us, event | category | flops | bytes accessed | tf_op | source)
XLA Modules:
  0.0 57.7 jit_solution(5317142658698724517)
XLA Ops:
  0.6 2.3 %pack.1 = (f32[768,128]{1,0:T(8,128)}, f32[768,128]{1,0:T(8,128)}, f32[64,128]{1,0:T(8,128)}) custom-call(f32[256,128]{1,0:T(8,128)} %bitcast.5, f32[256,128]{1,0:T(8,128)} %bitcast.7, f32[256,128]{1,0:T(8,128)} %bitcast.9, f32[256,128]{1,0:T(8,128)} %bitcast.11), custom_call_target="tpu_custom_call" | custom-call | tf_op jit(solution)/shard_map/pack/pallas_call | solution.py:321
  2.9 0.5 collective-permute-start
  3.4 0.7 %collective-permute-start.1 = (f32[768,128]{1,0:T(8,128)}, f32[768,128]{1,0:T(8,128)S(1)}, u32[]{:S(2)}, u32[]{:S(2)}) collective-permute-start(f32[768,128]{1,0:T(8,128)} %get-tuple-element.16), channel_id=1, source_target_pairs={{2,4},{6,8},{10,12},{14,16},{18,20},{22,24},{26,28},{4,2},{8,6},{1... | collective-permute-start | bytes 1179656 | tf_op jit(solution)/shard_map/ppermute | solution.py:339
  4.1 0.0 copy-start.2
  4.1 0.0 copy-start.3
  4.1 0.0 copy-start.4
  4.1 0.0 copy-start.5
  4.1 2.6 %collective-permute-start.2 = (f32[64,128]{1,0:T(8,128)}, f32[64,128]{1,0:T(8,128)S(1)}, u32[]{:S(2)}, u32[]{:S(2)}) collective-permute-start(f32[64,128]{1,0:T(8,128)} %get-tuple-element.17), channel_id=1, source_target_pairs={{0,1},{1,0},{2,3},{3,2},{4,5},{5,4},{6,7},{7,6},{8,9},{9,8},{10,11... | collective-permute-start | bytes 98312 | tf_op jit(solution)/shard_map/ppermute | solution.py:340
  6.7 2.7 %collective-permute-start.3 = (f32[64,128]{1,0:T(8,128)}, f32[64,128]{1,0:T(8,128)S(1)}, u32[]{:S(2)}, u32[]{:S(2)}) collective-permute-start(f32[64,128]{1,0:T(8,128)} %get-tuple-element.17), channel_id=1, source_target_pairs={{0,3},{1,2},{4,7},{5,6},{8,11},{9,10},{12,15},{13,14},{16,19},{17,... | collective-permute-start | bytes 98312 | tf_op jit(solution)/shard_map/ppermute | solution.py:343
  9.4 0.7 %collective-permute-start.4 = (f32[64,128]{1,0:T(8,128)}, f32[64,128]{1,0:T(8,128)S(1)}, u32[]{:S(2)}, u32[]{:S(2)}) collective-permute-start(f32[64,128]{1,0:T(8,128)} %get-tuple-element.17), channel_id=1, source_target_pairs={{2,5},{3,4},{6,9},{7,8},{10,13},{11,12},{14,17},{15,16},{18,21},{1... | collective-permute-start | bytes 98312 | tf_op jit(solution)/shard_map/ppermute | solution.py:341
  10.0 4.0 %weights.1 = (bf16[1152,384]{1,0:T(8,128)(2,1)}, bf16[1152,384]{1,0:T(8,128)(2,1)}) custom-call(f32[27,32,32]{2,1,0:T(8,128)} %refs_0_.1, f32[27,32,32]{2,1,0:T(8,128)} %refs_1_.1, f32[27,32,32]{2,1,0:T(8,128)} %refs_2_.1), custom_call_target="tpu_custom_call" | custom-call | flops 20000000 | bytes 4000000 | tf_op jit(solution)/shard_map/weights/pallas_call | solution.py:347
  14.1 0.0 collective-permute-done.2.refs_6_
  14.1 0.0 collective-permute-done.3.refs_7_
  14.1 0.0 collective-permute-done.4.refs_8_
  14.1 0.0 collective-permute-done.refs_4_
  14.1 0.0 collective-permute-done.1.refs_5_
  14.1 0.0 copy-done.2
  14.1 0.0 copy-done.3
  14.1 0.0 copy-done.4
  14.1 0.0 copy-done.5
  14.1 0.0 copy-start
  14.1 1.2 %copy-done = bf16[1152,384]{1,0:T(8,128)(2,1)S(1)} copy-done((bf16[1152,384]{1,0:T(8,128)(2,1)S(1)}, bf16[1152,384]{1,0:T(8,128)(2,1)}, u32[]{:S(2)}) %copy-start) | copy-done | bytes 884760
  15.3 0.0 copy-start.1
  15.3 1.2 %copy-done.1 = bf16[1152,384]{1,0:T(8,128)(2,1)S(1)} copy-done((bf16[1152,384]{1,0:T(8,128)(2,1)S(1)}, bf16[1152,384]{1,0:T(8,128)(2,1)}, u32[]{:S(2)}) %copy-start.1) | copy-done | bytes 884760
  16.5 6.9 %layers.1 = (f32[256,128]{1,0:T(8,128)}, f32[336,128]{1,0:T(8,128)S(1)}, f32[336,128]{1,0:T(8,128)S(1)}) custom-call(f32[256,128]{1,0:T(8,128)S(1)} %bitcast.6, f32[256,128]{1,0:T(8,128)S(1)} %bitcast.8, f32[256,128]{1,0:T(8,128)S(1)} %bitcast.10, f32[256,128]{1,0:T(8,128)S(1)} %bitcast.12, f32[768,128]{1,0:T(8,128)S(1)} %collective-permute-done.refs_4_, ...), custom_call_target="tpu_custom_call" | custom-call | tf_op jit(solution)/shard_map/layers/pallas_call | solution.py:358
  23.3 3.8 %collective-permute-start.5 = (f32[336,128]{1,0:T(8,128)S(1)}, f32[336,128]{1,0:T(8,128)S(1)}, u32[]{:S(2)}, u32[]{:S(2)}) collective-permute-start(f32[336,128]{1,0:T(8,128)S(1)} %get-tuple-element.22), channel_id=1, source_target_pairs={{0,2},{1,3},{2,0},{3,1},{4,6},{5,7},{6,4},{7,5},{8,10},{9,11},{10,... | collective-permute-start | bytes 516104 | tf_op jit(solution)/shard_map/ppermute | solution.py:293
  27.1 1.0 %collective-permute-done.5 = f32[336,128]{1,0:T(8,128)S(1)} collective-permute-done((f32[336,128]{1,0:T(8,128)S(1)}, f32[336,128]{1,0:T(8,128)S(1)}, u32[]{:S(2)}, u32[]{:S(2)}) %collective-permute-start.5) | collective-permute-done | bytes 172064 | tf_op jit(solution)/shard_map/ppermute | solution.py:293
  28.2 1.5 %collective-permute-start.6 = (f32[168,128]{1,0:T(8,128)S(1)}, f32[168,128]{1,0:T(8,128)S(1)}, u32[]{:S(2)}, u32[]{:S(2)}) collective-permute-start(f32[168,128]{1,0:T(8,128)S(1)} %constant_dynamic-slice_fusion), channel_id=1, source_target_pairs={{0,1},{1,0},{2,3},{3,2},{4,5},{5,4},{6,7},{7,6},{8,9},{9,8},{10,11... | collective-permute-start | bytes 258056 | tf_op jit(solution)/shard_map/ppermute | solution.py:293
  29.7 3.4 %collective-permute-done.6 = f32[168,128]{1,0:T(8,128)S(1)} collective-permute-done((f32[168,128]{1,0:T(8,128)S(1)}, f32[168,128]{1,0:T(8,128)S(1)}, u32[]{:S(2)}, u32[]{:S(2)}) %collective-permute-start.6) | collective-permute-done | bytes 86048 | tf_op jit(solution)/shard_map/ppermute | solution.py:293
  33.1 2.4 %collective-permute-start.7 = (f32[168,128]{1,0:T(8,128)S(1)}, f32[168,128]{1,0:T(8,128)S(1)}, u32[]{:S(2)}, u32[]{:S(2)}) collective-permute-start(f32[168,128]{1,0:T(8,128)S(1)} %dynamic-slice_add_fusion), channel_id=1, source_target_pairs={{0,4},{1,5},{2,6},{3,7},{4,0},{5,1},{6,2},{7,3},{8,12},{9,13},{10,... | collective-permute-start | bytes 258056 | tf_op jit(solution)/shard_map/ppermute | solution.py:293
  35.5 2.5 %collective-permute-done.7 = f32[168,128]{1,0:T(8,128)S(1)} collective-permute-done((f32[168,128]{1,0:T(8,128)S(1)}, f32[168,128]{1,0:T(8,128)S(1)}, u32[]{:S(2)}, u32[]{:S(2)}) %collective-permute-start.7) | collective-permute-done | bytes 86048 | tf_op jit(solution)/shard_map/ppermute | solution.py:293
  38.0 2.5 %collective-permute-start.8 = (f32[168,128]{1,0:T(8,128)S(1)}, f32[168,128]{1,0:T(8,128)S(1)}, u32[]{:S(2)}, u32[]{:S(2)}) collective-permute-start(f32[168,128]{1,0:T(8,128)S(1)} %add.25), channel_id=1, source_target_pairs={{0,8},{1,9},{2,10},{3,11},{4,12},{5,13},{6,14},{7,15},{8,0},{9,1},... | collective-permute-start | bytes 258056 | tf_op jit(solution)/shard_map/ppermute | solution.py:293
  40.5 2.5 %collective-permute-done.8 = f32[168,128]{1,0:T(8,128)S(1)} collective-permute-done((f32[168,128]{1,0:T(8,128)S(1)}, f32[168,128]{1,0:T(8,128)S(1)}, u32[]{:S(2)}, u32[]{:S(2)}) %collective-permute-start.8) | collective-permute-done | bytes 86048 | tf_op jit(solution)/shard_map/ppermute | solution.py:293
  43.0 3.3 %collective-permute-start.9 = (f32[168,128]{1,0:T(8,128)S(1)}, f32[168,128]{1,0:T(8,128)S(1)}, u32[]{:S(2)}, u32[]{:S(2)}) collective-permute-start(f32[168,128]{1,0:T(8,128)S(1)} %add.26), channel_id=1, source_target_pairs={{0,16},{1,17},{2,18},{3,19},{4,20},{5,21},{6,22},{7,23},{8,24},{9,... | collective-permute-start | bytes 258056 | tf_op jit(solution)/shard_map/ppermute | solution.py:293
  46.3 2.5 %collective-permute-done.9 = f32[168,128]{1,0:T(8,128)S(1)} collective-permute-done((f32[168,128]{1,0:T(8,128)S(1)}, f32[168,128]{1,0:T(8,128)S(1)}, u32[]{:S(2)}, u32[]{:S(2)}) %collective-permute-start.9) | collective-permute-done | bytes 86048 | tf_op jit(solution)/shard_map/ppermute | solution.py:293
  48.8 1.6 %collective-permute-start.10 = (f32[168,128]{1,0:T(8,128)S(1)}, f32[168,128]{1,0:T(8,128)S(1)}, u32[]{:S(2)}, u32[]{:S(2)}) collective-permute-start(f32[168,128]{1,0:T(8,128)S(1)} %add.27), channel_id=1, source_target_pairs={{0,1},{1,0},{2,3},{3,2},{4,5},{5,4},{6,7},{7,6},{8,9},{9,8},{10,11... | collective-permute-start | bytes 258056 | tf_op jit(solution)/shard_map/ppermute | solution.py:293
  50.3 3.0 %collective-permute-done.10 = f32[168,128]{1,0:T(8,128)S(1)} collective-permute-done((f32[168,128]{1,0:T(8,128)S(1)}, f32[168,128]{1,0:T(8,128)S(1)}, u32[]{:S(2)}, u32[]{:S(2)}) %collective-permute-start.10) | collective-permute-done | bytes 86048 | tf_op jit(solution)/shard_map/ppermute | solution.py:293
  53.4 0.0 copy-start.6
  53.4 0.1 collective-permute-start.11
  53.4 1.4 %collective-permute-done.11.other = f32[336,128]{1,0:T(8,128)S(1)} collective-permute-done((f32[336,128]{1,0:T(8,128)S(1)}, f32[336,128]{1,0:T(8,128)S(1)}, u32[]{:S(2)}, u32[]{:S(2)}) %collective-permute-start.11) | collective-permute-done | bytes 172064 | tf_op jit(solution)/shard_map/ppermute | solution.py:293
  54.8 0.0 copy-done.6
  54.8 0.0 copy-start.7
  54.8 0.7 %copy-done.7 = f32[336,128]{1,0:T(8,128)} copy-done((f32[336,128]{1,0:T(8,128)}, f32[336,128]{1,0:T(8,128)S(1)}, u32[]{:S(2)}) %copy-start.7) | copy-done | bytes 172056
  55.5 2.2 %unpack.1 = (f32[27,32,32]{2,1,0:T(8,128)}, f32[27,32,32]{2,1,0:T(8,128)}, f32[27,32,32]{2,1,0:T(8,128)}) custom-call(f32[336,128]{1,0:T(8,128)} %copy-done.6, f32[336,128]{1,0:T(8,128)} %copy-done.7), custom_call_target="tpu_custom_call" | custom-call | tf_op jit(solution)/shard_map/unpack/pallas_call | solution.py:379
  (7 shorter events, 0.1 us)
Async XLA Ops:
  2.9 11.1 %collective-permute-start = (f32[768,128]{1,0:T(8,128)}, f32[768,128]{1,0:T(8,128)S(1)}, u32[]{:S(2)}, u32[]{:S(2)}) collective-permute-start(f32[768,128]{1,0:T(8,128)} %get-tuple-element.15), channel_id=1, source_target_pairs={{0,2},{4,6},{8,10},{12,14},{16,18},{20,22},{24,26},{28,30},{2,0},{... | collective-permute-start | bytes 1179656 | tf_op jit(solution)/shard_map/ppermute | solution.py:342
  3.4 10.7 %collective-permute-start.1 = (f32[768,128]{1,0:T(8,128)}, f32[768,128]{1,0:T(8,128)S(1)}, u32[]{:S(2)}, u32[]{:S(2)}) collective-permute-start(f32[768,128]{1,0:T(8,128)} %get-tuple-element.16), channel_id=1, source_target_pairs={{2,4},{6,8},{10,12},{14,16},{18,20},{22,24},{26,28},{4,2},{8,6},{1... | collective-permute-start | bytes 1179656 | tf_op jit(solution)/shard_map/ppermute | solution.py:339
  4.1 10.0 %copy-start.2 = (f32[32,2,4,128]{3,2,1,0:T(4,128)S(1)}, f32[32,2,4,128]{3,2,1,0:T(4,128)}, u32[]{:S(2)}) copy-start(f32[32,2,4,128]{3,2,1,0:T(4,128)} %param.9) | copy-start | bytes 393220
  4.1 10.0 %copy-start.3 = (f32[32,2,4,128]{3,2,1,0:T(4,128)S(1)}, f32[32,2,4,128]{3,2,1,0:T(4,128)}, u32[]{:S(2)}) copy-start(f32[32,2,4,128]{3,2,1,0:T(4,128)} %param.10) | copy-start | bytes 393220
  4.1 10.0 %copy-start.4 = (f32[32,2,4,128]{3,2,1,0:T(4,128)S(1)}, f32[32,2,4,128]{3,2,1,0:T(4,128)}, u32[]{:S(2)}) copy-start(f32[32,2,4,128]{3,2,1,0:T(4,128)} %param.8) | copy-start | bytes 393220
  4.1 10.0 %copy-start.5 = (f32[32,2,4,128]{3,2,1,0:T(4,128)S(1)}, f32[32,2,4,128]{3,2,1,0:T(4,128)}, u32[]{:S(2)}) copy-start(f32[32,2,4,128]{3,2,1,0:T(4,128)} %param.7) | copy-start | bytes 393220
  4.1 10.0 %collective-permute-start.2 = (f32[64,128]{1,0:T(8,128)}, f32[64,128]{1,0:T(8,128)S(1)}, u32[]{:S(2)}, u32[]{:S(2)}) collective-permute-start(f32[64,128]{1,0:T(8,128)} %get-tuple-element.17), channel_id=1, source_target_pairs={{0,1},{1,0},{2,3},{3,2},{4,5},{5,4},{6,7},{7,6},{8,9},{9,8},{10,11... | collective-permute-start | bytes 98312 | tf_op jit(solution)/shard_map/ppermute | solution.py:340
  6.7 7.4 %collective-permute-start.3 = (f32[64,128]{1,0:T(8,128)}, f32[64,128]{1,0:T(8,128)S(1)}, u32[]{:S(2)}, u32[]{:S(2)}) collective-permute-start(f32[64,128]{1,0:T(8,128)} %get-tuple-element.17), channel_id=1, source_target_pairs={{0,3},{1,2},{4,7},{5,6},{8,11},{9,10},{12,15},{13,14},{16,19},{17,... | collective-permute-start | bytes 98312 | tf_op jit(solution)/shard_map/ppermute | solution.py:343
  9.4 4.7 %collective-permute-start.4 = (f32[64,128]{1,0:T(8,128)}, f32[64,128]{1,0:T(8,128)S(1)}, u32[]{:S(2)}, u32[]{:S(2)}) collective-permute-start(f32[64,128]{1,0:T(8,128)} %get-tuple-element.17), channel_id=1, source_target_pairs={{2,5},{3,4},{6,9},{7,8},{10,13},{11,12},{14,17},{15,16},{18,21},{1... | collective-permute-start | bytes 98312 | tf_op jit(solution)/shard_map/ppermute | solution.py:341
  14.1 1.2 %copy-start = (bf16[1152,384]{1,0:T(8,128)(2,1)S(1)}, bf16[1152,384]{1,0:T(8,128)(2,1)}, u32[]{:S(2)}) copy-start(bf16[1152,384]{1,0:T(8,128)(2,1)} %get-tuple-element.18.refs_9_) | copy-start | bytes 2654212
  15.3 1.2 %copy-start.1 = (bf16[1152,384]{1,0:T(8,128)(2,1)S(1)}, bf16[1152,384]{1,0:T(8,128)(2,1)}, u32[]{:S(2)}) copy-start(bf16[1152,384]{1,0:T(8,128)(2,1)} %get-tuple-element.19.refs_10_) | copy-start | bytes 2654212
  23.3 4.8 %collective-permute-start.5 = (f32[336,128]{1,0:T(8,128)S(1)}, f32[336,128]{1,0:T(8,128)S(1)}, u32[]{:S(2)}, u32[]{:S(2)}) collective-permute-start(f32[336,128]{1,0:T(8,128)S(1)} %get-tuple-element.22), channel_id=1, source_target_pairs={{0,2},{1,3},{2,0},{3,1},{4,6},{5,7},{6,4},{7,5},{8,10},{9,11},{10,... | collective-permute-start | bytes 516104 | tf_op jit(solution)/shard_map/ppermute | solution.py:293
  28.2 4.9 %collective-permute-start.6 = (f32[168,128]{1,0:T(8,128)S(1)}, f32[168,128]{1,0:T(8,128)S(1)}, u32[]{:S(2)}, u32[]{:S(2)}) collective-permute-start(f32[168,128]{1,0:T(8,128)S(1)} %constant_dynamic-slice_fusion), channel_id=1, source_target_pairs={{0,1},{1,0},{2,3},{3,2},{4,5},{5,4},{6,7},{7,6},{8,9},{9,8},{10,11... | collective-permute-start | bytes 258056 | tf_op jit(solution)/shard_map/ppermute | solution.py:293
  33.1 4.9 %collective-permute-start.7 = (f32[168,128]{1,0:T(8,128)S(1)}, f32[168,128]{1,0:T(8,128)S(1)}, u32[]{:S(2)}, u32[]{:S(2)}) collective-permute-start(f32[168,128]{1,0:T(8,128)S(1)} %dynamic-slice_add_fusion), channel_id=1, source_target_pairs={{0,4},{1,5},{2,6},{3,7},{4,0},{5,1},{6,2},{7,3},{8,12},{9,13},{10,... | collective-permute-start | bytes 258056 | tf_op jit(solution)/shard_map/ppermute | solution.py:293
  38.0 5.0 %collective-permute-start.8 = (f32[168,128]{1,0:T(8,128)S(1)}, f32[168,128]{1,0:T(8,128)S(1)}, u32[]{:S(2)}, u32[]{:S(2)}) collective-permute-start(f32[168,128]{1,0:T(8,128)S(1)} %add.25), channel_id=1, source_target_pairs={{0,8},{1,9},{2,10},{3,11},{4,12},{5,13},{6,14},{7,15},{8,0},{9,1},... | collective-permute-start | bytes 258056 | tf_op jit(solution)/shard_map/ppermute | solution.py:293
  43.0 5.8 %collective-permute-start.9 = (f32[168,128]{1,0:T(8,128)S(1)}, f32[168,128]{1,0:T(8,128)S(1)}, u32[]{:S(2)}, u32[]{:S(2)}) collective-permute-start(f32[168,128]{1,0:T(8,128)S(1)} %add.26), channel_id=1, source_target_pairs={{0,16},{1,17},{2,18},{3,19},{4,20},{5,21},{6,22},{7,23},{8,24},{9,... | collective-permute-start | bytes 258056 | tf_op jit(solution)/shard_map/ppermute | solution.py:293
  48.8 4.6 %collective-permute-start.10 = (f32[168,128]{1,0:T(8,128)S(1)}, f32[168,128]{1,0:T(8,128)S(1)}, u32[]{:S(2)}, u32[]{:S(2)}) collective-permute-start(f32[168,128]{1,0:T(8,128)S(1)} %add.27), channel_id=1, source_target_pairs={{0,1},{1,0},{2,3},{3,2},{4,5},{5,4},{6,7},{7,6},{8,9},{9,8},{10,11... | collective-permute-start | bytes 258056 | tf_op jit(solution)/shard_map/ppermute | solution.py:293
  53.4 1.5 %copy-start.6 = (f32[336,128]{1,0:T(8,128)}, f32[336,128]{1,0:T(8,128)S(1)}, u32[]{:S(2)}) copy-start(f32[336,128]{1,0:T(8,128)S(1)} %maximum_select_fusion.mine) | copy-start | bytes 516100
  53.4 1.5 %collective-permute-start.11 = (f32[336,128]{1,0:T(8,128)S(1)}, f32[336,128]{1,0:T(8,128)S(1)}, u32[]{:S(2)}, u32[]{:S(2)}) collective-permute-start(f32[336,128]{1,0:T(8,128)S(1)} %maximum_select_fusion.mine), channel_id=1, source_target_pairs={{0,2},{1,3},{2,0},{3,1},{4,6},{5,7},{6,4},{7,5},{8,10},{9,11},{10,... | collective-permute-start | bytes 516104 | tf_op jit(solution)/shard_map/ppermute | solution.py:293
  54.8 0.7 %copy-start.7 = (f32[336,128]{1,0:T(8,128)}, f32[336,128]{1,0:T(8,128)S(1)}, u32[]{:S(2)}) copy-start(f32[336,128]{1,0:T(8,128)S(1)} %collective-permute-done.11.other) | copy-start | bytes 516100

commit v2 on v1

--- a/solution.py
+++ b/solution.py
@@ -40,6 +40,18 @@
     return lax.broadcasted_iota(jnp.int32, (rows, LANES), 1)
 
 
+def near(value):
+    return pltpu.with_memory_space_constraint(value, pltpu.VMEM)
+
+
+def far(value):
+    return pltpu.with_memory_space_constraint(value, pltpu.HBM)
+
+
+def room(mib):
+    return pltpu.CompilerParams(vmem_limit_bytes=mib * 1024 * 1024)
+
+
 def vmem(count):
     return [pl.BlockSpec(memory_space=pltpu.VMEM)] * count
 
@@ -57,7 +69,16 @@
 
 
 def pack_kernel(depth, rows, *refs):
-    fields, (inner, outer, strip) = refs[:4], refs[4:]
+    count = 4 + LAYERS
+    inner, outer, strip = refs[2 * count : 2 * count + 3]
+    copies = [
+        pltpu.make_async_copy(refs[i], refs[count + i], refs[2 * count + 3].at[i]) for i in range(count)
+    ]
+    for copy in copies:
+        copy.start()
+    for copy in copies[:4]:
+        copy.wait()
+    fields = refs[count : count + 4]
     odd = lax.rem(lax.axis_index("gx"), 2)
     planes = fields[0].shape[0] // rows
     lane = lane_index(planes)
@@ -76,6 +97,8 @@
             total = jnp.where(first, roll(value, base), total)
             total = jnp.where(last, roll(value, base + SIDE), total)
     strip[...] = total
+    for copy in copies[4:]:
+        copy.wait()
 
 
 def weight_kernel(channels, depth, *refs):
@@ -100,12 +123,33 @@
                     ref[pl.ds(base + planes, planes), pl.ds(cc * LANES, LANES)] = low
 
 
+def conv(weights, layer, source, lane_start, count):
+    planes = weights.shape[0] // (LAYERS * 3 * 2)
+    total = None
+    for b in range(3):
+        kernel = weights[pl.ds((layer * 3 + b) * 2 * planes, 2 * planes), :]
+        window = source[:, pl.ds(lane_start + (b - 1) * LANES, count * LANES)]
+        term = lax.dot_general(kernel, window, NN, preferred_element_type=F32)
+        total = term if total is None else total + term
+    return total[:planes] + total[planes:]
+
+
+def conv_rows(weights, layer, source, low, high):
+    out = {}
+    for e in range(low, high, 2):
+        count = min(2, high - e)
+        value = conv(weights, layer, source, e * LANES, count)
+        for k in range(count):
+            out[e + k] = value[:, k * LANES : (k + 1) * LANES]
+    return out
+
+
 def main_kernel(depth, rows, channels, gy_rounds, factor, *refs):
     fields = refs[:4]
     inner, outer = refs[4:6]
     strips = refs[6 : 6 + 3 * gy_rounds]
     rest = refs[6 + 3 * gy_rounds :]
-    forward, backward, grad_out, keep, send, xs, xside, hs, hside, gsum = rest
+    forward, backward, hs, keep, send, xs, xside, hside, gsum = rest
     planes = depth * channels
     gx, gy = lax.axis_index("gx"), lax.axis_index("gy")
     gx_size, gy_size = lax.axis_size("gx"), lax.axis_size("gy")
@@ -168,15 +212,6 @@
                 into_side[pl.ds(base, planes), :] = high
                 into_side[pl.ds(base + planes, planes), :] = low
 
-    def conv(weights, layer, source, lane_start, count):
-        total = None
-        for b in range(3):
-            kernel = weights[pl.ds((layer * 3 + b) * 2 * planes, 2 * planes), :]
-            window = source[:, pl.ds(lane_start + (b - 1) * LANES, count * LANES)]
-            term = lax.dot_general(kernel, window, NN, preferred_element_type=F32)
-            total = term if total is None else total + term
-        return total[:planes] + total[planes:]
-
     def conv_side(weights, layer, source):
         total = None
         for b in range(3):
@@ -186,21 +221,15 @@
             total = term if total is None else total + term
         return total[:planes] + total[planes:]
 
-    def conv_rows(weights, layer, source, low, high):
-        out = {}
-        for e in range(low, high, 2):
-            count = min(2, high - e)
-            value = conv(weights, layer, source, e * LANES, count)
-            for k in range(count):
-                out[e + k] = value[:, k * LANES : (k + 1) * LANES]
-        return out
-
     side_row = lane // SIDE
     row_low = jnp.where(gx > 0, 0, HALO)
     row_high = jnp.where(gx < gx_size - 1, 2 * HALO + rows, HALO + rows)
     col_ok = jnp.where(right, (gy < gy_size - 1).astype(jnp.int32), (gy > 0).astype(jnp.int32))
     side_ok = (side_row >= row_low) & (side_row < row_high) & (col_ok > 0)
 
+    padding = gsum.shape[0] - LAYERS * 7 * channels
+    if padding:
+        gsum[pl.ds(LAYERS * 7 * channels, padding), :] = jnp.zeros((padding, LANES), F32)
     grad_main, grad_side = field_parts(1)
     half = lane_index(channels)
     for layer in range(LAYERS):
@@ -240,27 +269,40 @@
             gsum[pl.ds((layer * 7 + m) * channels, channels), :] = tile
 
         g_width = h_width - 1
-        grad_main = conv_rows(backward, layer, hs, HALO - g_width, HALO + rows + g_width)
         if g_width:
+            grad_main = conv_rows(backward, layer, hs, HALO - g_width, HALO + rows + g_width)
             grad_side = conv_side(backward, layer, hside)
 
+    size = keep.shape[0] // 4
+    core, quad = quad_place(gx, gy)
+    for k in range(4):
+        piece = lax.bitwise_xor(quad, k) * size
+        at = pl.ds(k * size, size)
+        keep[at, :] = gsum[pl.ds(pl.multiple_of(core * 4 * size + piece, 8), size), :]
+        send[at, :] = gsum[pl.ds(pl.multiple_of((1 - core) * 4 * size + piece, 8), size), :]
+
+
+def quad_place(gx, gy):
+    return lax.rem(gx, 2), lax.rem(gy, 2) + 2 * lax.rem(gx // 2, 2)
+
+
+def grad_kernel(depth, rows, channels, hs, backward, grad_out):
+    grad_main = conv_rows(backward, LAYERS - 1, hs, HALO, HALO + rows)
     for r in range(rows):
         for z in range(depth):
             at = pl.ds(z * rows + r, channels, stride=depth * rows)
             grad_out[at, :] = grad_main[HALO + r][z * channels : (z + 1) * channels]
-    size = keep.shape[0]
-    mine = pl.multiple_of(lax.rem(gx, 2) * size, 8)
-    other = pl.multiple_of((1 - lax.rem(gx, 2)) * size, 8)
-    keep[...] = gsum[pl.ds(mine, size), :]
-    send[...] = gsum[pl.ds(other, size), :]
 
 
 def unpack_kernel(channels, mine, other, *refs):
     outs, whole = refs[:LAYERS], refs[LAYERS]
-    size = mine.shape[0]
-    odd = lax.rem(lax.axis_index("gx"), 2)
-    whole[pl.ds(pl.multiple_of(odd * size, 8), size), :] = mine[...]
-    whole[pl.ds(pl.multiple_of((1 - odd) * size, 8), size), :] = other[...]
+    size = mine.shape[0] // 4
+    core, quad = quad_place(lax.axis_index("gx"), lax.axis_index("gy"))
+    for k in range(4):
+        piece = lax.bitwise_xor(quad, k) * size
+        at = pl.ds(k * size, size)
+        whole[pl.ds(pl.multiple_of(core * 4 * size + piece, 8), size), :] = mine[at, :]
+        whole[pl.ds(pl.multiple_of((1 - core) * 4 * size + piece, 8), size), :] = other[at, :]
     order = (0, 2, 1)
     for layer in range(LAYERS):
         for m in range(7):
@@ -284,30 +326,32 @@
     return rounds
 
 
-def reduce_halves(keep, send, gx_size, gy_size):
+def reduce_halves(keep, send, beside, gx_size, gy_size):
     axes = ("gx", "gy")
     total = gx_size * gy_size
-    gx, gy = lax.axis_index("gx"), lax.axis_index("gy")
-
-    def swap(value, bit):
-        return lax.ppermute(value, axes, [(i, i ^ bit) for i in range(total)])
-
-    value = keep + swap(send, gy_size)
-    size = value.shape[0] // 2
-    split_at = gy_size > 1
-    bits = [1 << k for k in range(1, gy_size.bit_length() - 1)]
-    bits += [gy_size << k for k in range(1, gx_size.bit_length() - 1)]
-    if split_at:
-        side = gy & 1
-        mine = lax.dynamic_slice_in_dim(value, side * size, size, axis=0)
-        other = lax.dynamic_slice_in_dim(value, (1 - side) * size, size, axis=0)
-        value = mine + swap(other, 1)
-    for bit in bits:
-        value = value + swap(value, bit)
-    if split_at:
-        got = swap(value, 1)
-        value = jnp.where(side == 0, jnp.concatenate([value, got]), jnp.concatenate([got, value]))
-    return value, swap(value, gy_size)
+
+    def swap(value, bits):
+        return lax.ppermute(value, axes, [(i, i ^ bits) for i in range(total)])
+
+    core, quad = gy_size, (1, 2 * gy_size, 2 * gy_size + 1)
+    value = keep + swap(send, core)
+    size = value.shape[0] // 4
+    pieces = [value[k * size : (k + 1) * size] for k in range(4)]
+    got = [swap(pieces[k + 1], quad[k]) for k in range(3)]
+    value = (pieces[0] + got[0]) + (got[1] + got[2])
+    value, beside = lax.optimization_barrier((value, beside))
+    bits = [gy_size << k for k in range(2, gx_size.bit_length() - 1)]
+    bits += [1 << k for k in range(1, gy_size.bit_length() - 1)]
+    while bits:
+        low, *high = bits[:2]
+        if high:
+            got = [swap(value, b) for b in (low, high[0], low | high[0])]
+            value = (value + got[0]) + (got[1] + got[2])
+        else:
+            value = value + swap(value, low)
+        bits = bits[2:]
+    value = jnp.concatenate([value] + [swap(value, b) for b in quad])
+    return value, swap(value, core), beside
 
 
 def per_device(input_one, input_two, input_three, cotangent, kernel_one, kernel_two, kernel_three):
@@ -318,17 +362,22 @@
     fields = [v.reshape(planes * rows, cols) for v in (input_three, cotangent, input_two, input_one)]
     shape = jax.ShapeDtypeStruct
 
-    inner, outer, strip = pl.pallas_call(
+    kernels = [kernel_three, kernel_two, kernel_one]
+    *local, inner, outer, strip = pl.pallas_call(
         functools.partial(pack_kernel, depth, rows),
-        out_shape=[
-            shape((SLABS * planes, cols), F32),
-            shape((SLABS * planes, cols), F32),
-            shape((planes, cols), F32),
+        out_shape=[pltpu.VMEM(v.shape, F32) for v in fields + kernels]
+        + [
+            pltpu.VMEM((SLABS * planes, cols), F32),
+            pltpu.VMEM((SLABS * planes, cols), F32),
+            pltpu.VMEM((planes, cols), F32),
         ],
-        in_specs=vmem(4),
-        out_specs=vmem(3),
+        in_specs=[pl.BlockSpec(memory_space=pltpu.HBM)] * (4 + LAYERS),
+        out_specs=vmem(7 + LAYERS),
+        scratch_shapes=[pltpu.SemaphoreType.DMA((4 + LAYERS,))],
+        compiler_params=room(8),
         name="pack",
-    )(*fields)
+    )(*(far(v) for v in fields + kernels))
+    fields, kernels = local[:4], local[4:]
 
     x_rounds, y_rounds = pair_rounds(gx_size), pair_rounds(gy_size)
     both = ("gx", "gy")
@@ -343,47 +392,58 @@
     strips_inner = [lax.ppermute(strip, both, diagonal(x_rounds[0], pairs)) for pairs in y_rounds]
     strips = strips_own + strips_inner + strips_outer
 
-    weight_shape = shape((LAYERS * 3 * 2 * planes, 3 * LANES), BF16)
+    weight_shape = pltpu.VMEM((LAYERS * 3 * 2 * planes, 3 * LANES), BF16)
     forward, backward = pl.pallas_call(
         functools.partial(weight_kernel, channels, depth),
         out_shape=[weight_shape, weight_shape],
         in_specs=vmem(LAYERS),
         out_specs=vmem(2),
         cost_estimate=pl.CostEstimate(flops=20_000_000, bytes_accessed=4_000_000, transcendentals=0),
+        compiler_params=room(12),
         name="weights",
-    )(kernel_three, kernel_two, kernel_one)
-
-    total_rows = LAYERS * 7 * channels
+    )(*(near(v) for v in kernels))
+
+    tiles = -(-LAYERS * 7 * channels // 64) * 64
     span = (2 * HALO + rows) * LANES
-    grad, keep, send = pl.pallas_call(
+    hs, keep, send = pl.pallas_call(
         functools.partial(main_kernel, depth, rows, channels, len(y_rounds), factor),
         out_shape=[
-            shape((planes * rows, cols), F32),
-            shape((total_rows // 2, LANES), F32),
-            shape((total_rows // 2, LANES), F32),
+            pltpu.VMEM((3 * LANES, span), BF16),
+            pltpu.VMEM((tiles // 2, LANES), F32),
+            pltpu.VMEM((tiles // 2, LANES), F32),
         ],
         in_specs=vmem(8 + len(strips)),
         out_specs=vmem(3),
         scratch_shapes=[
             pltpu.VMEM((3 * LANES, span), BF16),
             pltpu.VMEM((9 * LANES, LANES), BF16),
-            pltpu.VMEM((3 * LANES, span), BF16),
             pltpu.VMEM((9 * LANES, LANES), BF16),
-            pltpu.VMEM((total_rows, LANES), F32),
+            pltpu.VMEM((tiles, LANES), F32),
         ],
-        compiler_params=pltpu.CompilerParams(vmem_limit_bytes=40 * 1024 * 1024),
+        compiler_params=room(24),
         name="layers",
-    )(*fields, inner, outer, *strips, forward, backward)
-
-    mine, other = reduce_halves(keep, send, gx_size, gy_size)
+    )(*(near(v) for v in (*fields, inner, outer, *strips, forward, backward)))
+
+    grad = pl.pallas_call(
+        functools.partial(grad_kernel, depth, rows, channels),
+        out_shape=shape((planes * rows, cols), F32),
+        in_specs=vmem(2),
+        out_specs=vmem(1)[0],
+        cost_estimate=pl.CostEstimate(flops=600_000_000, bytes_accessed=1_000_000, transcendentals=0),
+        compiler_params=room(8),
+        name="grad_input",
+    )(near(hs), near(backward))
+
+    mine, other, grad = reduce_halves(keep, send, grad, gx_size, gy_size)
     results = pl.pallas_call(
         functools.partial(unpack_kernel, channels),
         out_shape=[shape(kernel_one.shape, F32)] * LAYERS,
         in_specs=vmem(2),
         out_specs=vmem(LAYERS),
-        scratch_shapes=[pltpu.VMEM((total_rows, LANES), F32)],
+        scratch_shapes=[pltpu.VMEM((tiles, LANES), F32)],
+        compiler_params=room(8),
         name="unpack",
-    )(mine, other)
+    )(near(mine), near(other))
     return (grad.reshape(input_one.shape), results[2], results[1], results[0])
 
 

time: 58 us -> 50.4 us (0.87)
  waiting for transfers between devices: 16.2 us -> 12.3 us
  Pallas kernels: 15.4 us -> 11.7 us
  starting transfers between devices: 22.2 us -> 25.4 us
  local copies, waits for them, and re-layouts: 3.03 us -> 0.01 us
    ppermute x7 -> x11, waiting for transfers between devices: 16.2 us -> 11.7 us  [swap(): return lax.ppermute(value, axes, [(i, i ^ bits) for i in range(total)])]
    ppermute x1, starting transfers between devices: 2.72 us -> 6.3 us  [per_device(): lax.ppermute(strip, both, diagonal(x_rounds[0], pairs))]
    unnamed x16 -> x0, local copies, waits for them, and re-layouts: 3.02 us -> none
    pallas_call x1, Pallas kernels: 4.02 us -> 1.63 us  [per_device(): pl.pallas_call(functools.partial(weight_kernel, channels, depth), out_sha...]
    pallas_call x1, Pallas kernels: 2.23 us -> 1.24 us  [per_device(): pl.pallas_call(functools.partial(unpack_kernel, channels), out_shape=[sha...]
    pallas_call x1, Pallas kernels: 6.86 us -> 6.21 us  [per_device(): pl.pallas_call(functools.partial(main_kernel, depth, rows, channels, len(...]
    ppermute x1, waiting for transfers between devices: 0.01 us -> 0.58 us  [per_device(): strips_own = [lax.ppermute(strip, 'gy', pairs) for pairs in y_rounds]]
    pallas_call x1 -> x2, Pallas kernels: 2.3 us -> 2.64 us  [the longest x1 1.61 us: per_device(): pl.pallas_call(functools.partial(pack_kernel, depth, rows), out_shape=[pl...]
  transfers between devices with their start and end apart: 12 -> 16, of which waited for: 7 -> 10; matrix products, arithmetic and copies ran while one was open for 0% -> 0% of each run, Pallas kernels for 7% -> 5%
where the time goes in v2:
time: 50.4 us; the launch traced here: 50.2 us
  starting transfers between devices  25.4 us (50%)
  waiting for transfers between devices  12.3 us (24%)
  Pallas kernels  11.7 us (23%)
  between operations  0.73 us (1%)
    ppermute x11, starting transfers between devices, swap(): return lax.ppermute(value, axes, [(i, i ^ bits) for i in range(total)])  15.2 us
    ppermute x11, waiting for transfers between devices, swap(): return lax.ppermute(value, axes, [(i, i ^ bits) for i in range(total)])  11.7 us
    ppermute x1, starting transfers between devices, per_device(): lax.ppermute(strip, both, diagonal(x_rounds[0], pairs))  6.3 us
    pallas_call x1, Pallas kernels, per_device(): pl.pallas_call(functools.partial(main_kernel, depth, rows, channels, len(...  6.21 us
    ppermute x1, starting transfers between devices, per_device(): strips_own = [lax.ppermute(strip, 'gy', pairs) for pairs in y_rounds]  2.06 us
    pallas_call x1, Pallas kernels, per_device(): pl.pallas_call(functools.partial(weight_kernel, channels, depth), out_sha...  1.63 us
    pallas_call x1, Pallas kernels, per_device(): pl.pallas_call(functools.partial(pack_kernel, depth, rows), out_shape=[pl...  1.61 us
    pallas_call x1, Pallas kernels, per_device(): pl.pallas_call(functools.partial(unpack_kernel, channels), out_shape=[sha...  1.24 us
  transfers between devices with their start and end apart: 16, of which 10 were waited for; matrix products, arithmetic and copies ran while one was open for 0% of the time, Pallas kernels for 5%

profile of v2, /device:TPU:0, one launch (start us, length us, event | category | flops | bytes accessed | tf_op | source)
XLA Modules:
  0.0 50.2 jit_solution(5179114098028161706)
XLA Ops:
  0.6 1.6 %pack.1 = (f32[256,128]{1,0:T(8,128)S(1)}, f32[256,128]{1,0:T(8,128)S(1)}, f32[256,128]{1,0:T(8,128)S(1)}, f32[256,128]{1,0:T(8,128)S(1)}, f32[27,32,32]{2,1,0:T...) custom-call(f32[256,128]{1,0:T(8,128)} %bitcast.5, ...), custom_call_target="tpu_custom_call" | custom-call | tf_op jit(solution)/shard_map/pack/pallas_call | solution.py:366
  2.2 0.5 %collective-permute-start = (f32[768,128]{1,0:T(8,128)S(1)}, f32[768,128]{1,0:T(8,128)S(1)}, u32[]{:S(2)}, u32[]{:S(2)}) collective-permute-start(f32[768,128]{1,0:T(8,128)S(1)} %get-tuple-element.28), channel_id=1, source_target_pairs={{0,2},{4,6},{8,10},{12,14},{16,18},{20,22},{24,26},{28,30},{2,0},{... | collective-permute-start | bytes 1179656 | tf_op jit(solution)/shard_map/ppermute | solution.py:391
  2.8 0.7 %collective-permute-start.1 = (f32[768,128]{1,0:T(8,128)S(1)}, f32[768,128]{1,0:T(8,128)S(1)}, u32[]{:S(2)}, u32[]{:S(2)}) collective-permute-start(f32[768,128]{1,0:T(8,128)S(1)} %get-tuple-element.29), channel_id=1, source_target_pairs={{2,4},{6,8},{10,12},{14,16},{18,20},{22,24},{26,28},{4,2},{8,6},{1... | collective-permute-start | bytes 1179656 | tf_op jit(solution)/shard_map/ppermute | solution.py:388
  3.4 0.7 %collective-permute-start.4 = (f32[64,128]{1,0:T(8,128)S(1)}, f32[64,128]{1,0:T(8,128)S(1)}, u32[]{:S(2)}, u32[]{:S(2)}) collective-permute-start(f32[64,128]{1,0:T(8,128)S(1)} %get-tuple-element.30), channel_id=1, source_target_pairs={{2,5},{3,4},{6,9},{7,8},{10,13},{11,12},{14,17},{15,16},{18,21},{1... | collective-permute-start | bytes 98312 | tf_op jit(solution)/shard_map/ppermute | solution.py:390
  4.1 6.3 %collective-permute-start.3 = (f32[64,128]{1,0:T(8,128)S(1)}, f32[64,128]{1,0:T(8,128)S(1)}, u32[]{:S(2)}, u32[]{:S(2)}) collective-permute-start(f32[64,128]{1,0:T(8,128)S(1)} %get-tuple-element.30), channel_id=1, source_target_pairs={{0,3},{1,2},{4,7},{5,6},{8,11},{9,10},{12,15},{13,14},{16,19},{17,... | collective-permute-start | bytes 98312 | tf_op jit(solution)/shard_map/ppermute | solution.py:392
  10.4 2.1 %collective-permute-start.2 = (f32[64,128]{1,0:T(8,128)S(1)}, f32[64,128]{1,0:T(8,128)S(1)}, u32[]{:S(2)}, u32[]{:S(2)}) collective-permute-start(f32[64,128]{1,0:T(8,128)S(1)} %get-tuple-element.30), channel_id=1, source_target_pairs={{0,1},{1,0},{2,3},{3,2},{4,5},{5,4},{6,7},{7,6},{8,9},{9,8},{10,11... | collective-permute-start | bytes 98312 | tf_op jit(solution)/shard_map/ppermute | solution.py:389
  12.5 1.6 %weights.1 = (bf16[1152,384]{1,0:T(8,128)(2,1)S(1)}, bf16[1152,384]{1,0:T(8,128)(2,1)S(1)}) custom-call(f32[27,32,32]{2,1,0:T(8,128)S(1)} %get-tuple-element.31.refs_0_, f32[27,32,32]{2,1,0:T(8,128)S(1)} %get-tuple-element.32.refs_1_, f32[27,32,32]{2,1,0:T(8,128)S(1)} %get-tuple-element.33.refs_2_), custom_call_target="tpu_custom_call" | custom-call | flops 20000000 | bytes 4000000 | tf_op jit(solution)/shard_map/weights/pallas_call | solution.py:396
  14.1 0.0 collective-permute-done.4.refs_8_
  14.1 0.0 collective-permute-done.3.refs_7_
  14.1 0.6 %collective-permute-done.2.refs_6_ = f32[64,128]{1,0:T(8,128)S(1)} collective-permute-done((f32[64,128]{1,0:T(8,128)S(1)}, f32[64,128]{1,0:T(8,128)S(1)}, u32[]{:S(2)}, u32[]{:S(2)}) %collective-permute-start.2) | collective-permute-done | bytes 32800 | tf_op jit(solution)/shard_map/ppermute | solution.py:389
  14.7 0.0 collective-permute-done.refs_4_
  14.7 0.0 collective-permute-done.1.refs_5_
  14.7 6.2 %layers.1 = (bf16[384,1536]{1,0:T(8,128)(2,1)S(1)}, f32[352,128]{1,0:T(8,128)S(1)}, f32[352,128]{1,0:T(8,128)S(1)}) custom-call(f32[256,128]{1,0:T(8,128)S(1)} %get-tuple-element.24.refs_0_, f32[256,128]{1,0:T(8,128)S(1)} %get-tuple-element.25.refs_1_, f32[256,128]{1,0:T(8,128)S(1)} %get-tuple-element.26.refs_2_, f32[256,128]{1,0:T(8,128)S(1)} %get-tuple-element.27.refs_3_, ...), custom_call_target="tpu_custom_call" | custom-call | tf_op jit(solution)/shard_map/layers/pallas_call | solution.py:408
  20.9 2.3 %collective-permute-start.5 = (f32[352,128]{1,0:T(8,128)S(1)}, f32[352,128]{1,0:T(8,128)S(1)}, u32[]{:S(2)}, u32[]{:S(2)}) collective-permute-start(f32[352,128]{1,0:T(8,128)S(1)} %get-tuple-element.37), channel_id=1, source_target_pairs={{0,2},{1,3},{2,0},{3,1},{4,6},{5,7},{6,4},{7,5},{8,10},{9,11},{10,... | collective-permute-start | bytes 540680 | tf_op jit(solution)/shard_map/ppermute | solution.py:334
  23.2 1.0 %collective-permute-done.5 = f32[352,128]{1,0:T(8,128)S(1)} collective-permute-done((f32[352,128]{1,0:T(8,128)S(1)}, f32[352,128]{1,0:T(8,128)S(1)}, u32[]{:S(2)}, u32[]{:S(2)}) %collective-permute-start.5) | collective-permute-done | bytes 180256 | tf_op jit(solution)/shard_map/ppermute | solution.py:334
  24.3 3.7 %collective-permute-start.8 = (f32[88,128]{1,0:T(8,128)S(1)}, f32[88,128]{1,0:T(8,128)S(1)}, u32[]{:S(2)}, u32[]{:S(2)}) collective-permute-start(f32[88,128]{1,0:T(8,128)S(1)} %get-tuple-element.44), channel_id=1, source_target_pairs={{0,5},{1,4},{2,7},{3,6},{4,1},{5,0},{6,3},{7,2},{8,13},{9,12},{10,... | collective-permute-start | bytes 135176 | tf_op jit(solution)/shard_map/ppermute | solution.py:334
  28.0 0.0 collective-permute-start.7
  28.1 0.6 %collective-permute-start.6 = (f32[88,128]{1,0:T(8,128)S(1)}, f32[88,128]{1,0:T(8,128)S(1)}, u32[]{:S(2)}, u32[]{:S(2)}) collective-permute-start(f32[88,128]{1,0:T(8,128)S(1)} %get-tuple-element.46), channel_id=1, source_target_pairs={{0,1},{1,0},{2,3},{3,2},{4,5},{5,4},{6,7},{7,6},{8,9},{9,8},{10,11... | collective-permute-start | bytes 135176 | tf_op jit(solution)/shard_map/ppermute | solution.py:334
  28.7 1.0 %grad_input.1 = f32[256,128]{1,0:T(8,128)} custom-call(bf16[384,1536]{1,0:T(8,128)(2,1)S(1)} %get-tuple-element.38.hs, bf16[1152,384]{1,0:T(8,128)(2,1)S(1)} %get-tuple-element.35.refs_10_.backward), custom_call_target="tpu_custom_call" | custom-call | flops 600000000 | bytes 1000000 | tf_op jit(solution)/shard_map/grad_input/pallas_call | solution.py:427
  29.7 0.3 collective-permute-done.8
  30.1 2.0 %collective-permute-done.7 = f32[88,128]{1,0:T(8,128)S(1)} collective-permute-done((f32[88,128]{1,0:T(8,128)S(1)}, f32[88,128]{1,0:T(8,128)S(1)}, u32[]{:S(2)}, u32[]{:S(2)}) %collective-permute-start.7) | collective-permute-done | bytes 45088 | tf_op jit(solution)/shard_map/ppermute | solution.py:334
  32.1 0.0 collective-permute-done.6
  32.1 4.3 %collective-permute-start.11 = (f32[88,128]{1,0:T(8,128)S(1)}, f32[88,128]{1,0:T(8,128)S(1)}, u32[]{:S(2)}, u32[]{:S(2)}) collective-permute-start(f32[88,128]{1,0:T(8,128)S(1)} %fusion), channel_id=1, source_target_pairs={{0,24},{1,25},{2,26},{3,27},{4,28},{5,29},{6,30},{7,31},{8,16},{9,... | collective-permute-start | bytes 135176 | tf_op jit(solution)/shard_map/ppermute | solution.py:334
  36.4 0.0 collective-permute-start.10
  36.4 0.6 %collective-permute-start.9 = (f32[88,128]{1,0:T(8,128)S(1)}, f32[88,128]{1,0:T(8,128)S(1)}, u32[]{:S(2)}, u32[]{:S(2)}) collective-permute-start(f32[88,128]{1,0:T(8,128)S(1)} %fusion), channel_id=1, source_target_pairs={{0,8},{1,9},{2,10},{3,11},{4,12},{5,13},{6,14},{7,15},{8,0},{9,1},... | collective-permute-start | bytes 135176 | tf_op jit(solution)/shard_map/ppermute | solution.py:334
  37.1 1.5 %collective-permute-done.11 = f32[88,128]{1,0:T(8,128)S(1)} collective-permute-done((f32[88,128]{1,0:T(8,128)S(1)}, f32[88,128]{1,0:T(8,128)S(1)}, u32[]{:S(2)}, u32[]{:S(2)}) %collective-permute-start.11) | collective-permute-done | bytes 45088 | tf_op jit(solution)/shard_map/ppermute | solution.py:334
  38.5 2.8 %collective-permute-done.10 = f32[88,128]{1,0:T(8,128)S(1)} collective-permute-done((f32[88,128]{1,0:T(8,128)S(1)}, f32[88,128]{1,0:T(8,128)S(1)}, u32[]{:S(2)}, u32[]{:S(2)}) %collective-permute-start.10) | collective-permute-done | bytes 45088 | tf_op jit(solution)/shard_map/ppermute | solution.py:334
  41.4 0.0 collective-permute-done.9
  41.4 0.8 %collective-permute-start.14 = (f32[88,128]{1,0:T(8,128)S(1)}, f32[88,128]{1,0:T(8,128)S(1)}, u32[]{:S(2)}, u32[]{:S(2)}) collective-permute-start(f32[88,128]{1,0:T(8,128)S(1)} %add_add_fusion), channel_id=1, source_target_pairs={{0,5},{1,4},{2,7},{3,6},{4,1},{5,0},{6,3},{7,2},{8,13},{9,12},{10,... | collective-permute-start | bytes 135176 | tf_op jit(solution)/shard_map/ppermute | solution.py:334
  42.2 1.2 %collective-permute-start.13 = (f32[88,128]{1,0:T(8,128)S(1)}, f32[88,128]{1,0:T(8,128)S(1)}, u32[]{:S(2)}, u32[]{:S(2)}) collective-permute-start(f32[88,128]{1,0:T(8,128)S(1)} %add_add_fusion), channel_id=1, source_target_pairs={{0,4},{1,5},{2,6},{3,7},{4,0},{5,1},{6,2},{7,3},{8,12},{9,13},{10,... | collective-permute-start | bytes 135176 | tf_op jit(solution)/shard_map/ppermute | solution.py:334
  43.4 1.5 %collective-permute-start.12 = (f32[88,128]{1,0:T(8,128)S(1)}, f32[88,128]{1,0:T(8,128)S(1)}, u32[]{:S(2)}, u32[]{:S(2)}) collective-permute-start(f32[88,128]{1,0:T(8,128)S(1)} %add_add_fusion), channel_id=1, source_target_pairs={{0,1},{1,0},{2,3},{3,2},{4,5},{5,4},{6,7},{7,6},{8,9},{9,8},{10,11... | collective-permute-start | bytes 135176 | tf_op jit(solution)/shard_map/ppermute | solution.py:334
  44.9 1.6 %collective-permute-done.14 = f32[88,128]{1,0:T(8,128)S(1)} collective-permute-done((f32[88,128]{1,0:T(8,128)S(1)}, f32[88,128]{1,0:T(8,128)S(1)}, u32[]{:S(2)}, u32[]{:S(2)}) %collective-permute-start.14) | collective-permute-done | bytes 45088 | tf_op jit(solution)/shard_map/ppermute | solution.py:334
  46.5 0.2 collective-permute-done.13
  46.7 0.8 %collective-permute-done.12 = f32[88,128]{1,0:T(8,128)S(1)} collective-permute-done((f32[88,128]{1,0:T(8,128)S(1)}, f32[88,128]{1,0:T(8,128)S(1)}, u32[]{:S(2)}, u32[]{:S(2)}) %collective-permute-start.12) | collective-permute-done | bytes 45088 | tf_op jit(solution)/shard_map/ppermute | solution.py:334
  47.5 0.1 collective-permute-start.15
  47.6 1.4 %collective-permute-done.15.other = f32[352,128]{1,0:T(8,128)S(1)} collective-permute-done((f32[352,128]{1,0:T(8,128)S(1)}, f32[352,128]{1,0:T(8,128)S(1)}, u32[]{:S(2)}, u32[]{:S(2)}) %collective-permute-start.15) | collective-permute-done | bytes 180256 | tf_op jit(solution)/shard_map/ppermute | solution.py:334
  49.0 1.2 %unpack.1 = (f32[27,32,32]{2,1,0:T(8,128)}, f32[27,32,32]{2,1,0:T(8,128)}, f32[27,32,32]{2,1,0:T(8,128)}) custom-call(f32[352,128]{1,0:T(8,128)S(1)} %pad_maximum_fusion.mine, f32[352,128]{1,0:T(8,128)S(1)} %collective-permute-done.15.other), custom_call_target="tpu_custom_call" | custom-call | tf_op jit(solution)/shard_map/unpack/pallas_call | solution.py:438
  (5 shorter events, 0.1 us)
Async XLA Ops:
  2.2 12.5 %collective-permute-start = (f32[768,128]{1,0:T(8,128)S(1)}, f32[768,128]{1,0:T(8,128)S(1)}, u32[]{:S(2)}, u32[]{:S(2)}) collective-permute-start(f32[768,128]{1,0:T(8,128)S(1)} %get-tuple-element.28), channel_id=1, source_target_pairs={{0,2},{4,6},{8,10},{12,14},{16,18},{20,22},{24,26},{28,30},{2,0},{... | collective-permute-start | bytes 1179656 | tf_op jit(solution)/shard_map/ppermute | solution.py:391
  2.8 12.0 %collective-permute-start.1 = (f32[768,128]{1,0:T(8,128)S(1)}, f32[768,128]{1,0:T(8,128)S(1)}, u32[]{:S(2)}, u32[]{:S(2)}) collective-permute-start(f32[768,128]{1,0:T(8,128)S(1)} %get-tuple-element.29), channel_id=1, source_target_pairs={{2,4},{6,8},{10,12},{14,16},{18,20},{22,24},{26,28},{4,2},{8,6},{1... | collective-permute-start | bytes 1179656 | tf_op jit(solution)/shard_map/ppermute | solution.py:388
  3.4 10.7 %collective-permute-start.4 = (f32[64,128]{1,0:T(8,128)S(1)}, f32[64,128]{1,0:T(8,128)S(1)}, u32[]{:S(2)}, u32[]{:S(2)}) collective-permute-start(f32[64,128]{1,0:T(8,128)S(1)} %get-tuple-element.30), channel_id=1, source_target_pairs={{2,5},{3,4},{6,9},{7,8},{10,13},{11,12},{14,17},{15,16},{18,21},{1... | collective-permute-start | bytes 98312 | tf_op jit(solution)/shard_map/ppermute | solution.py:390
  4.1 10.0 %collective-permute-start.3 = (f32[64,128]{1,0:T(8,128)S(1)}, f32[64,128]{1,0:T(8,128)S(1)}, u32[]{:S(2)}, u32[]{:S(2)}) collective-permute-start(f32[64,128]{1,0:T(8,128)S(1)} %get-tuple-element.30), channel_id=1, source_target_pairs={{0,3},{1,2},{4,7},{5,6},{8,11},{9,10},{12,15},{13,14},{16,19},{17,... | collective-permute-start | bytes 98312 | tf_op jit(solution)/shard_map/ppermute | solution.py:392
  10.4 4.3 %collective-permute-start.2 = (f32[64,128]{1,0:T(8,128)S(1)}, f32[64,128]{1,0:T(8,128)S(1)}, u32[]{:S(2)}, u32[]{:S(2)}) collective-permute-start(f32[64,128]{1,0:T(8,128)S(1)} %get-tuple-element.30), channel_id=1, source_target_pairs={{0,1},{1,0},{2,3},{3,2},{4,5},{5,4},{6,7},{7,6},{8,9},{9,8},{10,11... | collective-permute-start | bytes 98312 | tf_op jit(solution)/shard_map/ppermute | solution.py:389
  20.9 3.3 %collective-permute-start.5 = (f32[352,128]{1,0:T(8,128)S(1)}, f32[352,128]{1,0:T(8,128)S(1)}, u32[]{:S(2)}, u32[]{:S(2)}) collective-permute-start(f32[352,128]{1,0:T(8,128)S(1)} %get-tuple-element.37), channel_id=1, source_target_pairs={{0,2},{1,3},{2,0},{3,1},{4,6},{5,7},{6,4},{7,5},{8,10},{9,11},{10,... | collective-permute-start | bytes 540680 | tf_op jit(solution)/shard_map/ppermute | solution.py:334
  24.3 5.7 %collective-permute-start.8 = (f32[88,128]{1,0:T(8,128)S(1)}, f32[88,128]{1,0:T(8,128)S(1)}, u32[]{:S(2)}, u32[]{:S(2)}) collective-permute-start(f32[88,128]{1,0:T(8,128)S(1)} %get-tuple-element.44), channel_id=1, source_target_pairs={{0,5},{1,4},{2,7},{3,6},{4,1},{5,0},{6,3},{7,2},{8,13},{9,12},{10,... | collective-permute-start | bytes 135176 | tf_op jit(solution)/shard_map/ppermute | solution.py:334
  28.0 4.0 %collective-permute-start.7 = (f32[88,128]{1,0:T(8,128)S(1)}, f32[88,128]{1,0:T(8,128)S(1)}, u32[]{:S(2)}, u32[]{:S(2)}) collective-permute-start(f32[88,128]{1,0:T(8,128)S(1)} %get-tuple-element.45), channel_id=1, source_target_pairs={{0,4},{1,5},{2,6},{3,7},{4,0},{5,1},{6,2},{7,3},{8,12},{9,13},{10,... | collective-permute-start | bytes 135176 | tf_op jit(solution)/shard_map/ppermute | solution.py:334
  28.1 4.0 %collective-permute-start.6 = (f32[88,128]{1,0:T(8,128)S(1)}, f32[88,128]{1,0:T(8,128)S(1)}, u32[]{:S(2)}, u32[]{:S(2)}) collective-permute-start(f32[88,128]{1,0:T(8,128)S(1)} %get-tuple-element.46), channel_id=1, source_target_pairs={{0,1},{1,0},{2,3},{3,2},{4,5},{5,4},{6,7},{7,6},{8,9},{9,8},{10,11... | collective-permute-start | bytes 135176 | tf_op jit(solution)/shard_map/ppermute | solution.py:334
  32.1 6.4 %collective-permute-start.11 = (f32[88,128]{1,0:T(8,128)S(1)}, f32[88,128]{1,0:T(8,128)S(1)}, u32[]{:S(2)}, u32[]{:S(2)}) collective-permute-start(f32[88,128]{1,0:T(8,128)S(1)} %fusion), channel_id=1, source_target_pairs={{0,24},{1,25},{2,26},{3,27},{4,28},{5,29},{6,30},{7,31},{8,16},{9,... | collective-permute-start | bytes 135176 | tf_op jit(solution)/shard_map/ppermute | solution.py:334
  36.4 4.9 %collective-permute-start.10 = (f32[88,128]{1,0:T(8,128)S(1)}, f32[88,128]{1,0:T(8,128)S(1)}, u32[]{:S(2)}, u32[]{:S(2)}) collective-permute-start(f32[88,128]{1,0:T(8,128)S(1)} %fusion), channel_id=1, source_target_pairs={{0,16},{1,17},{2,18},{3,19},{4,20},{5,21},{6,22},{7,23},{8,24},{9,... | collective-permute-start | bytes 135176 | tf_op jit(solution)/shard_map/ppermute | solution.py:334
  36.4 4.9 %collective-permute-start.9 = (f32[88,128]{1,0:T(8,128)S(1)}, f32[88,128]{1,0:T(8,128)S(1)}, u32[]{:S(2)}, u32[]{:S(2)}) collective-permute-start(f32[88,128]{1,0:T(8,128)S(1)} %fusion), channel_id=1, source_target_pairs={{0,8},{1,9},{2,10},{3,11},{4,12},{5,13},{6,14},{7,15},{8,0},{9,1},... | collective-permute-start | bytes 135176 | tf_op jit(solution)/shard_map/ppermute | solution.py:334
  41.4 5.1 %collective-permute-start.14 = (f32[88,128]{1,0:T(8,128)S(1)}, f32[88,128]{1,0:T(8,128)S(1)}, u32[]{:S(2)}, u32[]{:S(2)}) collective-permute-start(f32[88,128]{1,0:T(8,128)S(1)} %add_add_fusion), channel_id=1, source_target_pairs={{0,5},{1,4},{2,7},{3,6},{4,1},{5,0},{6,3},{7,2},{8,13},{9,12},{10,... | collective-permute-start | bytes 135176 | tf_op jit(solution)/shard_map/ppermute | solution.py:334
  42.2 4.5 %collective-permute-start.13 = (f32[88,128]{1,0:T(8,128)S(1)}, f32[88,128]{1,0:T(8,128)S(1)}, u32[]{:S(2)}, u32[]{:S(2)}) collective-permute-start(f32[88,128]{1,0:T(8,128)S(1)} %add_add_fusion), channel_id=1, source_target_pairs={{0,4},{1,5},{2,6},{3,7},{4,0},{5,1},{6,2},{7,3},{8,12},{9,13},{10,... | collective-permute-start | bytes 135176 | tf_op jit(solution)/shard_map/ppermute | solution.py:334
  43.4 4.0 %collective-permute-start.12 = (f32[88,128]{1,0:T(8,128)S(1)}, f32[88,128]{1,0:T(8,128)S(1)}, u32[]{:S(2)}, u32[]{:S(2)}) collective-permute-start(f32[88,128]{1,0:T(8,128)S(1)} %add_add_fusion), channel_id=1, source_target_pairs={{0,1},{1,0},{2,3},{3,2},{4,5},{5,4},{6,7},{7,6},{8,9},{9,8},{10,11... | collective-permute-start | bytes 135176 | tf_op jit(solution)/shard_map/ppermute | solution.py:334
  47.5 1.5 %collective-permute-start.15 = (f32[352,128]{1,0:T(8,128)S(1)}, f32[352,128]{1,0:T(8,128)S(1)}, u32[]{:S(2)}, u32[]{:S(2)}) collective-permute-start(f32[352,128]{1,0:T(8,128)S(1)} %pad_maximum_fusion.mine), channel_id=1, source_target_pairs={{0,2},{1,3},{2,0},{3,1},{4,6},{5,7},{6,4},{7,5},{8,10},{9,11},{10,... | collective-permute-start | bytes 540680 | tf_op jit(solution)/shard_map/ppermute | solution.py:334

commit v3 on v2

--- a/solution.py
+++ b/solution.py
@@ -56,9 +56,12 @@
     return [pl.BlockSpec(memory_space=pltpu.VMEM)] * count
 
 
-def slab_at(ref, depth, rows, row):
-    channels = ref.shape[0] // (depth * rows)
-    parts = [ref[pl.ds(z * rows + row, channels, stride=depth * rows), :] for z in range(depth)]
+def slab_at(ref, field, depth, rows, row):
+    size = ref.shape[0] // 4
+    channels = size // (depth * rows)
+    parts = [
+        ref[pl.ds(field * size + z * rows + row, channels, stride=depth * rows), :] for z in range(depth)
+    ]
     return jnp.concatenate(parts, axis=0)
 
 
@@ -68,37 +71,42 @@
     return high, low
 
 
-def pack_kernel(depth, rows, *refs):
+def fetch_kernel(*refs):
     count = 4 + LAYERS
-    inner, outer, strip = refs[2 * count : 2 * count + 3]
+    sources, (local, *kernels), semaphores = refs[:count], refs[count : count + 1 + LAYERS], refs[-1]
+    size = sources[0].shape[0]
+    targets = [local.at[pl.ds(f * size, size), :] for f in range(4)] + kernels
     copies = [
-        pltpu.make_async_copy(refs[i], refs[count + i], refs[2 * count + 3].at[i]) for i in range(count)
+        pltpu.make_async_copy(source, target, semaphores.at[k])
+        for k, (source, target) in enumerate(zip(sources, targets))
     ]
     for copy in copies:
         copy.start()
-    for copy in copies[:4]:
+    for copy in copies:
         copy.wait()
-    fields = refs[count : count + 4]
+
+
+def pack_kernel(depth, rows, local, sibling, first, second, strips, strip):
     odd = lax.rem(lax.axis_index("gx"), 2)
-    planes = fields[0].shape[0] // rows
+    planes = local.shape[0] // (4 * rows)
     lane = lane_index(planes)
-    total = jnp.zeros((planes, LANES), F32)
-    for f, ref in enumerate(fields):
-        width = WIDTHS[f]
+    for f, width in enumerate(WIDTHS):
+        out, start = (first, 0) if f < 2 else (second, STARTS[2])
         for j in range(width):
-            at = pl.ds((STARTS[f] + j) * planes, planes)
-            inner[at, :] = slab_at(ref, depth, rows, (rows - width) * (1 - odd) + j)
-            outer[at, :] = slab_at(ref, depth, rows, (rows - width) * odd + j)
-        for r in range(rows):
-            value = slab_at(ref, depth, rows, r)
-            base = (f * rows + r) * SIDE
-            first = (lane >= base) & (lane < base + HALO)
-            last = (lane >= base + HALO) & (lane < base + SIDE)
-            total = jnp.where(first, roll(value, base), total)
-            total = jnp.where(last, roll(value, base + SIDE), total)
+            row = (rows - width) * (1 - odd) + j
+            out[pl.ds((STARTS[f] - start + j) * planes, planes), :] = slab_at(sibling, f, depth, rows, row)
+    for k, ref in enumerate((local, sibling)):
+        total = jnp.zeros((planes, LANES), F32)
+        for f in range(4):
+            for r in range(rows):
+                value = slab_at(ref, f, depth, rows, r)
+                base = (f * rows + r) * SIDE
+                leading = (lane >= base) & (lane < base + HALO)
+                trailing = (lane >= base + HALO) & (lane < base + SIDE)
+                total = jnp.where(leading, roll(value, base), total)
+                total = jnp.where(trailing, roll(value, base + SIDE), total)
+        strips[pl.ds(k * planes, planes), :] = total
     strip[...] = total
-    for copy in copies[4:]:
-        copy.wait()
 
 
 def weight_kernel(channels, depth, *refs):
@@ -144,23 +152,36 @@
     return out
 
 
-def main_kernel(depth, rows, channels, gy_rounds, factor, *refs):
-    fields = refs[:4]
-    inner, outer = refs[4:6]
-    strips = refs[6 : 6 + 3 * gy_rounds]
-    rest = refs[6 + 3 * gy_rounds :]
-    forward, backward, hs, keep, send, xs, xside, hside, gsum = rest
+def layers_kernel(depth, rows, channels, gy_rounds, factor, layers, *refs):
+    refs = list(refs)
+    take = lambda count: [refs.pop(0) for _ in range(count)]
+    opening = layers[0] == 0
+    chosen = (0, 1) if opening else (2, 3)
+    local, sibling, outer = take(3)
+    strips = take(2 * gy_rounds)
+    forward, backward = take(2)
+    if opening:
+        grad_out, sums, xs, xside, hs, hside = refs
+    else:
+        grad_in, first_sums, hs, keep, send, xs, xside, hside, gsum = refs
     planes = depth * channels
     gx, gy = lax.axis_index("gx"), lax.axis_index("gy")
     gx_size, gy_size = lax.axis_size("gx"), lax.axis_size("gy")
     x_odd, y_odd = lax.rem(gx, 2) == 1, lax.rem(gy, 2) == 1
+    odd = lax.rem(gx, 2)
+    ended = (gx == 0) | (gx == gx_size - 1)
     lane = lane_index(planes)
     place = lax.rem(lane, SIDE)
     right = place < HALO
     zero = jnp.zeros((planes, LANES), F32)
 
     def side_strip(group):
-        got = [strips[group * gy_rounds + r][...] for r in range(gy_rounds)]
+        got = []
+        for r in range(gy_rounds):
+            if group < 2:
+                got.append(strips[r][pl.ds(group * planes, planes), :])
+            else:
+                got.append(jnp.where(ended, 0.0, strips[gy_rounds + r][...]))
         if gy_rounds == 0:
             return zero
         if gy_rounds == 1:
@@ -178,12 +199,13 @@
         width = WIDTHS[f]
         main = {}
         for j in range(width):
-            at = pl.ds((STARTS[f] + j) * planes, planes)
-            a, b = inner[at, :], outer[at, :]
+            start = STARTS[f] + j - STARTS[chosen[0]]
+            a = slab_at(sibling, f, depth, rows, (rows - width) * odd + j)
+            b = jnp.where(ended, 0.0, outer[pl.ds(start * planes, planes), :])
             main[HALO - width + j] = jnp.where(x_odd, a, b)
             main[HALO + rows + j] = jnp.where(x_odd, b, a)
         for r in range(rows):
-            main[HALO + r] = slab_at(fields[f], depth, rows, r)
+            main[HALO + r] = slab_at(local, f, depth, rows, r)
         lead = HALO * SIDE
         before = roll(before_strip, lead - span - f * span)
         own = roll(own_strip, lead - f * span)
@@ -227,12 +249,21 @@
     col_ok = jnp.where(right, (gy < gy_size - 1).astype(jnp.int32), (gy > 0).astype(jnp.int32))
     side_ok = (side_row >= row_low) & (side_row < row_high) & (col_ok > 0)
 
-    padding = gsum.shape[0] - LAYERS * 7 * channels
-    if padding:
-        gsum[pl.ds(LAYERS * 7 * channels, padding), :] = jnp.zeros((padding, LANES), F32)
-    grad_main, grad_side = field_parts(1)
+    if opening:
+        gsum = sums
+        grad_main, grad_side = field_parts(1)
+    else:
+        low = HALO - LAYERS + layers[0]
+        count = rows + 2 * (HALO - low)
+        grad_main = {low + k: grad_in[pl.ds(k * planes, planes), :] for k in range(count)}
+        grad_side = grad_in[pl.ds(count * planes, planes), :]
+        done = layers[0] * 7 * channels
+        gsum[pl.ds(0, done), :] = first_sums[...]
+        padding = gsum.shape[0] - LAYERS * 7 * channels
+        if padding:
+            gsum[pl.ds(LAYERS * 7 * channels, padding), :] = jnp.zeros((padding, LANES), F32)
     half = lane_index(channels)
-    for layer in range(LAYERS):
+    for layer in layers:
         x_main, x_side = field_parts((0, 2, 3)[layer])
         store_shifted(x_main, x_side, xs, xside)
         h_width = LAYERS - layer
@@ -273,6 +304,11 @@
             grad_main = conv_rows(backward, layer, hs, HALO - g_width, HALO + rows + g_width)
             grad_side = conv_side(backward, layer, hside)
 
+    if opening:
+        for k, e in enumerate(sorted(grad_main)):
+            grad_out[pl.ds(k * planes, planes), :] = grad_main[e]
+        grad_out[pl.ds(len(grad_main) * planes, planes), :] = grad_side
+        return
     size = keep.shape[0] // 4
     core, quad = quad_place(gx, gy)
     for k in range(4):
@@ -363,34 +399,44 @@
     shape = jax.ShapeDtypeStruct
 
     kernels = [kernel_three, kernel_two, kernel_one]
-    *local, inner, outer, strip = pl.pallas_call(
+    size = planes * rows
+    local, *kernels = pl.pallas_call(
+        fetch_kernel,
+        out_shape=[pltpu.VMEM((4 * size, cols), F32)] + [pltpu.VMEM(v.shape, F32) for v in kernels],
+        in_specs=[pl.BlockSpec(memory_space=pltpu.HBM)] * (4 + LAYERS),
+        out_specs=vmem(1 + LAYERS),
+        scratch_shapes=[pltpu.SemaphoreType.DMA((4 + LAYERS,))],
+        compiler_params=room(8),
+        name="fetch",
+    )(*(far(v) for v in fields + kernels))
+
+    sibling = lax.ppermute(local, "gx", [(i, i ^ 1) for i in range(gx_size)])
+    across = [(i, i - 2) if i % 2 else (i, i + 2) for i in range(gx_size)]
+    across = [(i, j) if 0 <= j < gx_size else (i, i ^ 1) for i, j in across]
+    y_rounds = pair_rounds(gy_size)
+    first, second, strips, strip = pl.pallas_call(
         functools.partial(pack_kernel, depth, rows),
-        out_shape=[pltpu.VMEM(v.shape, F32) for v in fields + kernels]
-        + [
-            pltpu.VMEM((SLABS * planes, cols), F32),
-            pltpu.VMEM((SLABS * planes, cols), F32),
+        out_shape=[
+            pltpu.VMEM((STARTS[2] * planes, cols), F32),
+            pltpu.VMEM(((SLABS - STARTS[2]) * planes, cols), F32),
+            pltpu.VMEM((2 * planes, cols), F32),
             pltpu.VMEM((planes, cols), F32),
         ],
-        in_specs=[pl.BlockSpec(memory_space=pltpu.HBM)] * (4 + LAYERS),
-        out_specs=vmem(7 + LAYERS),
-        scratch_shapes=[pltpu.SemaphoreType.DMA((4 + LAYERS,))],
+        in_specs=vmem(2),
+        out_specs=vmem(4),
         compiler_params=room(8),
         name="pack",
-    )(*(far(v) for v in fields + kernels))
-    fields, kernels = local[:4], local[4:]
-
-    x_rounds, y_rounds = pair_rounds(gx_size), pair_rounds(gy_size)
-    both = ("gx", "gy")
+    )(near(local), near(sibling))
 
     def diagonal(x_pairs, y_pairs):
         return [(i * gy_size + k, j * gy_size + m) for i, j in x_pairs for k, m in y_pairs]
 
-    outer = lax.ppermute(outer, "gx", x_rounds[1])
-    strips_own = [lax.ppermute(strip, "gy", pairs) for pairs in y_rounds]
-    strips_outer = [lax.ppermute(strip, both, diagonal(x_rounds[1], pairs)) for pairs in y_rounds]
-    inner = lax.ppermute(inner, "gx", x_rounds[0])
-    strips_inner = [lax.ppermute(strip, both, diagonal(x_rounds[0], pairs)) for pairs in y_rounds]
-    strips = strips_own + strips_inner + strips_outer
+    first = lax.ppermute(first, "gx", across)
+    strips = [lax.ppermute(strips, "gy", pairs) for pairs in y_rounds]
+    corners = [lax.ppermute(strip, ("gx", "gy"), diagonal(across, pairs)) for pairs in y_rounds]
+    second, *strips = lax.optimization_barrier((second, *strips))
+    second = lax.ppermute(second, "gx", across)
+    strips += corners
 
     weight_shape = pltpu.VMEM((LAYERS * 3 * 2 * planes, 3 * LANES), BF16)
     forward, backward = pl.pallas_call(
@@ -405,24 +451,34 @@
 
     tiles = -(-LAYERS * 7 * channels // 64) * 64
     span = (2 * HALO + rows) * LANES
+    scratch = [pltpu.VMEM((3 * LANES, span), BF16), pltpu.VMEM((9 * LANES, LANES), BF16)]
+    kernel = functools.partial(layers_kernel, depth, rows, channels, len(y_rounds), factor)
+    grad, sums = pl.pallas_call(
+        functools.partial(kernel, (0,)),
+        out_shape=[
+            pltpu.VMEM(((rows + 2 * (LAYERS - 1) + 1) * planes, LANES), F32),
+            pltpu.VMEM((7 * channels, LANES), F32),
+        ],
+        in_specs=vmem(5 + len(strips)),
+        out_specs=vmem(2),
+        scratch_shapes=scratch * 2,
+        compiler_params=room(16),
+        cost_estimate=pl.CostEstimate(flops=3_000_000_000, bytes_accessed=3_000_000, transcendentals=0),
+        name="layer_three",
+    )(*(near(v) for v in (local, sibling, first, *strips, forward, backward)))
     hs, keep, send = pl.pallas_call(
-        functools.partial(main_kernel, depth, rows, channels, len(y_rounds), factor),
+        functools.partial(kernel, (1, 2)),
         out_shape=[
             pltpu.VMEM((3 * LANES, span), BF16),
             pltpu.VMEM((tiles // 2, LANES), F32),
             pltpu.VMEM((tiles // 2, LANES), F32),
         ],
-        in_specs=vmem(8 + len(strips)),
+        in_specs=vmem(7 + len(strips)),
         out_specs=vmem(3),
-        scratch_shapes=[
-            pltpu.VMEM((3 * LANES, span), BF16),
-            pltpu.VMEM((9 * LANES, LANES), BF16),
-            pltpu.VMEM((9 * LANES, LANES), BF16),
-            pltpu.VMEM((tiles, LANES), F32),
-        ],
-        compiler_params=room(24),
+        scratch_shapes=scratch + [pltpu.VMEM((9 * LANES, LANES), BF16), pltpu.VMEM((tiles, LANES), F32)],
+        compiler_params=room(16),
         name="layers",
-    )(*(near(v) for v in (*fields, inner, outer, *strips, forward, backward)))
+    )(*(near(v) for v in (local, sibling, second, *strips, forward, backward, grad, sums)))
 
     grad = pl.pallas_call(
         functools.partial(grad_kernel, depth, rows, channels),

time: 50.4 us -> 48.7 us (0.966)
  starting transfers between devices: 25.4 us -> 20.3 us
  waiting for transfers between devices: 12.3 us -> 15.3 us
    ppermute x5, waiting for transfers between devices: 0.6 us -> 3.79 us  [the longest x1 2.25 us: per_device(): first = lax.ppermute(first, 'gx', across)]
    ppermute x11, starting transfers between devices: 15.2 us -> 12.3 us  [swap(): return lax.ppermute(value, axes, [(i, i ^ bits) for i in range(total)])]
    ppermute x5, starting transfers between devices: 10.2 us -> 8.02 us  [the longest x1 2.94 us: per_device(): first = lax.ppermute(first, 'gx', across)]
    pallas_call x1 -> x3, Pallas kernels: 6.21 us -> 7.65 us  [the longest x1 3.79 us: per_device(): pl.pallas_call(functools.partial(kernel, (1, 2)), out_shape=[pltpu.VMEM((...]
    pallas_call x1, Pallas kernels: 1.61 us -> 0.6 us  [per_device(): pl.pallas_call(functools.partial(pack_kernel, depth, rows), out_shape=[pl...]
  transfers between devices with their start and end apart: 16 -> 16, of which waited for: 10 -> 11; matrix products, arithmetic and copies ran while one was open for 0% -> 0% of each run, Pallas kernels for 5% -> 10%
where the time goes in v3:
time: 48.7 us; the launch traced here: 48.5 us
  starting transfers between devices  20.3 us (42%)
  waiting for transfers between devices  15.3 us (31%)
  Pallas kernels  12.1 us (25%)
  between operations  0.74 us (2%)
    ppermute x11, starting transfers between devices, swap(): return lax.ppermute(value, axes, [(i, i ^ bits) for i in range(total)])  12.3 us
    ppermute x11, waiting for transfers between devices, swap(): return lax.ppermute(value, axes, [(i, i ^ bits) for i in range(total)])  11.5 us
    pallas_call x1, Pallas kernels, per_device(): pl.pallas_call(functools.partial(kernel, (1, 2)), out_shape=[pltpu.VMEM((...  3.79 us
    ppermute x1, starting transfers between devices, per_device(): first = lax.ppermute(first, 'gx', across)  2.94 us
    pallas_call x1, Pallas kernels, per_device(): pl.pallas_call(functools.partial(kernel, (0,)), out_shape=[pltpu.VMEM(((r...  2.25 us
    ppermute x1, waiting for transfers between devices, per_device(): first = lax.ppermute(first, 'gx', across)  2.25 us
    pallas_call x1, Pallas kernels, per_device(): pl.pallas_call(functools.partial(weight_kernel, channels, depth), out_sha...  1.63 us
    pallas_call x1, Pallas kernels, per_device(): pl.pallas_call(fetch_kernel, out_shape=[pltpu.VMEM((4 * size, cols), F32)...  1.6 us
  transfers between devices with their start and end apart: 16, of which 11 were waited for; matrix products, arithmetic and copies ran while one was open for 0% of the time, Pallas kernels for 10%

profile of v3, /device:TPU:0, one launch (start us, length us, event | category | flops | bytes accessed | tf_op | source)
XLA Modules:
  0.0 48.5 jit_solution(1481421664072610405)
XLA Ops:
  0.6 1.6 %fetch.1 = (f32[1024,128]{1,0:T(8,128)S(1)}, f32[27,32,32]{2,1,0:T(8,128)S(1)}, f32[27,32,32]{2,1,0:T(8,128)S(1)}, f32[27,32,32]{2,1,0:T(8,128)S(1)}) custom-call(f32[256,128]{1,0:T(8,128)} %bitcast.5, f32[256,128]{1,0:T(8,128)} %bitcast.6, f32[256,128]{1,0:T(8,128)} %bitcast.7, f32[256,128]{1,0:T(8,128)} %bitcast.8, f32[27,32,32]{2,1,0:T(8,128)} %refs_4_.1, ...), custom_call_target="tpu_custom_call" | custom-call | tf_op jit(solution)/shard_map/fetch/pallas_call | solution.py:403
  2.2 0.5 %collective-permute-start = (f32[1024,128]{1,0:T(8,128)S(1)}, f32[1024,128]{1,0:T(8,128)S(1)}, u32[]{:S(2)}, u32[]{:S(2)}) collective-permute-start(f32[1024,128]{1,0:T(8,128)S(1)} %get-tuple-element.26.local.refs_0_), channel_id=1, source_target_pairs={{0,2},{2,0},{4,6},{6,4},{8,10},{10,8},{12,14},{14,12},{16,18},{18,... | collective-permute-start | bytes 1572872 | tf_op jit(solution)/shard_map/ppermute | solution.py:413
  2.8 1.5 %collective-permute-done.sibling.refs_1_ = f32[1024,128]{1,0:T(8,128)S(1)} collective-permute-done((f32[1024,128]{1,0:T(8,128)S(1)}, f32[1024,128]{1,0:T(8,128)S(1)}, u32[]{:S(2)}, u32[]{:S(2)}) %collective-permute-start) | collective-permute-done | bytes 524320 | tf_op jit(solution)/shard_map/ppermute | solution.py:413
  4.3 0.6 %pack.1 = (f32[448,128]{1,0:T(8,128)S(1)}, f32[320,128]{1,0:T(8,128)S(1)}, f32[128,128]{1,0:T(8,128)S(1)}, f32[64,128]{1,0:T(8,128)S(1)}) custom-call(f32[1024,128]{1,0:T(8,128)S(1)} %get-tuple-element.26.local.refs_0_, f32[1024,128]{1,0:T(8,128)S(1)} %collective-permute-done.sibling.refs_1_), custom_call_target="tpu_custom_call" | custom-call | tf_op jit(solution)/shard_map/pack/pallas_call | solution.py:417
  4.9 2.9 %collective-permute-start.4 = (f32[448,128]{1,0:T(8,128)S(1)}, f32[448,128]{1,0:T(8,128)S(1)}, u32[]{:S(2)}, u32[]{:S(2)}) collective-permute-start(f32[448,128]{1,0:T(8,128)S(1)} %get-tuple-element.37), channel_id=1, source_target_pairs={{0,4},{2,0},{4,8},{6,2},{8,12},{10,6},{12,16},{14,10},{16,20},{18,... | collective-permute-start | bytes 688136 | tf_op jit(solution)/shard_map/ppermute | solution.py:434
  7.9 1.5 %collective-permute-start.1 = (f32[128,128]{1,0:T(8,128)S(1)}, f32[128,128]{1,0:T(8,128)S(1)}, u32[]{:S(2)}, u32[]{:S(2)}) collective-permute-start(f32[128,128]{1,0:T(8,128)S(1)} %get-tuple-element.28), channel_id=1, source_target_pairs={{0,1},{1,0},{2,3},{3,2},{4,5},{5,4},{6,7},{7,6},{8,9},{9,8},{10,11... | collective-permute-start | bytes 196616 | tf_op jit(solution)/shard_map/ppermute | solution.py:435
  9.3 1.5 %collective-permute-start.3 = (f32[64,128]{1,0:T(8,128)S(1)}, f32[64,128]{1,0:T(8,128)S(1)}, u32[]{:S(2)}, u32[]{:S(2)}) collective-permute-start(f32[64,128]{1,0:T(8,128)S(1)} %get-tuple-element.31), channel_id=1, source_target_pairs={{0,5},{1,4},{2,1},{3,0},{4,9},{5,8},{6,3},{7,2},{8,13},{9,12},{10,... | collective-permute-start | bytes 98312 | tf_op jit(solution)/shard_map/ppermute | solution.py:436
  10.8 1.6 %weights.1 = (bf16[1152,384]{1,0:T(8,128)(2,1)S(1)}, bf16[1152,384]{1,0:T(8,128)(2,1)S(1)}) custom-call(f32[27,32,32]{2,1,0:T(8,128)S(1)} %get-tuple-element.32.refs_0_, f32[27,32,32]{2,1,0:T(8,128)S(1)} %get-tuple-element.33.refs_1_, f32[27,32,32]{2,1,0:T(8,128)S(1)} %get-tuple-element.34.refs_2_), custom_call_target="tpu_custom_call" | custom-call | flops 20000000 | bytes 4000000 | tf_op jit(solution)/shard_map/weights/pallas_call | solution.py:442
  12.5 0.0 collective-permute-done.1.refs_3_
  12.5 1.6 %collective-permute-start.2 = (f32[320,128]{1,0:T(8,128)S(1)}, f32[320,128]{1,0:T(8,128)S(1)}, u32[]{:S(2)}, u32[]{:S(2)}) collective-permute-start(f32[320,128]{1,0:T(8,128)S(1)} %get-tuple-element.29), channel_id=1, source_target_pairs={{0,4},{2,0},{4,8},{6,2},{8,12},{10,6},{12,16},{14,10},{16,20},{18,... | collective-permute-start | bytes 491528 | tf_op jit(solution)/shard_map/ppermute | solution.py:438
  14.1 0.0 collective-permute-done.3.refs_4_
  14.1 2.2 %collective-permute-done.4.refs_2_ = f32[448,128]{1,0:T(8,128)S(1)} collective-permute-done((f32[448,128]{1,0:T(8,128)S(1)}, f32[448,128]{1,0:T(8,128)S(1)}, u32[]{:S(2)}, u32[]{:S(2)}) %collective-permute-start.4) | collective-permute-done | bytes 229408 | tf_op jit(solution)/shard_map/ppermute | solution.py:434
  16.3 2.3 %layer_three.1 = (f32[576,128]{1,0:T(8,128)S(1)}, f32[224,128]{1,0:T(8,128)S(1)}) custom-call(f32[1024,128]{1,0:T(8,128)S(1)} %get-tuple-element.26.local.refs_0_, f32[1024,128]{1,0:T(8,128)S(1)} %collective-permute-done.sibling.refs_1_, f32[448,128]{1,0:T(8,128)S(1)} %collective-permute-done.4.refs_2_, f32[128,128]{1,0:T(8,128)S(1)} %collective-permute-done.1.refs_3_, ...), custom_call_target="tpu_custom_call" | custom-call | flops 3000000000 | bytes 3000000 | tf_op jit(solution)/shard_map/layer_three/pallas_call | solution.py:456
  18.6 0.0 collective-permute-done.2.refs_2_
  18.6 3.8 %layers.1 = (bf16[384,1536]{1,0:T(8,128)(2,1)S(1)}, f32[352,128]{1,0:T(8,128)S(1)}, f32[352,128]{1,0:T(8,128)S(1)}) custom-call(f32[1024,128]{1,0:T(8,128)S(1)} %get-tuple-element.26.local.refs_0_, f32[1024,128]{1,0:T(8,128)S(1)} %collective-permute-done.sibling.refs_1_, f32[320,128]{1,0:T(8,128)S(1)} %collective-permute-done.2.refs_2_, ...), custom_call_target="tpu_custom_call" | custom-call | tf_op jit(solution)/shard_map/layers/pallas_call | solution.py:469
  22.4 0.1 collective-permute-start.5
  22.5 1.4 %collective-permute-done.5 = f32[352,128]{1,0:T(8,128)S(1)} collective-permute-done((f32[352,128]{1,0:T(8,128)S(1)}, f32[352,128]{1,0:T(8,128)S(1)}, u32[]{:S(2)}, u32[]{:S(2)}) %collective-permute-start.5) | collective-permute-done | bytes 180256 | tf_op jit(solution)/shard_map/ppermute | solution.py:370
  23.9 3.5 %collective-permute-start.8 = (f32[88,128]{1,0:T(8,128)S(1)}, f32[88,128]{1,0:T(8,128)S(1)}, u32[]{:S(2)}, u32[]{:S(2)}) collective-permute-start(f32[88,128]{1,0:T(8,128)S(1)} %get-tuple-element.48), channel_id=1, source_target_pairs={{0,5},{1,4},{2,7},{3,6},{4,1},{5,0},{6,3},{7,2},{8,13},{9,12},{10,... | collective-permute-start | bytes 135176 | tf_op jit(solution)/shard_map/ppermute | solution.py:370
  27.4 0.0 collective-permute-start.7
  27.4 0.6 %collective-permute-start.6 = (f32[88,128]{1,0:T(8,128)S(1)}, f32[88,128]{1,0:T(8,128)S(1)}, u32[]{:S(2)}, u32[]{:S(2)}) collective-permute-start(f32[88,128]{1,0:T(8,128)S(1)} %get-tuple-element.50), channel_id=1, source_target_pairs={{0,1},{1,0},{2,3},{3,2},{4,5},{5,4},{6,7},{7,6},{8,9},{9,8},{10,11... | collective-permute-start | bytes 135176 | tf_op jit(solution)/shard_map/ppermute | solution.py:370
  28.0 1.0 %grad_input.1 = f32[256,128]{1,0:T(8,128)} custom-call(bf16[384,1536]{1,0:T(8,128)(2,1)S(1)} %get-tuple-element.42.hs, bf16[1152,384]{1,0:T(8,128)(2,1)S(1)} %get-tuple-element.36.refs_6_.backward), custom_call_target="tpu_custom_call" | custom-call | flops 600000000 | bytes 1000000 | tf_op jit(solution)/shard_map/grad_input/pallas_call | solution.py:483
  29.1 0.4 collective-permute-done.8
  29.4 2.0 %collective-permute-done.7 = f32[88,128]{1,0:T(8,128)S(1)} collective-permute-done((f32[88,128]{1,0:T(8,128)S(1)}, f32[88,128]{1,0:T(8,128)S(1)}, u32[]{:S(2)}, u32[]{:S(2)}) %collective-permute-start.7) | collective-permute-done | bytes 45088 | tf_op jit(solution)/shard_map/ppermute | solution.py:370
  31.4 0.0 collective-permute-done.6
  31.5 3.0 %collective-permute-start.11 = (f32[88,128]{1,0:T(8,128)S(1)}, f32[88,128]{1,0:T(8,128)S(1)}, u32[]{:S(2)}, u32[]{:S(2)}) collective-permute-start(f32[88,128]{1,0:T(8,128)S(1)} %fusion), channel_id=1, source_target_pairs={{0,24},{1,25},{2,26},{3,27},{4,28},{5,29},{6,30},{7,31},{8,16},{9,... | collective-permute-start | bytes 135176 | tf_op jit(solution)/shard_map/ppermute | solution.py:370
  34.4 0.1 collective-permute-start.10
  34.5 1.4 %collective-permute-start.9 = (f32[88,128]{1,0:T(8,128)S(1)}, f32[88,128]{1,0:T(8,128)S(1)}, u32[]{:S(2)}, u32[]{:S(2)}) collective-permute-start(f32[88,128]{1,0:T(8,128)S(1)} %fusion), channel_id=1, source_target_pairs={{0,8},{1,9},{2,10},{3,11},{4,12},{5,13},{6,14},{7,15},{8,0},{9,1},... | collective-permute-start | bytes 135176 | tf_op jit(solution)/shard_map/ppermute | solution.py:370
  35.9 1.5 %collective-permute-done.11 = f32[88,128]{1,0:T(8,128)S(1)} collective-permute-done((f32[88,128]{1,0:T(8,128)S(1)}, f32[88,128]{1,0:T(8,128)S(1)}, u32[]{:S(2)}, u32[]{:S(2)}) %collective-permute-start.11) | collective-permute-done | bytes 45088 | tf_op jit(solution)/shard_map/ppermute | solution.py:370
  37.4 2.2 %collective-permute-done.10 = f32[88,128]{1,0:T(8,128)S(1)} collective-permute-done((f32[88,128]{1,0:T(8,128)S(1)}, f32[88,128]{1,0:T(8,128)S(1)}, u32[]{:S(2)}, u32[]{:S(2)}) %collective-permute-start.10) | collective-permute-done | bytes 45088 | tf_op jit(solution)/shard_map/ppermute | solution.py:370
  39.5 0.0 collective-permute-done.9
  39.6 1.1 %collective-permute-start.14 = (f32[88,128]{1,0:T(8,128)S(1)}, f32[88,128]{1,0:T(8,128)S(1)}, u32[]{:S(2)}, u32[]{:S(2)}) collective-permute-start(f32[88,128]{1,0:T(8,128)S(1)} %add_add_fusion), channel_id=1, source_target_pairs={{0,5},{1,4},{2,7},{3,6},{4,1},{5,0},{6,3},{7,2},{8,13},{9,12},{10,... | collective-permute-start | bytes 135176 | tf_op jit(solution)/shard_map/ppermute | solution.py:370
  40.7 1.0 %collective-permute-start.13 = (f32[88,128]{1,0:T(8,128)S(1)}, f32[88,128]{1,0:T(8,128)S(1)}, u32[]{:S(2)}, u32[]{:S(2)}) collective-permute-start(f32[88,128]{1,0:T(8,128)S(1)} %add_add_fusion), channel_id=1, source_target_pairs={{0,4},{1,5},{2,6},{3,7},{4,0},{5,1},{6,2},{7,3},{8,12},{9,13},{10,... | collective-permute-start | bytes 135176 | tf_op jit(solution)/shard_map/ppermute | solution.py:370
  41.7 1.4 %collective-permute-start.12 = (f32[88,128]{1,0:T(8,128)S(1)}, f32[88,128]{1,0:T(8,128)S(1)}, u32[]{:S(2)}, u32[]{:S(2)}) collective-permute-start(f32[88,128]{1,0:T(8,128)S(1)} %add_add_fusion), channel_id=1, source_target_pairs={{0,1},{1,0},{2,3},{3,2},{4,5},{5,4},{6,7},{7,6},{8,9},{9,8},{10,11... | collective-permute-start | bytes 135176 | tf_op jit(solution)/shard_map/ppermute | solution.py:370
  43.1 1.5 %collective-permute-done.14 = f32[88,128]{1,0:T(8,128)S(1)} collective-permute-done((f32[88,128]{1,0:T(8,128)S(1)}, f32[88,128]{1,0:T(8,128)S(1)}, u32[]{:S(2)}, u32[]{:S(2)}) %collective-permute-start.14) | collective-permute-done | bytes 45088 | tf_op jit(solution)/shard_map/ppermute | solution.py:370
  44.6 0.4 collective-permute-done.13
  45.0 0.7 %collective-permute-done.12 = f32[88,128]{1,0:T(8,128)S(1)} collective-permute-done((f32[88,128]{1,0:T(8,128)S(1)}, f32[88,128]{1,0:T(8,128)S(1)}, u32[]{:S(2)}, u32[]{:S(2)}) %collective-permute-start.12) | collective-permute-done | bytes 45088 | tf_op jit(solution)/shard_map/ppermute | solution.py:370
  45.8 0.1 collective-permute-start.15
  45.9 1.4 %collective-permute-done.15.other = f32[352,128]{1,0:T(8,128)S(1)} collective-permute-done((f32[352,128]{1,0:T(8,128)S(1)}, f32[352,128]{1,0:T(8,128)S(1)}, u32[]{:S(2)}, u32[]{:S(2)}) %collective-permute-start.15) | collective-permute-done | bytes 180256 | tf_op jit(solution)/shard_map/ppermute | solution.py:370
  47.3 1.2 %unpack.1 = (f32[27,32,32]{2,1,0:T(8,128)}, f32[27,32,32]{2,1,0:T(8,128)}, f32[27,32,32]{2,1,0:T(8,128)}) custom-call(f32[352,128]{1,0:T(8,128)S(1)} %pad_maximum_fusion.mine, f32[352,128]{1,0:T(8,128)S(1)} %collective-permute-done.15.other), custom_call_target="tpu_custom_call" | custom-call | tf_op jit(solution)/shard_map/unpack/pallas_call | solution.py:494
  (5 shorter events, 0.1 us)
Async XLA Ops:
  2.2 2.1 %collective-permute-start = (f32[1024,128]{1,0:T(8,128)S(1)}, f32[1024,128]{1,0:T(8,128)S(1)}, u32[]{:S(2)}, u32[]{:S(2)}) collective-permute-start(f32[1024,128]{1,0:T(8,128)S(1)} %get-tuple-element.26.local.refs_0_), channel_id=1, source_target_pairs={{0,2},{2,0},{4,6},{6,4},{8,10},{10,8},{12,14},{14,12},{16,18},{18,... | collective-permute-start | bytes 1572872 | tf_op jit(solution)/shard_map/ppermute | solution.py:413
  4.9 11.4 %collective-permute-start.4 = (f32[448,128]{1,0:T(8,128)S(1)}, f32[448,128]{1,0:T(8,128)S(1)}, u32[]{:S(2)}, u32[]{:S(2)}) collective-permute-start(f32[448,128]{1,0:T(8,128)S(1)} %get-tuple-element.37), channel_id=1, source_target_pairs={{0,4},{2,0},{4,8},{6,2},{8,12},{10,6},{12,16},{14,10},{16,20},{18,... | collective-permute-start | bytes 688136 | tf_op jit(solution)/shard_map/ppermute | solution.py:434
  7.9 4.6 %collective-permute-start.1 = (f32[128,128]{1,0:T(8,128)S(1)}, f32[128,128]{1,0:T(8,128)S(1)}, u32[]{:S(2)}, u32[]{:S(2)}) collective-permute-start(f32[128,128]{1,0:T(8,128)S(1)} %get-tuple-element.28), channel_id=1, source_target_pairs={{0,1},{1,0},{2,3},{3,2},{4,5},{5,4},{6,7},{7,6},{8,9},{9,8},{10,11... | collective-permute-start | bytes 196616 | tf_op jit(solution)/shard_map/ppermute | solution.py:435
  9.3 4.7 %collective-permute-start.3 = (f32[64,128]{1,0:T(8,128)S(1)}, f32[64,128]{1,0:T(8,128)S(1)}, u32[]{:S(2)}, u32[]{:S(2)}) collective-permute-start(f32[64,128]{1,0:T(8,128)S(1)} %get-tuple-element.31), channel_id=1, source_target_pairs={{0,5},{1,4},{2,1},{3,0},{4,9},{5,8},{6,3},{7,2},{8,13},{9,12},{10,... | collective-permute-start | bytes 98312 | tf_op jit(solution)/shard_map/ppermute | solution.py:436
  12.5 6.1 %collective-permute-start.2 = (f32[320,128]{1,0:T(8,128)S(1)}, f32[320,128]{1,0:T(8,128)S(1)}, u32[]{:S(2)}, u32[]{:S(2)}) collective-permute-start(f32[320,128]{1,0:T(8,128)S(1)} %get-tuple-element.29), channel_id=1, source_target_pairs={{0,4},{2,0},{4,8},{6,2},{8,12},{10,6},{12,16},{14,10},{16,20},{18,... | collective-permute-start | bytes 491528 | tf_op jit(solution)/shard_map/ppermute | solution.py:438
  22.4 1.5 %collective-permute-start.5 = (f32[352,128]{1,0:T(8,128)S(1)}, f32[352,128]{1,0:T(8,128)S(1)}, u32[]{:S(2)}, u32[]{:S(2)}) collective-permute-start(f32[352,128]{1,0:T(8,128)S(1)} %get-tuple-element.41), channel_id=1, source_target_pairs={{0,2},{1,3},{2,0},{3,1},{4,6},{5,7},{6,4},{7,5},{8,10},{9,11},{10,... | collective-permute-start | bytes 540680 | tf_op jit(solution)/shard_map/ppermute | solution.py:370
  23.9 5.5 %collective-permute-start.8 = (f32[88,128]{1,0:T(8,128)S(1)}, f32[88,128]{1,0:T(8,128)S(1)}, u32[]{:S(2)}, u32[]{:S(2)}) collective-permute-start(f32[88,128]{1,0:T(8,128)S(1)} %get-tuple-element.48), channel_id=1, source_target_pairs={{0,5},{1,4},{2,7},{3,6},{4,1},{5,0},{6,3},{7,2},{8,13},{9,12},{10,... | collective-permute-start | bytes 135176 | tf_op jit(solution)/shard_map/ppermute | solution.py:370
  27.4 4.0 %collective-permute-start.7 = (f32[88,128]{1,0:T(8,128)S(1)}, f32[88,128]{1,0:T(8,128)S(1)}, u32[]{:S(2)}, u32[]{:S(2)}) collective-permute-start(f32[88,128]{1,0:T(8,128)S(1)} %get-tuple-element.49), channel_id=1, source_target_pairs={{0,4},{1,5},{2,6},{3,7},{4,0},{5,1},{6,2},{7,3},{8,12},{9,13},{10,... | collective-permute-start | bytes 135176 | tf_op jit(solution)/shard_map/ppermute | solution.py:370
  27.4 4.0 %collective-permute-start.6 = (f32[88,128]{1,0:T(8,128)S(1)}, f32[88,128]{1,0:T(8,128)S(1)}, u32[]{:S(2)}, u32[]{:S(2)}) collective-permute-start(f32[88,128]{1,0:T(8,128)S(1)} %get-tuple-element.50), channel_id=1, source_target_pairs={{0,1},{1,0},{2,3},{3,2},{4,5},{5,4},{6,7},{7,6},{8,9},{9,8},{10,11... | collective-permute-start | bytes 135176 | tf_op jit(solution)/shard_map/ppermute | solution.py:370
  31.5 5.9 %collective-permute-start.11 = (f32[88,128]{1,0:T(8,128)S(1)}, f32[88,128]{1,0:T(8,128)S(1)}, u32[]{:S(2)}, u32[]{:S(2)}) collective-permute-start(f32[88,128]{1,0:T(8,128)S(1)} %fusion), channel_id=1, source_target_pairs={{0,24},{1,25},{2,26},{3,27},{4,28},{5,29},{6,30},{7,31},{8,16},{9,... | collective-permute-start | bytes 135176 | tf_op jit(solution)/shard_map/ppermute | solution.py:370
  34.4 5.1 %collective-permute-start.10 = (f32[88,128]{1,0:T(8,128)S(1)}, f32[88,128]{1,0:T(8,128)S(1)}, u32[]{:S(2)}, u32[]{:S(2)}) collective-permute-start(f32[88,128]{1,0:T(8,128)S(1)} %fusion), channel_id=1, source_target_pairs={{0,16},{1,17},{2,18},{3,19},{4,20},{5,21},{6,22},{7,23},{8,24},{9,... | collective-permute-start | bytes 135176 | tf_op jit(solution)/shard_map/ppermute | solution.py:370
  34.5 5.0 %collective-permute-start.9 = (f32[88,128]{1,0:T(8,128)S(1)}, f32[88,128]{1,0:T(8,128)S(1)}, u32[]{:S(2)}, u32[]{:S(2)}) collective-permute-start(f32[88,128]{1,0:T(8,128)S(1)} %fusion), channel_id=1, source_target_pairs={{0,8},{1,9},{2,10},{3,11},{4,12},{5,13},{6,14},{7,15},{8,0},{9,1},... | collective-permute-start | bytes 135176 | tf_op jit(solution)/shard_map/ppermute | solution.py:370
  39.6 5.0 %collective-permute-start.14 = (f32[88,128]{1,0:T(8,128)S(1)}, f32[88,128]{1,0:T(8,128)S(1)}, u32[]{:S(2)}, u32[]{:S(2)}) collective-permute-start(f32[88,128]{1,0:T(8,128)S(1)} %add_add_fusion), channel_id=1, source_target_pairs={{0,5},{1,4},{2,7},{3,6},{4,1},{5,0},{6,3},{7,2},{8,13},{9,12},{10,... | collective-permute-start | bytes 135176 | tf_op jit(solution)/shard_map/ppermute | solution.py:370
  40.7 4.4 %collective-permute-start.13 = (f32[88,128]{1,0:T(8,128)S(1)}, f32[88,128]{1,0:T(8,128)S(1)}, u32[]{:S(2)}, u32[]{:S(2)}) collective-permute-start(f32[88,128]{1,0:T(8,128)S(1)} %add_add_fusion), channel_id=1, source_target_pairs={{0,4},{1,5},{2,6},{3,7},{4,0},{5,1},{6,2},{7,3},{8,12},{9,13},{10,... | collective-permute-start | bytes 135176 | tf_op jit(solution)/shard_map/ppermute | solution.py:370
  41.7 4.0 %collective-permute-start.12 = (f32[88,128]{1,0:T(8,128)S(1)}, f32[88,128]{1,0:T(8,128)S(1)}, u32[]{:S(2)}, u32[]{:S(2)}) collective-permute-start(f32[88,128]{1,0:T(8,128)S(1)} %add_add_fusion), channel_id=1, source_target_pairs={{0,1},{1,0},{2,3},{3,2},{4,5},{5,4},{6,7},{7,6},{8,9},{9,8},{10,11... | collective-permute-start | bytes 135176 | tf_op jit(solution)/shard_map/ppermute | solution.py:370
  45.8 1.5 %collective-permute-start.15 = (f32[352,128]{1,0:T(8,128)S(1)}, f32[352,128]{1,0:T(8,128)S(1)}, u32[]{:S(2)}, u32[]{:S(2)}) collective-permute-start(f32[352,128]{1,0:T(8,128)S(1)} %pad_maximum_fusion.mine), channel_id=1, source_target_pairs={{0,2},{1,3},{2,0},{3,1},{4,6},{5,7},{6,4},{7,5},{8,10},{9,11},{10,... | collective-permute-start | bytes 540680 | tf_op jit(solution)/shard_map/ppermute | solution.py:370

commit v4 on v3

v4 whole, which is shorter than its diff:
```python
import functools
import math

import jax
import jax.numpy as jnp
from jax import lax
from jax.experimental import pallas as pl
from jax.experimental.pallas import tpu as pltpu
from jax.sharding import PartitionSpec as P

inv_root_two = 0.7071067811865476
inv_root_two_pi = 0.3989422804014327

LAYERS = 3
HALO = LAYERS + 1
SIDE = 2 * HALO
LANES = 128
F32 = jnp.float32
BF16 = jnp.bfloat16
NN = (((1,), (0,)), ((), ()))
NT = (((1,), (1,)), ((), ()))

WIDTHS = (LAYERS, LAYERS - 1, LAYERS - 1, LAYERS - 2)
STARTS = tuple(sum(WIDTHS[:f]) for f in range(4))
SLABS = sum(WIDTHS)


def gelu_slope(value):
    normal_cdf = 0.5 * (1.0 + lax.erf(value * inv_root_two))
    density = jnp.exp(-0.5 * value * value) * inv_root_two_pi
    return normal_cdf + value * density


def roll(value, shift):
    shift %= LANES
    return pltpu.roll(value, shift, 1) if shift else value


def lane_index(rows):
    return lax.broadcasted_iota(jnp.int32, (rows, LANES), 1)


def near(value):
    return pltpu.with_memory_space_constraint(value, pltpu.VMEM)


def far(value):
    return pltpu.with_memory_space_constraint(value, pltpu.HBM)


def room(mib):
    return pltpu.CompilerParams(vmem_limit_bytes=mib * 1024 * 1024)


def vmem(count):
    return [pl.BlockSpec(memory_space=pltpu.VMEM)] * count


def slab_at(ref, field, depth, rows, row):
    size = ref.shape[0] // 4
    channels = size // (depth * rows)
    parts = [
        ref[pl.ds(field * size + z * rows + row, channels, stride=depth * rows), :] for z in range(depth)
    ]
    return jnp.concatenate(parts, axis=0)


def split(value):
    high = value.astype(BF16)
    low = (value - high.astype(F32)).astype(BF16)
    return high, low


def fetch_kernel(*refs):
    count = 4 + LAYERS
    sources, (local, *kernels), semaphores = refs[:count], refs[count : count + 1 + LAYERS], refs[-1]
    size = sources[0].shape[0]
    targets = [local.at[pl.ds(f * size, size), :] for f in range(4)] + kernels
    copies = [
        pltpu.make_async_copy(source, target, semaphores.at[k])
        for k, (source, target) in enumerate(zip(sources, targets))
    ]
    for copy in copies:
        copy.start()
    for copy in copies:
        copy.wait()


def pack_rows(depth, rows, sibling, out):
    odd = lax.rem(lax.axis_index("gx"), 2)
    planes = sibling.shape[0] // (4 * rows)
    for f, width in enumerate(WIDTHS):
        for j in range(width):
            row = (rows - width) * (1 - odd) + j
            out[pl.ds((STARTS[f] + j) * planes, planes), :] = slab_at(sibling, f, depth, rows, row)


def pack_strips(depth, rows, local, sibling, strips, strip):
    planes = local.shape[0] // (4 * rows)
    lane = lane_index(planes)
    for k, ref in enumerate((local, sibling)):
        total = jnp.zeros((planes, LANES), F32)
        for f in range(4):
            for r in range(rows):
                value = slab_at(ref, f, depth, rows, r)
                base = (f * rows + r) * SIDE
                here = (lane >= base) & (lane < base + SIDE)
                total = jnp.where(here, roll(value, base + HALO), total)
        strips[pl.ds(k * planes, planes), :] = total
    strip[...] = total


def weight_kernel(channels, depth, *refs):
    kernels, (forward, backward) = refs[:LAYERS], refs[LAYERS:]
    planes = channels * depth
    in_low = lax.rem(lane_index(channels), planes) < channels
    for layer in range(LAYERS):
        for b in range(3):
            for c in range(3):
                tiles = []
                for a in range(3):
                    tap = kernels[layer][9 * a + 3 * b + c]
                    tiles.append(jnp.concatenate([tap] * (LANES // channels), axis=1))
                upper = jnp.where(in_low, tiles[1], tiles[2])
                lower = jnp.where(in_low, tiles[0], tiles[1])
                whole = jnp.concatenate([upper, lower], axis=0)
                turned = jnp.concatenate([whole, whole], axis=0).T[:planes]
                for ref, value, bb, cc in ((forward, whole, b, c), (backward, turned, 2 - b, 2 - c)):
                    base, lanes = layer * 2 * planes, pl.ds((bb * 3 + cc) * LANES, LANES)
                    high, low = split(value)
                    ref[pl.ds(base, planes), lanes] = high
                    ref[pl.ds(base + planes, planes), lanes] = low


def conv(weights, layer, window):
    planes = weights.shape[0] // (LAYERS * 2)
    kernel = weights[pl.ds(layer * 2 * planes, 2 * planes), :]
    total = lax.dot_general(kernel, window, NN, preferred_element_type=F32)
    return total[:planes] + total[planes:]


def conv_rows(weights, layer, source, low, high):
    out = {}
    for e in range(low, high, 2):
        count = min(2, high - e)
        window = [source[:, pl.ds((e + b - 1) * LANES, count * LANES)] for b in range(3)]
        value = conv(weights, layer, jnp.concatenate(window, axis=0))
        for k in range(count):
            out[e + k] = value[:, k * LANES : (k + 1) * LANES]
    return out


def store_shifted(main, side, into, into_side=None):
    planes = side.shape[0]
    lane = lane_index(planes)
    ahead, behind = side, side

    def store(target, c, lanes, value):
        high, low = split(value)
        target[pl.ds(c * LANES, planes), lanes] = high
        target[pl.ds(c * LANES + planes, planes), lanes] = low

    for e, value in main.items():
        base = e * SIDE
        ends = roll(side, -base)
        down = roll(jnp.where(lane == LANES - 1, ends, value), 1)
        up = roll(jnp.where(lane == 0, ends, value), -1)
        for c, shifted in enumerate((down, value, up)):
            store(into, c, pl.ds(e * LANES, LANES), shifted)
        if into_side is not None:
            value = roll(value, base)
            ahead = jnp.where(lane == base, value, ahead)
            behind = jnp.where(lane == (base - 1) % LANES, value, behind)
    if into_side is not None:
        for c, shifted in enumerate((roll(behind, 1), side, roll(ahead, -1))):
            store(into_side, c, pl.ds(0, LANES), shifted)


def conv_side(weights, layer, shifted):
    planes = weights.shape[0] // (LAYERS * 2)
    parts = []
    for b in range(3):
        kernel = weights[pl.ds(layer * 2 * planes, 2 * planes), pl.ds(b * 3 * LANES, 3 * LANES)]
        part = lax.dot_general(kernel, shifted[...], NN, preferred_element_type=F32)
        parts.append(roll(part[:planes] + part[planes:], -(b - 1) * SIDE))
    return parts[0] + parts[1] + parts[2]


def layers_kernel(depth, rows, channels, gy_rounds, factor, *refs):
    local, sibling, outer = refs[:3]
    strips = refs[3 : 3 + 2 * gy_rounds]
    forward, backward, h_out, keep, send, xs, xside, hs, hside, gsum = refs[3 + 2 * gy_rounds :]
    planes = depth * channels
    gx, gy = lax.axis_index("gx"), lax.axis_index("gy")
    gx_size, gy_size = lax.axis_size("gx"), lax.axis_size("gy")
    x_odd, y_odd = lax.rem(gx, 2) == 1, lax.rem(gy, 2) == 1
    odd = lax.rem(gx, 2)
    ended = (gx == 0) | (gx == gx_size - 1)
    lane = lane_index(planes)
    right = lax.rem(lane, SIDE) >= HALO
    zero = jnp.zeros((planes, LANES), F32)

    def side_strip(group):
        got = []
        for r in range(gy_rounds):
            if group < 2:
                got.append(strips[r][pl.ds(group * planes, planes), :])
            else:
                got.append(jnp.where(ended, 0.0, strips[gy_rounds + r][...]))
        if gy_rounds == 0:
            return zero
        if gy_rounds == 1:
            got.append(zero)
        from_right = jnp.where(y_odd, got[1], got[0])
        from_left = jnp.where(y_odd, got[0], got[1])
        return jnp.where(right, from_right, from_left)

    own_strip, inner_strip, outer_strip = (side_strip(g) for g in range(3))
    before_strip = jnp.where(x_odd, inner_strip, outer_strip)
    after_strip = jnp.where(x_odd, outer_strip, inner_strip)
    span = rows * SIDE

    def field_parts(f):
        width = WIDTHS[f]
        main = {}
        for j in range(width):
            start = STARTS[f] + j
            a = slab_at(sibling, f, depth, rows, (rows - width) * odd + j)
            b = jnp.where(ended, 0.0, outer[pl.ds(start * planes, planes), :])
            main[HALO - width + j] = jnp.where(x_odd, a, b)
            main[HALO + rows + j] = jnp.where(x_odd, b, a)
        for r in range(rows):
            main[HALO + r] = slab_at(local, f, depth, rows, r)
        lead = HALO * SIDE - HALO
        before = roll(before_strip, lead - span - f * span)
        own = roll(own_strip, lead - f * span)
        after = roll(after_strip, lead + span - f * span)
        side = jnp.where(lane < lead, before, jnp.where(lane < lead + span, own, after))
        side = jnp.where(lane < lead + 2 * span, side, 0.0)
        return main, side

    side_row = (lane + HALO) // SIDE
    right = lax.rem(lane + HALO, SIDE) >= HALO
    row_low = jnp.where(gx > 0, 0, HALO)
    row_high = jnp.where(gx < gx_size - 1, 2 * HALO + rows, HALO + rows)
    col_ok = jnp.where(right, (gy < gy_size - 1).astype(jnp.int32), (gy > 0).astype(jnp.int32))
    side_ok = (side_row >= row_low) & (side_row < row_high) & (col_ok > 0)

    padding = gsum.shape[0] - LAYERS * 7 * channels
    if padding:
        gsum[pl.ds(LAYERS * 7 * channels, padding), :] = jnp.zeros((padding, LANES), F32)
    grad_main, grad_side = field_parts(1)
    half = lane_index(channels)
    for layer in range(LAYERS):
        x_main, x_side = field_parts((0, 2, 3)[layer])
        store_shifted(x_main, x_side, xs, xside)
        h_width = LAYERS - 1 - layer
        low, high = HALO - h_width, HALO + rows + h_width
        pre = conv_rows(forward, layer, xs, low, high)
        h_main = {}
        for e in range(low, high):
            value = grad_main[e] * gelu_slope(pre[e])
            if e < HALO:
                value = jnp.where(gx > 0, value, 0.0)
            if e >= HALO + rows:
                value = jnp.where(gx < gx_size - 1, value, 0.0)
            h_main[e] = value
        h_side = jnp.where(side_ok, grad_side * gelu_slope(conv_side(forward, layer, xside)), 0.0)
        if h_width:
            store_shifted(h_main, h_side, hs, hside)
            own = hs[pl.ds(LANES, 2 * planes), pl.ds(HALO * LANES, rows * LANES)]
        else:
            parts = [split(h_main[HALO + r]) for r in range(rows)]
            own = [jnp.concatenate([part[k] for part in parts], axis=1) for k in range(2)]
            own = jnp.concatenate(own, axis=0)
        tiles, extra = [], []
        for b in range(3):
            window = xs[:, pl.ds((HALO + b - 1) * LANES, rows * LANES)]
            product = lax.dot_general(own, window, NT, preferred_element_type=F32)
            product = product[:planes] + product[planes:]
            for c in range(3):
                tile = product[:, c * LANES : (c + 1) * LANES]
                tile = (tile + roll(tile, planes)) * factor
                upper, lower = tile[:channels], tile[channels:]
                middle = upper + roll(lower, -channels)
                tiles.append(jnp.where(half < channels, lower, jnp.where(half < 2 * channels, upper, middle)))
        for m in range(7):
            tile = tiles[m]
            if m < 6:
                source, part = tiles[7 + m // 3], m % 3
                tile = jnp.where(half < 3 * channels, tile, roll(source, (3 - part) * channels))
            gsum[pl.ds((layer * 7 + m) * channels, channels), :] = tile

        if h_width:
            g_width = h_width - 1
            grad_main = conv_rows(backward, layer, hs, HALO - g_width, HALO + rows + g_width)
            grad_side = conv_side(backward, layer, hside)

    for r in range(rows):
        h_out[pl.ds(r * planes, planes), :] = h_main[HALO + r]
    h_out[pl.ds(rows * planes, planes), :] = h_side
    head, tail = h_main[HALO], h_main[HALO + rows - 1]
    base = keep.shape[0]
    send[pl.ds(base, planes), :] = jnp.where(x_odd, head, tail)
    send[pl.ds(base + planes, planes), :] = jnp.where(x_odd, tail, head)
    send[pl.ds(base + 2 * planes, planes), :] = h_side
    size = keep.shape[0] // 4
    core, quad = quad_place(gx, gy)
    for k in range(4):
        piece = lax.bitwise_xor(quad, k) * size
        at = pl.ds(k * size, size)
        keep[at, :] = gsum[pl.ds(pl.multiple_of(core * 4 * size + piece, 8), size), :]
        send[at, :] = gsum[pl.ds(pl.multiple_of((1 - core) * 4 * size + piece, 8), size), :]


def quad_place(gx, gy):
    return lax.rem(gx, 2), lax.rem(gy, 2) + 2 * lax.rem(gx // 2, 2)


def grad_kernel(depth, rows, channels, own, swapped, ringed, backward, grad_out, hs):
    planes = depth * channels
    gx, gx_size = lax.axis_index("gx"), lax.axis_size("gx")
    x_odd, ended = lax.rem(gx, 2) == 1, (gx == 0) | (gx == gx_size - 1)
    lane = lane_index(planes)
    span = rows * SIDE
    inner, inner_side = swapped[pl.ds(0, planes), :], swapped[pl.ds(2 * planes, planes), :]
    outer = jnp.where(ended, 0.0, ringed[pl.ds(0, planes), :])
    outer_side = jnp.where(ended, 0.0, ringed[pl.ds(planes, planes), :])
    main = {HALO + r: own[pl.ds(r * planes, planes), :] for r in range(rows)}
    main[HALO - 1] = jnp.where(x_odd, inner, outer)
    main[HALO + rows] = jnp.where(x_odd, outer, inner)
    before = roll(jnp.where(x_odd, inner_side, outer_side), -span)
    after = roll(jnp.where(x_odd, outer_side, inner_side), span)
    side = own[pl.ds(rows * planes, planes), :]
    lead = HALO * SIDE - HALO
    side = jnp.where(lane < lead, before, jnp.where(lane < lead + span, side, after))
    store_shifted(main, side, hs)
    grad_main = conv_rows(backward, LAYERS - 1, hs, HALO, HALO + rows)
    for r in range(rows):
        for z in range(depth):
            at = pl.ds(z * rows + r, channels, stride=depth * rows)
            grad_out[at, :] = grad_main[HALO + r][z * channels : (z + 1) * channels]


def unpack_kernel(channels, mine, other, *refs):
    outs, whole = refs[:LAYERS], refs[LAYERS]
    size = mine.shape[0] // 4
    core, quad = quad_place(lax.axis_index("gx"), lax.axis_index("gy"))
    for k in range(4):
        piece = lax.bitwise_xor(quad, k) * size
        at = pl.ds(k * size, size)
        whole[pl.ds(pl.multiple_of(core * 4 * size + piece, 8), size), :] = mine[at, :]
        whole[pl.ds(pl.multiple_of((1 - core) * 4 * size + piece, 8), size), :] = other[at, :]
    order = (0, 2, 1)
    for layer in range(LAYERS):
        for m in range(7):
            tile = whole[pl.ds((layer * 7 + m) * channels, channels), :]
            for s in range(4):
                if s < 3:
                    tap = 9 * order[s] + m
                elif m < 6:
                    tap = 9 * order[m % 3] + 7 + m // 3
                else:
                    continue
                outs[layer][tap] = roll(tile, -s * channels)[:, :channels]


def pair_rounds(size):
    rounds = []
    for start in range(2):
        pairs = [(i, i + 1) for i in range(start, size - 1, 2)]
        if pairs:
            rounds.append(pairs + [(j, i) for i, j in pairs])
    return rounds


def reduce_halves(keep, send, beside, gx_size, gy_size):
    axes = ("gx", "gy")
    total = gx_size * gy_size

    def swap(value, bits):
        return lax.ppermute(value, axes, [(i, i ^ bits) for i in range(total)])

    core, quad = gy_size, (1, 2 * gy_size, 2 * gy_size + 1)
    got = swap(send, core)
    count = keep.shape[0]
    value, beside = keep + got[:count], beside(got[count:])
    size = value.shape[0] // 4
    pieces = [value[k * size : (k + 1) * size] for k in range(4)]
    got = [swap(pieces[k + 1], quad[k]) for k in range(3)]
    value = (pieces[0] + got[0]) + (got[1] + got[2])
    bits = [gy_size << k for k in range(2, gx_size.bit_length() - 1)]
    bits += [1 << k for k in range(1, gy_size.bit_length() - 1)]
    while bits:
        low, *high = bits[:2]
        if high:
            got = [swap(value, b) for b in (low, high[0], low | high[0])]
            value = (value + got[0]) + (got[1] + got[2])
        else:
            value = value + swap(value, low)
        bits = bits[2:]
    value, beside = lax.optimization_barrier((value, beside))
    value = jnp.concatenate([value] + [swap(value, b) for b in quad])
    return value, swap(value, core), beside


def per_device(input_one, input_two, input_three, cotangent, kernel_one, kernel_two, kernel_three):
    channels, depth, rows, cols = input_one.shape
    gx_size, gy_size = lax.axis_size("gx"), lax.axis_size("gy")
    planes = channels * depth
    factor = 1.0 / math.sqrt(depth * rows * cols * gx_size * gy_size)
    fields = [v.reshape(planes * rows, cols) for v in (input_three, cotangent, input_two, input_one)]
    shape = jax.ShapeDtypeStruct

    kernels = [kernel_three, kernel_two, kernel_one]
    size = planes * rows
    local, *kernels = pl.pallas_call(
        fetch_kernel,
        out_shape=[pltpu.VMEM((4 * size, cols), F32)] + [pltpu.VMEM(v.shape, F32) for v in kernels],
        in_specs=[pl.BlockSpec(memory_space=pltpu.HBM)] * (4 + LAYERS),
        out_specs=vmem(1 + LAYERS),
        scratch_shapes=[pltpu.SemaphoreType.DMA((4 + LAYERS,))],
        compiler_params=room(8),
        name="fetch",
    )(*(far(v) for v in fields + kernels))

    sibling = lax.ppermute(local, "gx", [(i, i ^ 1) for i in range(gx_size)])
    across = [(i, i - 2) if i % 2 else (i, i + 2) for i in range(gx_size)]
    across = [(i, j) if 0 <= j < gx_size else (i, i ^ 1) for i, j in across]
    y_rounds = pair_rounds(gy_size)
    weight_shape = pltpu.VMEM((LAYERS * 2 * planes, 9 * LANES), BF16)
    forward, backward = pl.pallas_call(
        functools.partial(weight_kernel, channels, depth),
        out_shape=[weight_shape, weight_shape],
        in_specs=vmem(LAYERS),
        out_specs=vmem(2),
        cost_estimate=pl.CostEstimate(flops=20_000_000, bytes_accessed=4_000_000, transcendentals=0),
        compiler_params=room(12),
        name="weights",
    )(*(near(v) for v in kernels))

    sibling, forward, backward = lax.optimization_barrier((sibling, forward, backward))
    outer = pl.pallas_call(
        functools.partial(pack_rows, depth, rows),
        out_shape=pltpu.VMEM((SLABS * planes, cols), F32),
        in_specs=vmem(1),
        out_specs=vmem(1)[0],
        compiler_params=room(8),
        name="pack_rows",
    )(near(sibling))
    strips, strip = pl.pallas_call(
        functools.partial(pack_strips, depth, rows),
        out_shape=[pltpu.VMEM((2 * planes, cols), F32), pltpu.VMEM((planes, cols), F32)],
        in_specs=vmem(2),
        out_specs=vmem(2),
        compiler_params=room(8),
        cost_estimate=pl.CostEstimate(flops=5_000_000, bytes_accessed=2_000_000, transcendentals=0),
        name="pack_strips",
    )(near(local), near(sibling))

    def diagonal(x_pairs, y_pairs):
        return [(i * gy_size + k, j * gy_size + m) for i, j in x_pairs for k, m in y_pairs]

    outer = lax.ppermute(outer, "gx", across)
    corners = [lax.ppermute(strip, ("gx", "gy"), diagonal(across, pairs)) for pairs in y_rounds]
    strips = [lax.ppermute(strips, "gy", pairs) for pairs in y_rounds] + corners

    tiles = -(-LAYERS * 7 * channels // 64) * 64
    span = (2 * HALO + rows) * LANES
    shifted, shifted_side = pltpu.VMEM((3 * LANES, span), BF16), pltpu.VMEM((3 * LANES, LANES), BF16)
    h_own, keep, send = pl.pallas_call(
        functools.partial(layers_kernel, depth, rows, channels, len(y_rounds), factor),
        out_shape=[
            pltpu.VMEM(((rows + 1) * planes, LANES), F32),
            pltpu.VMEM((tiles // 2, LANES), F32),
            pltpu.VMEM((tiles // 2 + 3 * planes, LANES), F32),
        ],
        in_specs=vmem(5 + len(strips)),
        out_specs=vmem(3),
        scratch_shapes=[shifted, shifted_side] * 2 + [pltpu.VMEM((tiles, LANES), F32)],
        compiler_params=room(16),
        name="layers",
    )(*(near(v) for v in (local, sibling, outer, *strips, forward, backward)))

    def input_gradient(swapped):
        ringed = lax.ppermute(swapped[planes:], "gx", across)
        return pl.pallas_call(
            functools.partial(grad_kernel, depth, rows, channels),
            out_shape=shape((planes * rows, cols), F32),
            in_specs=vmem(4),
            out_specs=vmem(1)[0],
            scratch_shapes=[shifted],
            compiler_params=room(8),
            cost_estimate=pl.CostEstimate(flops=600_000_000, bytes_accessed=1_000_000, transcendentals=0),
            name="grad_input",
        )(near(h_own), near(swapped), near(ringed), near(backward))

    mine, other, grad = reduce_halves(keep, send, input_gradient, gx_size, gy_size)
    results = pl.pallas_call(
        functools.partial(unpack_kernel, channels),
        out_shape=[shape(kernel_one.shape, F32)] * LAYERS,
        in_specs=vmem(2),
        out_specs=vmem(LAYERS),
        scratch_shapes=[pltpu.VMEM((tiles, LANES), F32)],
        compiler_params=room(8),
        name="unpack",
    )(near(mine), near(other))
    return (grad.reshape(input_one.shape), results[2], results[1], results[0])


def solution(mesh):
    placed = (
        P(None, None, "gx", "gy"),
        P(None, None, "gx", "gy"),
        P(None, None, "gx", "gy"),
        P(None, None, "gx", "gy"),
        P(),
        P(),
        P(),
    )
    return jax.shard_map(
        per_device,
        mesh=mesh,
        in_specs=placed,
        out_specs=(P(None, None, "gx", "gy"), P(), P(), P()),
        check_vma=False,
    )
```

time: 48.7 us -> 47 us (0.965)
  waiting for transfers between devices: 15.3 us -> 13.7 us
    ppermute x1, waiting for transfers between devices: 0.01 us -> 1.85 us  [per_device(): lax.ppermute(strip, ('gx', 'gy'), diagonal(across, pairs))]
    ppermute x11, waiting for transfers between devices: 11.5 us -> 9.69 us  [swap(): return lax.ppermute(value, axes, [(i, i ^ bits) for i in range(total)])]
    ppermute x1, waiting for transfers between devices: 1.54 us -> 0.01 us  [per_device(): sibling = lax.ppermute(local, 'gx', [(i, i ^ 1) for i in range(gx_size)])]
  transfers between devices with their start and end apart: 16 -> 16, of which waited for: 11 -> 8; matrix products, arithmetic and copies ran while one was open for 0% -> 0% of each run, Pallas kernels for 10% -> 7%
where the time goes in v4:
time: 47 us; the launch traced here: 46.8 us
  starting transfers between devices  20.6 us (44%)
  waiting for transfers between devices  13.7 us (29%)
  Pallas kernels  11.7 us (25%)
  between operations  0.75 us (2%)
    ppermute x11, starting transfers between devices, swap(): return lax.ppermute(value, axes, [(i, i ^ bits) for i in range(total)])  12.3 us
    ppermute x11, waiting for transfers between devices, swap(): return lax.ppermute(value, axes, [(i, i ^ bits) for i in range(total)])  9.69 us
    pallas_call x1, Pallas kernels, per_device(): pl.pallas_call(functools.partial(layers_kernel, depth, rows, channels, le...  5.56 us
    ppermute x1, starting transfers between devices, per_device(): outer = lax.ppermute(outer, 'gx', across)  2.82 us
    ppermute x1, waiting for transfers between devices, per_device(): outer = lax.ppermute(outer, 'gx', across)  2.16 us
    ppermute x1, starting transfers between devices, input_gradient(): ringed = lax.ppermute(swapped[planes:], 'gx', across)  1.91 us
    ppermute x1, waiting for transfers between devices, per_device(): lax.ppermute(strip, ('gx', 'gy'), diagonal(across, pairs))  1.85 us
    pallas_call x1, Pallas kernels, per_device(): pl.pallas_call(functools.partial(weight_kernel, channels, depth), out_sha...  1.63 us
  transfers between devices with their start and end apart: 16, of which 8 were waited for; matrix products, arithmetic and copies ran while one was open for 0% of the time, Pallas kernels for 7%

profile of v4, /device:TPU:0, one launch (start us, length us, event | category | flops | bytes accessed | tf_op | source)
XLA Modules:
  0.0 46.8 jit_solution(11261860121196582214)
XLA Ops:
  0.6 1.6 %fetch.1 = (f32[1024,128]{1,0:T(8,128)S(1)}, f32[27,32,32]{2,1,0:T(8,128)S(1)}, f32[27,32,32]{2,1,0:T(8,128)S(1)}, f32[27,32,32]{2,1,0:T(8,128)S(1)}) custom-call(f32[256,128]{1,0:T(8,128)} %bitcast.5, f32[256,128]{1,0:T(8,128)} %bitcast.6, f32[256,128]{1,0:T(8,128)} %bitcast.7, f32[256,128]{1,0:T(8,128)} %bitcast.8, f32[27,32,32]{2,1,0:T(8,128)} %refs_4_.1, ...), custom_call_target="tpu_custom_call" | custom-call | tf_op jit(solution)/shard_map/fetch/pallas_call | solution.py:417
  2.2 0.5 %collective-permute-start = (f32[1024,128]{1,0:T(8,128)S(1)}, f32[1024,128]{1,0:T(8,128)S(1)}, u32[]{:S(2)}, u32[]{:S(2)}) collective-permute-start(f32[1024,128]{1,0:T(8,128)S(1)} %get-tuple-element.23.local.refs_0_), channel_id=1, source_target_pairs={{0,2},{2,0},{4,6},{6,4},{8,10},{10,8},{12,14},{14,12},{16,18},{18,... | collective-permute-start | bytes 1572872 | tf_op jit(solution)/shard_map/ppermute | solution.py:427
  2.8 1.6 %weights.1 = (bf16[384,1152]{1,0:T(8,128)(2,1)S(1)}, bf16[384,1152]{1,0:T(8,128)(2,1)S(1)}) custom-call(f32[27,32,32]{2,1,0:T(8,128)S(1)} %get-tuple-element.24.refs_0_, f32[27,32,32]{2,1,0:T(8,128)S(1)} %get-tuple-element.25.refs_1_, f32[27,32,32]{2,1,0:T(8,128)S(1)} %get-tuple-element.26.refs_2_), custom_call_target="tpu_custom_call" | custom-call | flops 20000000 | bytes 4000000 | tf_op jit(solution)/shard_map/weights/pallas_call | solution.py:432
  4.4 0.0 collective-permute-done.sibling.refs_1_
  4.4 0.1 pack_rows.1
  4.5 2.8 %collective-permute-start.1 = (f32[512,128]{1,0:T(8,128)S(1)}, f32[512,128]{1,0:T(8,128)S(1)}, u32[]{:S(2)}, u32[]{:S(2)}) collective-permute-start(f32[512,128]{1,0:T(8,128)S(1)} %pack_rows.1), channel_id=1, source_target_pairs={{0,4},{2,0},{4,8},{6,2},{8,12},{10,6},{12,16},{14,10},{16,20},{18,... | collective-permute-start | bytes 786440 | tf_op jit(solution)/shard_map/ppermute | solution.py:464
  7.3 0.3 pack_strips.1
  7.6 1.6 %collective-permute-start.2 = (f32[128,128]{1,0:T(8,128)S(1)}, f32[128,128]{1,0:T(8,128)S(1)}, u32[]{:S(2)}, u32[]{:S(2)}) collective-permute-start(f32[128,128]{1,0:T(8,128)S(1)} %get-tuple-element.30), channel_id=1, source_target_pairs={{0,1},{1,0},{2,3},{3,2},{4,5},{5,4},{6,7},{7,6},{8,9},{9,8},{10,11... | collective-permute-start | bytes 196616 | tf_op jit(solution)/shard_map/ppermute | solution.py:466
  9.2 1.5 %collective-permute-start.3 = (f32[64,128]{1,0:T(8,128)S(1)}, f32[64,128]{1,0:T(8,128)S(1)}, u32[]{:S(2)}, u32[]{:S(2)}) collective-permute-start(f32[64,128]{1,0:T(8,128)S(1)} %get-tuple-element.31), channel_id=1, source_target_pairs={{0,5},{1,4},{2,1},{3,0},{4,9},{5,8},{6,3},{7,2},{8,13},{9,12},{10,... | collective-permute-start | bytes 98312 | tf_op jit(solution)/shard_map/ppermute | solution.py:465
  10.7 1.8 %collective-permute-done.3.refs_4_ = f32[64,128]{1,0:T(8,128)S(1)} collective-permute-done((f32[64,128]{1,0:T(8,128)S(1)}, f32[64,128]{1,0:T(8,128)S(1)}, u32[]{:S(2)}, u32[]{:S(2)}) %collective-permute-start.3) | collective-permute-done | bytes 32800 | tf_op jit(solution)/shard_map/ppermute | solution.py:465
  12.5 0.0 collective-permute-done.2.refs_3_
  12.5 2.2 %collective-permute-done.1.refs_2_ = f32[512,128]{1,0:T(8,128)S(1)} collective-permute-done((f32[512,128]{1,0:T(8,128)S(1)}, f32[512,128]{1,0:T(8,128)S(1)}, u32[]{:S(2)}, u32[]{:S(2)}) %collective-permute-start.1) | collective-permute-done | bytes 262176 | tf_op jit(solution)/shard_map/ppermute | solution.py:464
  14.7 5.6 %layers.1 = (f32[320,128]{1,0:T(8,128)S(1)}, f32[352,128]{1,0:T(8,128)S(1)}, f32[544,128]{1,0:T(8,128)S(1)}) custom-call(f32[1024,128]{1,0:T(8,128)S(1)} %get-tuple-element.23.local.refs_0_, f32[1024,128]{1,0:T(8,128)S(1)} %collective-permute-done.sibling.refs_1_, f32[512,128]{1,0:T(8,128)S(1)} %collective-permute-done.1.refs_2_, ...), custom_call_target="tpu_custom_call" | custom-call | tf_op jit(solution)/shard_map/layers/pallas_call | solution.py:471
  20.3 0.1 collective-permute-start.4
  20.4 1.5 %collective-permute-done.4 = f32[544,128]{1,0:T(8,128)S(1)} collective-permute-done((f32[544,128]{1,0:T(8,128)S(1)}, f32[544,128]{1,0:T(8,128)S(1)}, u32[]{:S(2)}, u32[]{:S(2)}) %collective-permute-start.4) | collective-permute-done | bytes 278560 | tf_op jit(solution)/shard_map/ppermute | solution.py:382
  21.9 3.5 %collective-permute-start.7 = (f32[88,128]{1,0:T(8,128)S(1)}, f32[88,128]{1,0:T(8,128)S(1)}, u32[]{:S(2)}, u32[]{:S(2)}) collective-permute-start(f32[88,128]{1,0:T(8,128)S(1)} %get-tuple-element.42), channel_id=1, source_target_pairs={{0,5},{1,4},{2,7},{3,6},{4,1},{5,0},{6,3},{7,2},{8,13},{9,12},{10,... | collective-permute-start | bytes 135176 | tf_op jit(solution)/shard_map/ppermute | solution.py:382
  25.4 0.0 collective-permute-start.6
  25.4 0.6 %collective-permute-start.5 = (f32[88,128]{1,0:T(8,128)S(1)}, f32[88,128]{1,0:T(8,128)S(1)}, u32[]{:S(2)}, u32[]{:S(2)}) collective-permute-start(f32[88,128]{1,0:T(8,128)S(1)} %get-tuple-element.44), channel_id=1, source_target_pairs={{0,1},{1,0},{2,3},{3,2},{4,5},{5,4},{6,7},{7,6},{8,9},{9,8},{10,11... | collective-permute-start | bytes 135176 | tf_op jit(solution)/shard_map/ppermute | solution.py:382
  26.1 1.9 %collective-permute-start.11 = (f32[128,128]{1,0:T(8,128)S(1)}, f32[128,128]{1,0:T(8,128)S(1)}, u32[]{:S(2)}, u32[]{:S(2)}) collective-permute-start(f32[128,128]{1,0:T(8,128)S(1)} %slice.35), channel_id=1, source_target_pairs={{0,4},{2,0},{4,8},{6,2},{8,12},{10,6},{12,16},{14,10},{16,20},{18,... | collective-permute-start | bytes 196616 | tf_op jit(solution)/shard_map/ppermute | solution.py:486
  28.0 0.0 collective-permute-done.7
  28.0 1.5 %collective-permute-done.6 = f32[88,128]{1,0:T(8,128)S(1)} collective-permute-done((f32[88,128]{1,0:T(8,128)S(1)}, f32[88,128]{1,0:T(8,128)S(1)}, u32[]{:S(2)}, u32[]{:S(2)}) %collective-permute-start.6) | collective-permute-done | bytes 45088 | tf_op jit(solution)/shard_map/ppermute | solution.py:382
  29.5 0.0 collective-permute-done.5
  29.6 2.8 %collective-permute-start.10 = (f32[88,128]{1,0:T(8,128)S(1)}, f32[88,128]{1,0:T(8,128)S(1)}, u32[]{:S(2)}, u32[]{:S(2)}) collective-permute-start(f32[88,128]{1,0:T(8,128)S(1)} %fusion), channel_id=1, source_target_pairs={{0,24},{1,25},{2,26},{3,27},{4,28},{5,29},{6,30},{7,31},{8,16},{9,... | collective-permute-start | bytes 135176 | tf_op jit(solution)/shard_map/ppermute | solution.py:382
  32.4 0.3 collective-permute-start.9
  32.7 1.4 %collective-permute-start.8 = (f32[88,128]{1,0:T(8,128)S(1)}, f32[88,128]{1,0:T(8,128)S(1)}, u32[]{:S(2)}, u32[]{:S(2)}) collective-permute-start(f32[88,128]{1,0:T(8,128)S(1)} %fusion), channel_id=1, source_target_pairs={{0,8},{1,9},{2,10},{3,11},{4,12},{5,13},{6,14},{7,15},{8,0},{9,1},... | collective-permute-start | bytes 135176 | tf_op jit(solution)/shard_map/ppermute | solution.py:382
  34.0 0.0 collective-permute-done.11.ringed
  34.0 1.3 %grad_input.1 = f32[256,128]{1,0:T(8,128)} custom-call(f32[320,128]{1,0:T(8,128)S(1)} %get-tuple-element.36.own, f32[192,128]{1,0:T(8,128)S(1)} %slice.34.swapped, f32[128,128]{1,0:T(8,128)S(1)} %collective-permute-done.11.ringed, bf16[384,1152]{1,0:T(8,128)(2,1)S(1)} %get-tuple-element.33.refs_6_.backward), custom_call_target="tpu_custom_call" | custom-call | flops 600000000 | bytes 1000000 | tf_op jit(solution)/shard_map/grad_input/pallas_call | solution.py:487
  35.3 0.2 collective-permute-done.10
  35.5 2.2 %collective-permute-done.9 = f32[88,128]{1,0:T(8,128)S(1)} collective-permute-done((f32[88,128]{1,0:T(8,128)S(1)}, f32[88,128]{1,0:T(8,128)S(1)}, u32[]{:S(2)}, u32[]{:S(2)}) %collective-permute-start.9) | collective-permute-done | bytes 45088 | tf_op jit(solution)/shard_map/ppermute | solution.py:382
  37.6 0.0 collective-permute-done.8
  37.7 1.1 %collective-permute-start.14 = (f32[88,128]{1,0:T(8,128)S(1)}, f32[88,128]{1,0:T(8,128)S(1)}, u32[]{:S(2)}, u32[]{:S(2)}) collective-permute-start(f32[88,128]{1,0:T(8,128)S(1)} %add_add_fusion), channel_id=1, source_target_pairs={{0,5},{1,4},{2,7},{3,6},{4,1},{5,0},{6,3},{7,2},{8,13},{9,12},{10,... | collective-permute-start | bytes 135176 | tf_op jit(solution)/shard_map/ppermute | solution.py:382
  38.7 1.3 %collective-permute-start.13 = (f32[88,128]{1,0:T(8,128)S(1)}, f32[88,128]{1,0:T(8,128)S(1)}, u32[]{:S(2)}, u32[]{:S(2)}) collective-permute-start(f32[88,128]{1,0:T(8,128)S(1)} %add_add_fusion), channel_id=1, source_target_pairs={{0,4},{1,5},{2,6},{3,7},{4,0},{5,1},{6,2},{7,3},{8,12},{9,13},{10,... | collective-permute-start | bytes 135176 | tf_op jit(solution)/shard_map/ppermute | solution.py:382
  40.0 1.2 %collective-permute-start.12 = (f32[88,128]{1,0:T(8,128)S(1)}, f32[88,128]{1,0:T(8,128)S(1)}, u32[]{:S(2)}, u32[]{:S(2)}) collective-permute-start(f32[88,128]{1,0:T(8,128)S(1)} %add_add_fusion), channel_id=1, source_target_pairs={{0,1},{1,0},{2,3},{3,2},{4,5},{5,4},{6,7},{7,6},{8,9},{9,8},{10,11... | collective-permute-start | bytes 135176 | tf_op jit(solution)/shard_map/ppermute | solution.py:382
  41.2 2.9 %collective-permute-done.12 = f32[88,128]{1,0:T(8,128)S(1)} collective-permute-done((f32[88,128]{1,0:T(8,128)S(1)}, f32[88,128]{1,0:T(8,128)S(1)}, u32[]{:S(2)}, u32[]{:S(2)}) %collective-permute-start.12) | collective-permute-done | bytes 45088 | tf_op jit(solution)/shard_map/ppermute | solution.py:382
  44.1 0.0 collective-permute-done.13
  44.1 0.0 collective-permute-done.14
  44.1 0.1 collective-permute-start.15
  44.2 1.4 %collective-permute-done.15.other = f32[352,128]{1,0:T(8,128)S(1)} collective-permute-done((f32[352,128]{1,0:T(8,128)S(1)}, f32[352,128]{1,0:T(8,128)S(1)}, u32[]{:S(2)}, u32[]{:S(2)}) %collective-permute-start.15) | collective-permute-done | bytes 180256 | tf_op jit(solution)/shard_map/ppermute | solution.py:382
  45.6 1.2 %unpack.1 = (f32[27,32,32]{2,1,0:T(8,128)}, f32[27,32,32]{2,1,0:T(8,128)}, f32[27,32,32]{2,1,0:T(8,128)}) custom-call(f32[352,128]{1,0:T(8,128)S(1)} %constant_dynamic-update-slice_fusion.mine, f32[352,128]{1,0:T(8,128)S(1)} %collective-permute-done.15.other), custom_call_target="tpu_custom_call" | custom-call | tf_op jit(solution)/shard_map/unpack/pallas_call | solution.py:499
  (10 shorter events, 0.1 us)
Async XLA Ops:
  2.2 2.2 %collective-permute-start = (f32[1024,128]{1,0:T(8,128)S(1)}, f32[1024,128]{1,0:T(8,128)S(1)}, u32[]{:S(2)}, u32[]{:S(2)}) collective-permute-start(f32[1024,128]{1,0:T(8,128)S(1)} %get-tuple-element.23.local.refs_0_), channel_id=1, source_target_pairs={{0,2},{2,0},{4,6},{6,4},{8,10},{10,8},{12,14},{14,12},{16,18},{18,... | collective-permute-start | bytes 1572872 | tf_op jit(solution)/shard_map/ppermute | solution.py:427
  4.5 10.2 %collective-permute-start.1 = (f32[512,128]{1,0:T(8,128)S(1)}, f32[512,128]{1,0:T(8,128)S(1)}, u32[]{:S(2)}, u32[]{:S(2)}) collective-permute-start(f32[512,128]{1,0:T(8,128)S(1)} %pack_rows.1), channel_id=1, source_target_pairs={{0,4},{2,0},{4,8},{6,2},{8,12},{10,6},{12,16},{14,10},{16,20},{18,... | collective-permute-start | bytes 786440 | tf_op jit(solution)/shard_map/ppermute | solution.py:464
  7.6 4.9 %collective-permute-start.2 = (f32[128,128]{1,0:T(8,128)S(1)}, f32[128,128]{1,0:T(8,128)S(1)}, u32[]{:S(2)}, u32[]{:S(2)}) collective-permute-start(f32[128,128]{1,0:T(8,128)S(1)} %get-tuple-element.30), channel_id=1, source_target_pairs={{0,1},{1,0},{2,3},{3,2},{4,5},{5,4},{6,7},{7,6},{8,9},{9,8},{10,11... | collective-permute-start | bytes 196616 | tf_op jit(solution)/shard_map/ppermute | solution.py:466
  9.2 3.3 %collective-permute-start.3 = (f32[64,128]{1,0:T(8,128)S(1)}, f32[64,128]{1,0:T(8,128)S(1)}, u32[]{:S(2)}, u32[]{:S(2)}) collective-permute-start(f32[64,128]{1,0:T(8,128)S(1)} %get-tuple-element.31), channel_id=1, source_target_pairs={{0,5},{1,4},{2,1},{3,0},{4,9},{5,8},{6,3},{7,2},{8,13},{9,12},{10,... | collective-permute-start | bytes 98312 | tf_op jit(solution)/shard_map/ppermute | solution.py:465
  20.3 1.6 %collective-permute-start.4 = (f32[544,128]{1,0:T(8,128)S(1)}, f32[544,128]{1,0:T(8,128)S(1)}, u32[]{:S(2)}, u32[]{:S(2)}) collective-permute-start(f32[544,128]{1,0:T(8,128)S(1)} %get-tuple-element.35), channel_id=1, source_target_pairs={{0,2},{1,3},{2,0},{3,1},{4,6},{5,7},{6,4},{7,5},{8,10},{9,11},{10,... | collective-permute-start | bytes 835592 | tf_op jit(solution)/shard_map/ppermute | solution.py:382
  21.9 6.1 %collective-permute-start.7 = (f32[88,128]{1,0:T(8,128)S(1)}, f32[88,128]{1,0:T(8,128)S(1)}, u32[]{:S(2)}, u32[]{:S(2)}) collective-permute-start(f32[88,128]{1,0:T(8,128)S(1)} %get-tuple-element.42), channel_id=1, source_target_pairs={{0,5},{1,4},{2,7},{3,6},{4,1},{5,0},{6,3},{7,2},{8,13},{9,12},{10,... | collective-permute-start | bytes 135176 | tf_op jit(solution)/shard_map/ppermute | solution.py:382
  25.4 4.1 %collective-permute-start.6 = (f32[88,128]{1,0:T(8,128)S(1)}, f32[88,128]{1,0:T(8,128)S(1)}, u32[]{:S(2)}, u32[]{:S(2)}) collective-permute-start(f32[88,128]{1,0:T(8,128)S(1)} %get-tuple-element.43), channel_id=1, source_target_pairs={{0,4},{1,5},{2,6},{3,7},{4,0},{5,1},{6,2},{7,3},{8,12},{9,13},{10,... | collective-permute-start | bytes 135176 | tf_op jit(solution)/shard_map/ppermute | solution.py:382
  25.4 4.1 %collective-permute-start.5 = (f32[88,128]{1,0:T(8,128)S(1)}, f32[88,128]{1,0:T(8,128)S(1)}, u32[]{:S(2)}, u32[]{:S(2)}) collective-permute-start(f32[88,128]{1,0:T(8,128)S(1)} %get-tuple-element.44), channel_id=1, source_target_pairs={{0,1},{1,0},{2,3},{3,2},{4,5},{5,4},{6,7},{7,6},{8,9},{9,8},{10,11... | collective-permute-start | bytes 135176 | tf_op jit(solution)/shard_map/ppermute | solution.py:382
  26.1 7.9 %collective-permute-start.11 = (f32[128,128]{1,0:T(8,128)S(1)}, f32[128,128]{1,0:T(8,128)S(1)}, u32[]{:S(2)}, u32[]{:S(2)}) collective-permute-start(f32[128,128]{1,0:T(8,128)S(1)} %slice.35), channel_id=1, source_target_pairs={{0,4},{2,0},{4,8},{6,2},{8,12},{10,6},{12,16},{14,10},{16,20},{18,... | collective-permute-start | bytes 196616 | tf_op jit(solution)/shard_map/ppermute | solution.py:486
  29.6 5.9 %collective-permute-start.10 = (f32[88,128]{1,0:T(8,128)S(1)}, f32[88,128]{1,0:T(8,128)S(1)}, u32[]{:S(2)}, u32[]{:S(2)}) collective-permute-start(f32[88,128]{1,0:T(8,128)S(1)} %fusion), channel_id=1, source_target_pairs={{0,24},{1,25},{2,26},{3,27},{4,28},{5,29},{6,30},{7,31},{8,16},{9,... | collective-permute-start | bytes 135176 | tf_op jit(solution)/shard_map/ppermute | solution.py:382
  32.4 5.2 %collective-permute-start.9 = (f32[88,128]{1,0:T(8,128)S(1)}, f32[88,128]{1,0:T(8,128)S(1)}, u32[]{:S(2)}, u32[]{:S(2)}) collective-permute-start(f32[88,128]{1,0:T(8,128)S(1)} %fusion), channel_id=1, source_target_pairs={{0,16},{1,17},{2,18},{3,19},{4,20},{5,21},{6,22},{7,23},{8,24},{9,... | collective-permute-start | bytes 135176 | tf_op jit(solution)/shard_map/ppermute | solution.py:382
  32.7 5.0 %collective-permute-start.8 = (f32[88,128]{1,0:T(8,128)S(1)}, f32[88,128]{1,0:T(8,128)S(1)}, u32[]{:S(2)}, u32[]{:S(2)}) collective-permute-start(f32[88,128]{1,0:T(8,128)S(1)} %fusion), channel_id=1, source_target_pairs={{0,8},{1,9},{2,10},{3,11},{4,12},{5,13},{6,14},{7,15},{8,0},{9,1},... | collective-permute-start | bytes 135176 | tf_op jit(solution)/shard_map/ppermute | solution.py:382
  37.7 6.4 %collective-permute-start.14 = (f32[88,128]{1,0:T(8,128)S(1)}, f32[88,128]{1,0:T(8,128)S(1)}, u32[]{:S(2)}, u32[]{:S(2)}) collective-permute-start(f32[88,128]{1,0:T(8,128)S(1)} %add_add_fusion), channel_id=1, source_target_pairs={{0,5},{1,4},{2,7},{3,6},{4,1},{5,0},{6,3},{7,2},{8,13},{9,12},{10,... | collective-permute-start | bytes 135176 | tf_op jit(solution)/shard_map/ppermute | solution.py:382
  38.7 5.4 %collective-permute-start.13 = (f32[88,128]{1,0:T(8,128)S(1)}, f32[88,128]{1,0:T(8,128)S(1)}, u32[]{:S(2)}, u32[]{:S(2)}) collective-permute-start(f32[88,128]{1,0:T(8,128)S(1)} %add_add_fusion), channel_id=1, source_target_pairs={{0,4},{1,5},{2,6},{3,7},{4,0},{5,1},{6,2},{7,3},{8,12},{9,13},{10,... | collective-permute-start | bytes 135176 | tf_op jit(solution)/shard_map/ppermute | solution.py:382
  40.0 4.0 %collective-permute-start.12 = (f32[88,128]{1,0:T(8,128)S(1)}, f32[88,128]{1,0:T(8,128)S(1)}, u32[]{:S(2)}, u32[]{:S(2)}) collective-permute-start(f32[88,128]{1,0:T(8,128)S(1)} %add_add_fusion), channel_id=1, source_target_pairs={{0,1},{1,0},{2,3},{3,2},{4,5},{5,4},{6,7},{7,6},{8,9},{9,8},{10,11... | collective-permute-start | bytes 135176 | tf_op jit(solution)/shard_map/ppermute | solution.py:382
  44.1 1.5 %collective-permute-start.15 = (f32[352,128]{1,0:T(8,128)S(1)}, f32[352,128]{1,0:T(8,128)S(1)}, u32[]{:S(2)}, u32[]{:S(2)}) collective-permute-start(f32[352,128]{1,0:T(8,128)S(1)} %constant_dynamic-update-slice_fusion.mine), channel_id=1, source_target_pairs={{0,2},{1,3},{2,0},{3,1},{4,6},{5,7},{6,4},{7,5},{8,10},{9,11},{10,... | collective-permute-start | bytes 540680 | tf_op jit(solution)/shard_map/ppermute | solution.py:382

commit v5 on v4

--- a/solution.py
+++ b/solution.py
@@ -32,6 +32,8 @@
 
 
 def roll(value, shift):
+    if not isinstance(shift, int):
+        return pltpu.roll(value, lax.rem(shift + LANES, LANES), 1)
     shift %= LANES
     return pltpu.roll(value, shift, 1) if shift else value
 
@@ -150,30 +152,74 @@
     return out
 
 
-def store_shifted(main, side, into, into_side=None):
-    planes = side.shape[0]
-    lane = lane_index(planes)
-    ahead, behind = side, side
-
-    def store(target, c, lanes, value):
-        high, low = split(value)
-        target[pl.ds(c * LANES, planes), lanes] = high
-        target[pl.ds(c * LANES + planes, planes), lanes] = low
-
-    for e, value in main.items():
-        base = e * SIDE
+def store_split(target, c, lanes, value):
+    planes = value.shape[0]
+    high, low = split(value)
+    target[pl.ds(c * LANES, planes), lanes] = high
+    target[pl.ds(c * LANES + planes, planes), lanes] = low
+
+
+def shift_rows(main, side, into, edges=None):
+    lane = lane_index(side.shape[0])
+    for e, value in main:
+        base, start = e * SIDE, e * LANES
+        if not isinstance(e, int):
+            start = pl.multiple_of(start, LANES)
         ends = roll(side, -base)
         down = roll(jnp.where(lane == LANES - 1, ends, value), 1)
         up = roll(jnp.where(lane == 0, ends, value), -1)
         for c, shifted in enumerate((down, value, up)):
-            store(into, c, pl.ds(e * LANES, LANES), shifted)
-        if into_side is not None:
-            value = roll(value, base)
-            ahead = jnp.where(lane == base, value, ahead)
-            behind = jnp.where(lane == (base - 1) % LANES, value, behind)
-    if into_side is not None:
-        for c, shifted in enumerate((roll(behind, 1), side, roll(ahead, -1))):
-            store(into_side, c, pl.ds(0, LANES), shifted)
+            store_split(into, c, pl.ds(start, LANES), shifted)
+        if edges is not None:
+            edges = jnp.where((lane == base) | (lane == base - 1), roll(value, base), edges)
+    return edges
+
+
+def shift_side(side, edges, into):
+    place = lax.rem(lane_index(side.shape[0]), SIDE)
+    ahead = roll(jnp.where(place == 0, edges, side), -1)
+    behind = roll(jnp.where(place == SIDE - 1, edges, side), 1)
+    for c, shifted in enumerate((behind, side, ahead)):
+        store_split(into, c, pl.ds(0, LANES), shifted)
+
+
+def side_strips(got, y_odd):
+    zero = jnp.zeros_like(got[0])
+    got = (got + [zero])[:2]
+    from_right = jnp.where(y_odd, got[1], got[0])
+    from_left = jnp.where(y_odd, got[0], got[1])
+    return jnp.where(lax.rem(lane_index(zero.shape[0]), SIDE) >= HALO, from_right, from_left)
+
+
+def field_side(f, rows, before, own, after):
+    lane = lane_index(own.shape[0])
+    span, lead = rows * SIDE, HALO * SIDE - HALO
+    before = roll(before, lead - span - f * span)
+    after = roll(after, lead + span - f * span)
+    side = jnp.where(lane < lead + span, roll(own, lead - f * span), after)
+    side = jnp.where(lane < lead, before, side)
+    return jnp.where(lane < lead + 2 * span, side, 0.0)
+
+
+INPUTS = (0, 2, 3)
+
+
+def early_kernel(depth, rows, *refs):
+    local, sibling, *strips = refs[: -2 * LAYERS]
+    shifted, edges = refs[-2 * LAYERS : -LAYERS], refs[-LAYERS:]
+    planes = local.shape[0] // (4 * rows)
+    odd = lax.rem(lax.axis_index("gx"), 2)
+    y_odd = lax.rem(lax.axis_index("gy"), 2) == 1
+    own, inner = (side_strips([v[pl.ds(k * planes, planes), :] for v in strips], y_odd) for k in range(2))
+    for layer, f in enumerate(INPUTS):
+        width = WIDTHS[f]
+        side = field_side(f, rows, inner, own, inner)
+        main = [(HALO + r, slab_at(local, f, depth, rows, r)) for r in range(rows)]
+        for j in range(width):
+            e = odd * (HALO - width) + (1 - odd) * (HALO + rows) + j
+            main.append((e, slab_at(sibling, f, depth, rows, (rows - width) * odd + j)))
+        zero = jnp.zeros((planes, LANES), F32)
+        edges[layer][...] = shift_rows(main, side, shifted[layer], zero)
 
 
 def conv_side(weights, layer, shifted):
@@ -187,9 +233,16 @@
 
 
 def layers_kernel(depth, rows, channels, gy_rounds, factor, *refs):
-    local, sibling, outer = refs[:3]
-    strips = refs[3 : 3 + 2 * gy_rounds]
-    forward, backward, h_out, keep, send, xs, xside, hs, hside, gsum = refs[3 + 2 * gy_rounds :]
+    refs = list(refs)
+    take = lambda count: [refs.pop(0) for _ in range(count)]
+    local, sibling, outer = take(3)
+    strips, corners = take(gy_rounds), take(gy_rounds)
+    forward, backward = take(2)
+    early_edges = take(LAYERS)
+    take(LAYERS)
+    h_out, keep, send = take(3)
+    shifted = take(LAYERS)
+    xside, hs, hside, gsum = refs
     planes = depth * channels
     gx, gy = lax.axis_index("gx"), lax.axis_index("gy")
     gx_size, gy_size = lax.axis_size("gx"), lax.axis_size("gy")
@@ -197,47 +250,26 @@
     odd = lax.rem(gx, 2)
     ended = (gx == 0) | (gx == gx_size - 1)
     lane = lane_index(planes)
-    right = lax.rem(lane, SIDE) >= HALO
-    zero = jnp.zeros((planes, LANES), F32)
-
-    def side_strip(group):
-        got = []
-        for r in range(gy_rounds):
-            if group < 2:
-                got.append(strips[r][pl.ds(group * planes, planes), :])
-            else:
-                got.append(jnp.where(ended, 0.0, strips[gy_rounds + r][...]))
-        if gy_rounds == 0:
-            return zero
-        if gy_rounds == 1:
-            got.append(zero)
-        from_right = jnp.where(y_odd, got[1], got[0])
-        from_left = jnp.where(y_odd, got[0], got[1])
-        return jnp.where(right, from_right, from_left)
-
-    own_strip, inner_strip, outer_strip = (side_strip(g) for g in range(3))
-    before_strip = jnp.where(x_odd, inner_strip, outer_strip)
-    after_strip = jnp.where(x_odd, outer_strip, inner_strip)
-    span = rows * SIDE
-
-    def field_parts(f):
+
+    own, inner = (side_strips([v[pl.ds(k * planes, planes), :] for v in strips], y_odd) for k in range(2))
+    corner = jnp.where(ended, 0.0, side_strips([v[...] for v in corners], y_odd))
+    before, after = jnp.where(x_odd, inner, corner), jnp.where(x_odd, corner, inner)
+
+    def outer_row(f, j):
+        value = outer[pl.ds((STARTS[f] + j) * planes, planes), :]
+        return jnp.where(ended, 0.0, value)
+
+    def cotangent_rows():
+        f, main = 1, {}
         width = WIDTHS[f]
-        main = {}
         for j in range(width):
-            start = STARTS[f] + j
             a = slab_at(sibling, f, depth, rows, (rows - width) * odd + j)
-            b = jnp.where(ended, 0.0, outer[pl.ds(start * planes, planes), :])
+            b = outer_row(f, j)
             main[HALO - width + j] = jnp.where(x_odd, a, b)
             main[HALO + rows + j] = jnp.where(x_odd, b, a)
         for r in range(rows):
             main[HALO + r] = slab_at(local, f, depth, rows, r)
-        lead = HALO * SIDE - HALO
-        before = roll(before_strip, lead - span - f * span)
-        own = roll(own_strip, lead - f * span)
-        after = roll(after_strip, lead + span - f * span)
-        side = jnp.where(lane < lead, before, jnp.where(lane < lead + span, own, after))
-        side = jnp.where(lane < lead + 2 * span, side, 0.0)
-        return main, side
+        return main
 
     side_row = (lane + HALO) // SIDE
     right = lax.rem(lane + HALO, SIDE) >= HALO
@@ -249,11 +281,16 @@
     padding = gsum.shape[0] - LAYERS * 7 * channels
     if padding:
         gsum[pl.ds(LAYERS * 7 * channels, padding), :] = jnp.zeros((padding, LANES), F32)
-    grad_main, grad_side = field_parts(1)
+    grad_main, grad_side = cotangent_rows(), field_side(1, rows, before, own, after)
     half = lane_index(channels)
     for layer in range(LAYERS):
-        x_main, x_side = field_parts((0, 2, 3)[layer])
-        store_shifted(x_main, x_side, xs, xside)
+        f, xs = INPUTS[layer], shifted[layer]
+        x_side = field_side(f, rows, before, own, after)
+        x_main = []
+        for j in range(WIDTHS[f]):
+            e = (1 - odd) * (HALO - WIDTHS[f]) + odd * (HALO + rows) + j
+            x_main.append((e, outer_row(f, j)))
+        shift_side(x_side, shift_rows(x_main, x_side, xs, early_edges[layer][...]), xside)
         h_width = LAYERS - 1 - layer
         low, high = HALO - h_width, HALO + rows + h_width
         pre = conv_rows(forward, layer, xs, low, high)
@@ -267,16 +304,17 @@
             h_main[e] = value
         h_side = jnp.where(side_ok, grad_side * gelu_slope(conv_side(forward, layer, xside)), 0.0)
         if h_width:
-            store_shifted(h_main, h_side, hs, hside)
-            own = hs[pl.ds(LANES, 2 * planes), pl.ds(HALO * LANES, rows * LANES)]
+            edges = shift_rows(h_main.items(), h_side, hs, jnp.zeros((planes, LANES), F32))
+            shift_side(h_side, edges, hside)
+            center = hs[pl.ds(LANES, 2 * planes), pl.ds(HALO * LANES, rows * LANES)]
         else:
             parts = [split(h_main[HALO + r]) for r in range(rows)]
-            own = [jnp.concatenate([part[k] for part in parts], axis=1) for k in range(2)]
-            own = jnp.concatenate(own, axis=0)
+            center = [jnp.concatenate([part[k] for part in parts], axis=1) for k in range(2)]
+            center = jnp.concatenate(center, axis=0)
         tiles, extra = [], []
         for b in range(3):
             window = xs[:, pl.ds((HALO + b - 1) * LANES, rows * LANES)]
-            product = lax.dot_general(own, window, NT, preferred_element_type=F32)
+            product = lax.dot_general(center, window, NT, preferred_element_type=F32)
             product = product[:planes] + product[planes:]
             for c in range(3):
                 tile = product[:, c * LANES : (c + 1) * LANES]
@@ -334,7 +372,7 @@
     side = own[pl.ds(rows * planes, planes), :]
     lead = HALO * SIDE - HALO
     side = jnp.where(lane < lead, before, jnp.where(lane < lead + span, side, after))
-    store_shifted(main, side, hs)
+    shift_rows(main.items(), side, hs)
     grad_main = conv_rows(backward, LAYERS - 1, hs, HALO, HALO + rows)
     for r in range(rows):
         for z in range(depth):
@@ -463,24 +501,37 @@
 
     outer = lax.ppermute(outer, "gx", across)
     corners = [lax.ppermute(strip, ("gx", "gy"), diagonal(across, pairs)) for pairs in y_rounds]
-    strips = [lax.ppermute(strips, "gy", pairs) for pairs in y_rounds] + corners
+    strips = [lax.ppermute(strips, "gy", pairs) for pairs in y_rounds]
 
     tiles = -(-LAYERS * 7 * channels // 64) * 64
     span = (2 * HALO + rows) * LANES
     shifted, shifted_side = pltpu.VMEM((3 * LANES, span), BF16), pltpu.VMEM((3 * LANES, LANES), BF16)
-    h_own, keep, send = pl.pallas_call(
+    early = pl.pallas_call(
+        functools.partial(early_kernel, depth, rows),
+        out_shape=[shifted] * LAYERS + [pltpu.VMEM((planes, LANES), F32)] * LAYERS,
+        in_specs=vmem(2 + len(strips)),
+        out_specs=vmem(2 * LAYERS),
+        compiler_params=room(12),
+        cost_estimate=pl.CostEstimate(flops=20_000_000, bytes_accessed=6_000_000, transcendentals=0),
+        name="early",
+    )(*(near(v) for v in (local, sibling, *strips)))
+    operands = [local, sibling, outer, *strips, *corners, forward, backward, *early[LAYERS:]]
+    count = len(operands)
+    h_own, keep, send, *_ = pl.pallas_call(
         functools.partial(layers_kernel, depth, rows, channels, len(y_rounds), factor),
         out_shape=[
             pltpu.VMEM(((rows + 1) * planes, LANES), F32),
             pltpu.VMEM((tiles // 2, LANES), F32),
             pltpu.VMEM((tiles // 2 + 3 * planes, LANES), F32),
-        ],
-        in_specs=vmem(5 + len(strips)),
-        out_specs=vmem(3),
-        scratch_shapes=[shifted, shifted_side] * 2 + [pltpu.VMEM((tiles, LANES), F32)],
+        ]
+        + [shifted] * LAYERS,
+        in_specs=vmem(count + LAYERS),
+        out_specs=vmem(3 + LAYERS),
+        input_output_aliases={count + k: 3 + k for k in range(LAYERS)},
+        scratch_shapes=[shifted_side, shifted, shifted_side, pltpu.VMEM((tiles, LANES), F32)],
         compiler_params=room(16),
         name="layers",
-    )(*(near(v) for v in (local, sibling, outer, *strips, forward, backward)))
+    )(*(near(v) for v in operands + list(early[:LAYERS])))
 
     def input_gradient(swapped):
         ringed = lax.ppermute(swapped[planes:], "gx", across)

time: 47 us -> 46.1 us (0.981)
  waiting for transfers between devices: 13.7 us -> 12 us
  Pallas kernels: 11.7 us -> 12.5 us
    ppermute x1, waiting for transfers between devices: 1.85 us -> 0.01 us  [per_device(): lax.ppermute(strip, ('gx', 'gy'), diagonal(across, pairs))]
    pallas_call x0 -> x1, Pallas kernels: none -> 1.69 us  [per_device(): pl.pallas_call(functools.partial(early_kernel, depth, rows), out_shape=[s...]
    ppermute x1, waiting for transfers between devices: 0.01 us -> 1.28 us  [per_device(): strips = [lax.ppermute(strips, 'gy', pairs) for pairs in y_rounds]]
    ppermute x1, waiting for transfers between devices: 2.16 us -> 1.02 us  [per_device(): outer = lax.ppermute(outer, 'gx', across)]
    pallas_call x1, Pallas kernels: 5.56 us -> 4.64 us  [per_device(): pl.pallas_call(functools.partial(layers_kernel, depth, rows, channels, le...]
  transfers between devices with their start and end apart: 16 -> 16, of which waited for: 8 -> 8; matrix products, arithmetic and copies ran while one was open for 0% -> 0% of each run, Pallas kernels for 7% -> 11%
where the time goes in v5:
time: 46.1 us; the launch traced here: 45.9 us
  starting transfers between devices  20.6 us (45%)
  Pallas kernels  12.5 us (27%)
  waiting for transfers between devices  12 us (26%)
  between operations  0.77 us (2%)
    ppermute x11, starting transfers between devices, swap(): return lax.ppermute(value, axes, [(i, i ^ bits) for i in range(total)])  12.3 us
    ppermute x11, waiting for transfers between devices, swap(): return lax.ppermute(value, axes, [(i, i ^ bits) for i in range(total)])  9.69 us
    pallas_call x1, Pallas kernels, per_device(): pl.pallas_call(functools.partial(layers_kernel, depth, rows, channels, le...  4.64 us
    ppermute x1, starting transfers between devices, per_device(): outer = lax.ppermute(outer, 'gx', across)  2.82 us
    ppermute x1, starting transfers between devices, input_gradient(): ringed = lax.ppermute(swapped[planes:], 'gx', across)  1.91 us
    pallas_call x1, Pallas kernels, per_device(): pl.pallas_call(functools.partial(early_kernel, depth, rows), out_shape=[s...  1.69 us
    pallas_call x1, Pallas kernels, per_device(): pl.pallas_call(functools.partial(weight_kernel, channels, depth), out_sha...  1.63 us
    pallas_call x1, Pallas kernels, per_device(): pl.pallas_call(fetch_kernel, out_shape=[pltpu.VMEM((4 * size, cols), F32)...  1.6 us
  transfers between devices with their start and end apart: 16, of which 8 were waited for; matrix products, arithmetic and copies ran while one was open for 0% of the time, Pallas kernels for 11%

profile of v5, /device:TPU:0, one launch (start us, length us, event | category | flops | bytes accessed | tf_op | source)
XLA Modules:
  0.0 45.9 jit_solution(7309998160461828769)
XLA Ops:
  0.6 1.6 %fetch.1 = (f32[1024,128]{1,0:T(8,128)S(1)}, f32[27,32,32]{2,1,0:T(8,128)S(1)}, f32[27,32,32]{2,1,0:T(8,128)S(1)}, f32[27,32,32]{2,1,0:T(8,128)S(1)}) custom-call(f32[256,128]{1,0:T(8,128)} %bitcast.5, f32[256,128]{1,0:T(8,128)} %bitcast.6, f32[256,128]{1,0:T(8,128)} %bitcast.7, f32[256,128]{1,0:T(8,128)} %bitcast.8, f32[27,32,32]{2,1,0:T(8,128)} %refs_4_.1, ...), custom_call_target="tpu_custom_call" | custom-call | tf_op jit(solution)/shard_map/fetch/pallas_call | solution.py:455
  2.2 0.5 %collective-permute-start = (f32[1024,128]{1,0:T(8,128)S(1)}, f32[1024,128]{1,0:T(8,128)S(1)}, u32[]{:S(2)}, u32[]{:S(2)}) collective-permute-start(f32[1024,128]{1,0:T(8,128)S(1)} %get-tuple-element.29.local.refs_0_), channel_id=1, source_target_pairs={{0,2},{2,0},{4,6},{6,4},{8,10},{10,8},{12,14},{14,12},{16,18},{18,... | collective-permute-start | bytes 1572872 | tf_op jit(solution)/shard_map/ppermute | solution.py:465
  2.8 1.6 %weights.1 = (bf16[384,1152]{1,0:T(8,128)(2,1)S(1)}, bf16[384,1152]{1,0:T(8,128)(2,1)S(1)}) custom-call(f32[27,32,32]{2,1,0:T(8,128)S(1)} %get-tuple-element.30.refs_0_, f32[27,32,32]{2,1,0:T(8,128)S(1)} %get-tuple-element.31.refs_1_, f32[27,32,32]{2,1,0:T(8,128)S(1)} %get-tuple-element.32.refs_2_), custom_call_target="tpu_custom_call" | custom-call | flops 20000000 | bytes 4000000 | tf_op jit(solution)/shard_map/weights/pallas_call | solution.py:470
  4.4 0.0 collective-permute-done.sibling.refs_1_
  4.4 0.1 pack_rows.1
  4.5 2.8 %collective-permute-start.1 = (f32[512,128]{1,0:T(8,128)S(1)}, f32[512,128]{1,0:T(8,128)S(1)}, u32[]{:S(2)}, u32[]{:S(2)}) collective-permute-start(f32[512,128]{1,0:T(8,128)S(1)} %pack_rows.1), channel_id=1, source_target_pairs={{0,4},{2,0},{4,8},{6,2},{8,12},{10,6},{12,16},{14,10},{16,20},{18,... | collective-permute-start | bytes 786440 | tf_op jit(solution)/shard_map/ppermute | solution.py:502
  7.3 0.3 pack_strips.1
  7.6 1.6 %collective-permute-start.2 = (f32[128,128]{1,0:T(8,128)S(1)}, f32[128,128]{1,0:T(8,128)S(1)}, u32[]{:S(2)}, u32[]{:S(2)}) collective-permute-start(f32[128,128]{1,0:T(8,128)S(1)} %get-tuple-element.36), channel_id=1, source_target_pairs={{0,1},{1,0},{2,3},{3,2},{4,5},{5,4},{6,7},{7,6},{8,9},{9,8},{10,11... | collective-permute-start | bytes 196616 | tf_op jit(solution)/shard_map/ppermute | solution.py:504
  9.2 1.5 %collective-permute-start.3 = (f32[64,128]{1,0:T(8,128)S(1)}, f32[64,128]{1,0:T(8,128)S(1)}, u32[]{:S(2)}, u32[]{:S(2)}) collective-permute-start(f32[64,128]{1,0:T(8,128)S(1)} %get-tuple-element.37), channel_id=1, source_target_pairs={{0,5},{1,4},{2,1},{3,0},{4,9},{5,8},{6,3},{7,2},{8,13},{9,12},{10,... | collective-permute-start | bytes 98312 | tf_op jit(solution)/shard_map/ppermute | solution.py:503
  10.7 1.3 %collective-permute-done.2.refs_2_.refs_3_ = f32[128,128]{1,0:T(8,128)S(1)} collective-permute-done((f32[128,128]{1,0:T(8,128)S(1)}, f32[128,128]{1,0:T(8,128)S(1)}, u32[]{:S(2)}, u32[]{:S(2)}) %collective-permute-start.2) | collective-permute-done | bytes 65568 | tf_op jit(solution)/shard_map/ppermute | solution.py:504
  12.0 1.7 %early.1 = (bf16[384,1536]{1,0:T(8,128)(2,1)S(1)}, bf16[384,1536]{1,0:T(8,128)(2,1)S(1)}, bf16[384,1536]{1,0:T(8,128)(2,1)S(1)}, f32[64,128]{1,0:T(8,128)S(1)}, ...) custom-call(f32[1024,128]{1,0:T(8,128)S(1)} %get-tuple-element.29.local.refs_0_, ...), custom_call_target="tpu_custom_call" | custom-call | flops 20000000 | bytes 6000000 | tf_op jit(solution)/shard_map/early/pallas_call | solution.py:509
  13.7 0.0 collective-permute-done.3.refs_4_
  13.7 1.0 %collective-permute-done.1.refs_2_ = f32[512,128]{1,0:T(8,128)S(1)} collective-permute-done((f32[512,128]{1,0:T(8,128)S(1)}, f32[512,128]{1,0:T(8,128)S(1)}, u32[]{:S(2)}, u32[]{:S(2)}) %collective-permute-start.1) | collective-permute-done | bytes 262176 | tf_op jit(solution)/shard_map/ppermute | solution.py:502
  14.7 4.6 %layers.1 = (f32[320,128]{1,0:T(8,128)S(1)}, f32[352,128]{1,0:T(8,128)S(1)}, f32[544,128]{1,0:T(8,128)S(1)}, bf16[384,1536]{1,0:T(8,128)(2,1)S(1)}, bf16[384,153...) custom-call(f32[1024,128]{1,0:T(8,128)S(1)} %get-tuple-element.29.lo, ...), custom_call_target="tpu_custom_call", output_to_operand_aliasing={{3}: (10, {}), {4}: (11, {}), {5}: (12, {})} | custom-call | tf_op jit(solution)/shard_map/layers/pallas_call | solution.py:520
  19.4 0.1 collective-permute-start.4
  19.4 1.5 %collective-permute-done.4 = f32[544,128]{1,0:T(8,128)S(1)} collective-permute-done((f32[544,128]{1,0:T(8,128)S(1)}, f32[544,128]{1,0:T(8,128)S(1)}, u32[]{:S(2)}, u32[]{:S(2)}) %collective-permute-start.4) | collective-permute-done | bytes 278560 | tf_op jit(solution)/shard_map/ppermute | solution.py:420
  21.0 3.5 %collective-permute-start.7 = (f32[88,128]{1,0:T(8,128)S(1)}, f32[88,128]{1,0:T(8,128)S(1)}, u32[]{:S(2)}, u32[]{:S(2)}) collective-permute-start(f32[88,128]{1,0:T(8,128)S(1)} %get-tuple-element.54), channel_id=1, source_target_pairs={{0,5},{1,4},{2,7},{3,6},{4,1},{5,0},{6,3},{7,2},{8,13},{9,12},{10,... | collective-permute-start | bytes 135176 | tf_op jit(solution)/shard_map/ppermute | solution.py:420
  24.5 0.0 collective-permute-start.6
  24.5 0.6 %collective-permute-start.5 = (f32[88,128]{1,0:T(8,128)S(1)}, f32[88,128]{1,0:T(8,128)S(1)}, u32[]{:S(2)}, u32[]{:S(2)}) collective-permute-start(f32[88,128]{1,0:T(8,128)S(1)} %get-tuple-element.56), channel_id=1, source_target_pairs={{0,1},{1,0},{2,3},{3,2},{4,5},{5,4},{6,7},{7,6},{8,9},{9,8},{10,11... | collective-permute-start | bytes 135176 | tf_op jit(solution)/shard_map/ppermute | solution.py:420
  25.1 1.9 %collective-permute-start.11 = (f32[128,128]{1,0:T(8,128)S(1)}, f32[128,128]{1,0:T(8,128)S(1)}, u32[]{:S(2)}, u32[]{:S(2)}) collective-permute-start(f32[128,128]{1,0:T(8,128)S(1)} %slice.35), channel_id=1, source_target_pairs={{0,4},{2,0},{4,8},{6,2},{8,12},{10,6},{12,16},{14,10},{16,20},{18,... | collective-permute-start | bytes 196616 | tf_op jit(solution)/shard_map/ppermute | solution.py:537
  27.1 0.0 collective-permute-done.7
  27.1 1.5 %collective-permute-done.6 = f32[88,128]{1,0:T(8,128)S(1)} collective-permute-done((f32[88,128]{1,0:T(8,128)S(1)}, f32[88,128]{1,0:T(8,128)S(1)}, u32[]{:S(2)}, u32[]{:S(2)}) %collective-permute-start.6) | collective-permute-done | bytes 45088 | tf_op jit(solution)/shard_map/ppermute | solution.py:420
  28.6 0.0 collective-permute-done.5
  28.6 2.8 %collective-permute-start.10 = (f32[88,128]{1,0:T(8,128)S(1)}, f32[88,128]{1,0:T(8,128)S(1)}, u32[]{:S(2)}, u32[]{:S(2)}) collective-permute-start(f32[88,128]{1,0:T(8,128)S(1)} %fusion), channel_id=1, source_target_pairs={{0,24},{1,25},{2,26},{3,27},{4,28},{5,29},{6,30},{7,31},{8,16},{9,... | collective-permute-start | bytes 135176 | tf_op jit(solution)/shard_map/ppermute | solution.py:420
  31.5 0.3 collective-permute-start.9
  31.7 1.4 %collective-permute-start.8 = (f32[88,128]{1,0:T(8,128)S(1)}, f32[88,128]{1,0:T(8,128)S(1)}, u32[]{:S(2)}, u32[]{:S(2)}) collective-permute-start(f32[88,128]{1,0:T(8,128)S(1)} %fusion), channel_id=1, source_target_pairs={{0,8},{1,9},{2,10},{3,11},{4,12},{5,13},{6,14},{7,15},{8,0},{9,1},... | collective-permute-start | bytes 135176 | tf_op jit(solution)/shard_map/ppermute | solution.py:420
  33.1 0.0 collective-permute-done.11.ringed
  33.1 1.3 %grad_input.1 = f32[256,128]{1,0:T(8,128)} custom-call(f32[320,128]{1,0:T(8,128)S(1)} %get-tuple-element.48.own, f32[192,128]{1,0:T(8,128)S(1)} %slice.34.swapped, f32[128,128]{1,0:T(8,128)S(1)} %collective-permute-done.11.ringed, bf16[384,1152]{1,0:T(8,128)(2,1)S(1)} %get-tuple-element.39.refs_6_.backward), custom_call_target="tpu_custom_call" | custom-call | flops 600000000 | bytes 1000000 | tf_op jit(solution)/shard_map/grad_input/pallas_call | solution.py:538
  34.4 0.2 collective-permute-done.10
  34.6 2.2 %collective-permute-done.9 = f32[88,128]{1,0:T(8,128)S(1)} collective-permute-done((f32[88,128]{1,0:T(8,128)S(1)}, f32[88,128]{1,0:T(8,128)S(1)}, u32[]{:S(2)}, u32[]{:S(2)}) %collective-permute-start.9) | collective-permute-done | bytes 45088 | tf_op jit(solution)/shard_map/ppermute | solution.py:420
  36.7 0.0 collective-permute-done.8
  36.7 1.1 %collective-permute-start.14 = (f32[88,128]{1,0:T(8,128)S(1)}, f32[88,128]{1,0:T(8,128)S(1)}, u32[]{:S(2)}, u32[]{:S(2)}) collective-permute-start(f32[88,128]{1,0:T(8,128)S(1)} %add_add_fusion), channel_id=1, source_target_pairs={{0,5},{1,4},{2,7},{3,6},{4,1},{5,0},{6,3},{7,2},{8,13},{9,12},{10,... | collective-permute-start | bytes 135176 | tf_op jit(solution)/shard_map/ppermute | solution.py:420
  37.8 1.3 %collective-permute-start.13 = (f32[88,128]{1,0:T(8,128)S(1)}, f32[88,128]{1,0:T(8,128)S(1)}, u32[]{:S(2)}, u32[]{:S(2)}) collective-permute-start(f32[88,128]{1,0:T(8,128)S(1)} %add_add_fusion), channel_id=1, source_target_pairs={{0,4},{1,5},{2,6},{3,7},{4,0},{5,1},{6,2},{7,3},{8,12},{9,13},{10,... | collective-permute-start | bytes 135176 | tf_op jit(solution)/shard_map/ppermute | solution.py:420
  39.1 1.2 %collective-permute-start.12 = (f32[88,128]{1,0:T(8,128)S(1)}, f32[88,128]{1,0:T(8,128)S(1)}, u32[]{:S(2)}, u32[]{:S(2)}) collective-permute-start(f32[88,128]{1,0:T(8,128)S(1)} %add_add_fusion), channel_id=1, source_target_pairs={{0,1},{1,0},{2,3},{3,2},{4,5},{5,4},{6,7},{7,6},{8,9},{9,8},{10,11... | collective-permute-start | bytes 135176 | tf_op jit(solution)/shard_map/ppermute | solution.py:420
  40.3 2.9 %collective-permute-done.12 = f32[88,128]{1,0:T(8,128)S(1)} collective-permute-done((f32[88,128]{1,0:T(8,128)S(1)}, f32[88,128]{1,0:T(8,128)S(1)}, u32[]{:S(2)}, u32[]{:S(2)}) %collective-permute-start.12) | collective-permute-done | bytes 45088 | tf_op jit(solution)/shard_map/ppermute | solution.py:420
  43.2 0.0 collective-permute-done.13
  43.2 0.0 collective-permute-done.14
  43.2 0.1 collective-permute-start.15
  43.3 1.4 %collective-permute-done.15.other = f32[352,128]{1,0:T(8,128)S(1)} collective-permute-done((f32[352,128]{1,0:T(8,128)S(1)}, f32[352,128]{1,0:T(8,128)S(1)}, u32[]{:S(2)}, u32[]{:S(2)}) %collective-permute-start.15) | collective-permute-done | bytes 180256 | tf_op jit(solution)/shard_map/ppermute | solution.py:420
  44.7 1.2 %unpack.1 = (f32[27,32,32]{2,1,0:T(8,128)}, f32[27,32,32]{2,1,0:T(8,128)}, f32[27,32,32]{2,1,0:T(8,128)}) custom-call(f32[352,128]{1,0:T(8,128)S(1)} %constant_dynamic-update-slice_fusion.mine, f32[352,128]{1,0:T(8,128)S(1)} %collective-permute-done.15.other), custom_call_target="tpu_custom_call" | custom-call | tf_op jit(solution)/shard_map/unpack/pallas_call | solution.py:550
  (10 shorter events, 0.1 us)
Async XLA Ops:
  2.2 2.2 %collective-permute-start = (f32[1024,128]{1,0:T(8,128)S(1)}, f32[1024,128]{1,0:T(8,128)S(1)}, u32[]{:S(2)}, u32[]{:S(2)}) collective-permute-start(f32[1024,128]{1,0:T(8,128)S(1)} %get-tuple-element.29.local.refs_0_), channel_id=1, source_target_pairs={{0,2},{2,0},{4,6},{6,4},{8,10},{10,8},{12,14},{14,12},{16,18},{18,... | collective-permute-start | bytes 1572872 | tf_op jit(solution)/shard_map/ppermute | solution.py:465
  4.5 10.2 %collective-permute-start.1 = (f32[512,128]{1,0:T(8,128)S(1)}, f32[512,128]{1,0:T(8,128)S(1)}, u32[]{:S(2)}, u32[]{:S(2)}) collective-permute-start(f32[512,128]{1,0:T(8,128)S(1)} %pack_rows.1), channel_id=1, source_target_pairs={{0,4},{2,0},{4,8},{6,2},{8,12},{10,6},{12,16},{14,10},{16,20},{18,... | collective-permute-start | bytes 786440 | tf_op jit(solution)/shard_map/ppermute | solution.py:502
  7.6 4.3 %collective-permute-start.2 = (f32[128,128]{1,0:T(8,128)S(1)}, f32[128,128]{1,0:T(8,128)S(1)}, u32[]{:S(2)}, u32[]{:S(2)}) collective-permute-start(f32[128,128]{1,0:T(8,128)S(1)} %get-tuple-element.36), channel_id=1, source_target_pairs={{0,1},{1,0},{2,3},{3,2},{4,5},{5,4},{6,7},{7,6},{8,9},{9,8},{10,11... | collective-permute-start | bytes 196616 | tf_op jit(solution)/shard_map/ppermute | solution.py:504
  9.2 4.5 %collective-permute-start.3 = (f32[64,128]{1,0:T(8,128)S(1)}, f32[64,128]{1,0:T(8,128)S(1)}, u32[]{:S(2)}, u32[]{:S(2)}) collective-permute-start(f32[64,128]{1,0:T(8,128)S(1)} %get-tuple-element.37), channel_id=1, source_target_pairs={{0,5},{1,4},{2,1},{3,0},{4,9},{5,8},{6,3},{7,2},{8,13},{9,12},{10,... | collective-permute-start | bytes 98312 | tf_op jit(solution)/shard_map/ppermute | solution.py:503
  19.4 1.6 %collective-permute-start.4 = (f32[544,128]{1,0:T(8,128)S(1)}, f32[544,128]{1,0:T(8,128)S(1)}, u32[]{:S(2)}, u32[]{:S(2)}) collective-permute-start(f32[544,128]{1,0:T(8,128)S(1)} %get-tuple-element.47), channel_id=1, source_target_pairs={{0,2},{1,3},{2,0},{3,1},{4,6},{5,7},{6,4},{7,5},{8,10},{9,11},{10,... | collective-permute-start | bytes 835592 | tf_op jit(solution)/shard_map/ppermute | solution.py:420
  21.0 6.1 %collective-permute-start.7 = (f32[88,128]{1,0:T(8,128)S(1)}, f32[88,128]{1,0:T(8,128)S(1)}, u32[]{:S(2)}, u32[]{:S(2)}) collective-permute-start(f32[88,128]{1,0:T(8,128)S(1)} %get-tuple-element.54), channel_id=1, source_target_pairs={{0,5},{1,4},{2,7},{3,6},{4,1},{5,0},{6,3},{7,2},{8,13},{9,12},{10,... | collective-permute-start | bytes 135176 | tf_op jit(solution)/shard_map/ppermute | solution.py:420
  24.5 4.1 %collective-permute-start.6 = (f32[88,128]{1,0:T(8,128)S(1)}, f32[88,128]{1,0:T(8,128)S(1)}, u32[]{:S(2)}, u32[]{:S(2)}) collective-permute-start(f32[88,128]{1,0:T(8,128)S(1)} %get-tuple-element.55), channel_id=1, source_target_pairs={{0,4},{1,5},{2,6},{3,7},{4,0},{5,1},{6,2},{7,3},{8,12},{9,13},{10,... | collective-permute-start | bytes 135176 | tf_op jit(solution)/shard_map/ppermute | solution.py:420
  24.5 4.1 %collective-permute-start.5 = (f32[88,128]{1,0:T(8,128)S(1)}, f32[88,128]{1,0:T(8,128)S(1)}, u32[]{:S(2)}, u32[]{:S(2)}) collective-permute-start(f32[88,128]{1,0:T(8,128)S(1)} %get-tuple-element.56), channel_id=1, source_target_pairs={{0,1},{1,0},{2,3},{3,2},{4,5},{5,4},{6,7},{7,6},{8,9},{9,8},{10,11... | collective-permute-start | bytes 135176 | tf_op jit(solution)/shard_map/ppermute | solution.py:420
  25.1 7.9 %collective-permute-start.11 = (f32[128,128]{1,0:T(8,128)S(1)}, f32[128,128]{1,0:T(8,128)S(1)}, u32[]{:S(2)}, u32[]{:S(2)}) collective-permute-start(f32[128,128]{1,0:T(8,128)S(1)} %slice.35), channel_id=1, source_target_pairs={{0,4},{2,0},{4,8},{6,2},{8,12},{10,6},{12,16},{14,10},{16,20},{18,... | collective-permute-start | bytes 196616 | tf_op jit(solution)/shard_map/ppermute | solution.py:537
  28.6 5.9 %collective-permute-start.10 = (f32[88,128]{1,0:T(8,128)S(1)}, f32[88,128]{1,0:T(8,128)S(1)}, u32[]{:S(2)}, u32[]{:S(2)}) collective-permute-start(f32[88,128]{1,0:T(8,128)S(1)} %fusion), channel_id=1, source_target_pairs={{0,24},{1,25},{2,26},{3,27},{4,28},{5,29},{6,30},{7,31},{8,16},{9,... | collective-permute-start | bytes 135176 | tf_op jit(solution)/shard_map/ppermute | solution.py:420
  31.5 5.2 %collective-permute-start.9 = (f32[88,128]{1,0:T(8,128)S(1)}, f32[88,128]{1,0:T(8,128)S(1)}, u32[]{:S(2)}, u32[]{:S(2)}) collective-permute-start(f32[88,128]{1,0:T(8,128)S(1)} %fusion), channel_id=1, source_target_pairs={{0,16},{1,17},{2,18},{3,19},{4,20},{5,21},{6,22},{7,23},{8,24},{9,... | collective-permute-start | bytes 135176 | tf_op jit(solution)/shard_map/ppermute | solution.py:420
  31.7 5.0 %collective-permute-start.8 = (f32[88,128]{1,0:T(8,128)S(1)}, f32[88,128]{1,0:T(8,128)S(1)}, u32[]{:S(2)}, u32[]{:S(2)}) collective-permute-start(f32[88,128]{1,0:T(8,128)S(1)} %fusion), channel_id=1, source_target_pairs={{0,8},{1,9},{2,10},{3,11},{4,12},{5,13},{6,14},{7,15},{8,0},{9,1},... | collective-permute-start | bytes 135176 | tf_op jit(solution)/shard_map/ppermute | solution.py:420
  36.7 6.4 %collective-permute-start.14 = (f32[88,128]{1,0:T(8,128)S(1)}, f32[88,128]{1,0:T(8,128)S(1)}, u32[]{:S(2)}, u32[]{:S(2)}) collective-permute-start(f32[88,128]{1,0:T(8,128)S(1)} %add_add_fusion), channel_id=1, source_target_pairs={{0,5},{1,4},{2,7},{3,6},{4,1},{5,0},{6,3},{7,2},{8,13},{9,12},{10,... | collective-permute-start | bytes 135176 | tf_op jit(solution)/shard_map/ppermute | solution.py:420
  37.8 5.4 %collective-permute-start.13 = (f32[88,128]{1,0:T(8,128)S(1)}, f32[88,128]{1,0:T(8,128)S(1)}, u32[]{:S(2)}, u32[]{:S(2)}) collective-permute-start(f32[88,128]{1,0:T(8,128)S(1)} %add_add_fusion), channel_id=1, source_target_pairs={{0,4},{1,5},{2,6},{3,7},{4,0},{5,1},{6,2},{7,3},{8,12},{9,13},{10,... | collective-permute-start | bytes 135176 | tf_op jit(solution)/shard_map/ppermute | solution.py:420
  39.1 4.0 %collective-permute-start.12 = (f32[88,128]{1,0:T(8,128)S(1)}, f32[88,128]{1,0:T(8,128)S(1)}, u32[]{:S(2)}, u32[]{:S(2)}) collective-permute-start(f32[88,128]{1,0:T(8,128)S(1)} %add_add_fusion), channel_id=1, source_target_pairs={{0,1},{1,0},{2,3},{3,2},{4,5},{5,4},{6,7},{7,6},{8,9},{9,8},{10,11... | collective-permute-start | bytes 135176 | tf_op jit(solution)/shard_map/ppermute | solution.py:420
  43.2 1.5 %collective-permute-start.15 = (f32[352,128]{1,0:T(8,128)S(1)}, f32[352,128]{1,0:T(8,128)S(1)}, u32[]{:S(2)}, u32[]{:S(2)}) collective-permute-start(f32[352,128]{1,0:T(8,128)S(1)} %constant_dynamic-update-slice_fusion.mine), channel_id=1, source_target_pairs={{0,2},{1,3},{2,0},{3,1},{4,6},{5,7},{6,4},{7,5},{8,10},{9,11},{10,... | collective-permute-start | bytes 540680 | tf_op jit(solution)/shard_map/ppermute | solution.py:420

commit v6 on v5

--- a/solution.py
+++ b/solution.py
@@ -311,22 +311,27 @@
             parts = [split(h_main[HALO + r]) for r in range(rows)]
             center = [jnp.concatenate([part[k] for part in parts], axis=1) for k in range(2)]
             center = jnp.concatenate(center, axis=0)
-        tiles, extra = [], []
-        for b in range(3):
-            window = xs[:, pl.ds((HALO + b - 1) * LANES, rows * LANES)]
-            product = lax.dot_general(center, window, NT, preferred_element_type=F32)
-            product = product[:planes] + product[planes:]
-            for c in range(3):
-                tile = product[:, c * LANES : (c + 1) * LANES]
-                tile = (tile + roll(tile, planes)) * factor
-                upper, lower = tile[:channels], tile[channels:]
-                middle = upper + roll(lower, -channels)
-                tiles.append(jnp.where(half < channels, lower, jnp.where(half < 2 * channels, upper, middle)))
-        for m in range(7):
-            tile = tiles[m]
-            if m < 6:
-                source, part = tiles[7 + m // 3], m % 3
-                tile = jnp.where(half < 3 * channels, tile, roll(source, (3 - part) * channels))
+        blocks = []
+        for m in range(9):
+            at = pl.ds((HALO + m // 3 - 1) * LANES, rows * LANES)
+            base = m % 3 * LANES
+            parts = [xs[pl.ds(base + k * planes, planes), at] for k in range(2)]
+            blocks.append(jnp.concatenate(parts, axis=1))
+        window = jnp.concatenate(blocks + blocks[-1:], axis=0)
+        center = jnp.concatenate([center, center], axis=1)
+        product = lax.dot_general(center, window, NT, preferred_element_type=F32)
+        product = (product[:planes] + product[planes:]) * factor
+        first = lax.rem(half // channels, 2) == 0
+        mixed, summed = [], []
+        for t in range(5):
+            part = product[:, t * LANES : (t + 1) * LANES]
+            upper, lower = part[:channels], part[channels:]
+            mixed.append(jnp.where(first, lower, upper))
+            summed.append(upper + roll(lower, -channels))
+        tiles = mixed[:4] + [jnp.where(half < planes, mixed[4], summed[4])]
+        for t in (0, 2):
+            tiles.append(jnp.where(first, summed[t], roll(summed[t + 1], channels)))
+        for m, tile in enumerate(tiles):
             gsum[pl.ds((layer * 7 + m) * channels, channels), :] = tile
 
         if h_width:
@@ -389,18 +394,14 @@
         at = pl.ds(k * size, size)
         whole[pl.ds(pl.multiple_of(core * 4 * size + piece, 8), size), :] = mine[at, :]
         whole[pl.ds(pl.multiple_of((1 - core) * 4 * size + piece, 8), size), :] = other[at, :]
-    order = (0, 2, 1)
+    places = [[(s % 2 * 2, 2 * t + s // 2) for s in range(4)] for t in range(4)]
+    places.append([(0, 8), (2, 8), (1, 8)])
+    places += [[(1, t + k) for k in (0, 2, 1, 3)] for t in (0, 4)]
     for layer in range(LAYERS):
-        for m in range(7):
-            tile = whole[pl.ds((layer * 7 + m) * channels, channels), :]
-            for s in range(4):
-                if s < 3:
-                    tap = 9 * order[s] + m
-                elif m < 6:
-                    tap = 9 * order[m % 3] + 7 + m // 3
-                else:
-                    continue
-                outs[layer][tap] = roll(tile, -s * channels)[:, :channels]
+        for t, blocks in enumerate(places):
+            tile = whole[pl.ds((layer * 7 + t) * channels, channels), :]
+            for s, (a, m) in enumerate(blocks):
+                outs[layer][9 * a + m] = roll(tile, -s * channels)[:, :channels]
 
 
 def pair_rounds(size):

time: 46.1 us -> 45.6 us (0.989)
  no operation moved by 1% of the time
where the time goes in v6:
time: 45.6 us; the launch traced here: 45.5 us
  starting transfers between devices  20.6 us (45%)
  Pallas kernels  12.1 us (27%)
  waiting for transfers between devices  12 us (26%)
  between operations  0.76 us (2%)
    ppermute x11, starting transfers between devices, swap(): return lax.ppermute(value, axes, [(i, i ^ bits) for i in range(total)])  12.3 us
    ppermute x11, waiting for transfers between devices, swap(): return lax.ppermute(value, axes, [(i, i ^ bits) for i in range(total)])  9.69 us
    pallas_call x1, Pallas kernels, per_device(): pl.pallas_call(functools.partial(layers_kernel, depth, rows, channels, le...  4.21 us
    ppermute x1, starting transfers between devices, per_device(): outer = lax.ppermute(outer, 'gx', across)  2.82 us
    ppermute x1, starting transfers between devices, input_gradient(): ringed = lax.ppermute(swapped[planes:], 'gx', across)  1.91 us
    pallas_call x1, Pallas kernels, per_device(): pl.pallas_call(functools.partial(early_kernel, depth, rows), out_shape=[s...  1.69 us
    pallas_call x1, Pallas kernels, per_device(): pl.pallas_call(functools.partial(weight_kernel, channels, depth), out_sha...  1.63 us
    pallas_call x1, Pallas kernels, per_device(): pl.pallas_call(fetch_kernel, out_shape=[pltpu.VMEM((4 * size, cols), F32)...  1.6 us
  transfers between devices with their start and end apart: 16, of which 8 were waited for; matrix products, arithmetic and copies ran while one was open for 0% of the time, Pallas kernels for 11%

profile of v6, /device:TPU:0, one launch (start us, length us, event | category | flops | bytes accessed | tf_op | source)
XLA Modules:
  0.0 45.5 jit_solution(6704819032742699680)
XLA Ops:
  0.6 1.6 %fetch.1 = (f32[1024,128]{1,0:T(8,128)S(1)}, f32[27,32,32]{2,1,0:T(8,128)S(1)}, f32[27,32,32]{2,1,0:T(8,128)S(1)}, f32[27,32,32]{2,1,0:T(8,128)S(1)}) custom-call(f32[256,128]{1,0:T(8,128)} %bitcast.5, f32[256,128]{1,0:T(8,128)} %bitcast.6, f32[256,128]{1,0:T(8,128)} %bitcast.7, f32[256,128]{1,0:T(8,128)} %bitcast.8, f32[27,32,32]{2,1,0:T(8,128)} %refs_4_.1, ...), custom_call_target="tpu_custom_call" | custom-call | tf_op jit(solution)/shard_map/fetch/pallas_call | solution.py:456
  2.2 0.5 %collective-permute-start = (f32[1024,128]{1,0:T(8,128)S(1)}, f32[1024,128]{1,0:T(8,128)S(1)}, u32[]{:S(2)}, u32[]{:S(2)}) collective-permute-start(f32[1024,128]{1,0:T(8,128)S(1)} %get-tuple-element.29.local.refs_0_), channel_id=1, source_target_pairs={{0,2},{2,0},{4,6},{6,4},{8,10},{10,8},{12,14},{14,12},{16,18},{18,... | collective-permute-start | bytes 1572872 | tf_op jit(solution)/shard_map/ppermute | solution.py:466
  2.8 1.6 %weights.1 = (bf16[384,1152]{1,0:T(8,128)(2,1)S(1)}, bf16[384,1152]{1,0:T(8,128)(2,1)S(1)}) custom-call(f32[27,32,32]{2,1,0:T(8,128)S(1)} %get-tuple-element.30.refs_0_, f32[27,32,32]{2,1,0:T(8,128)S(1)} %get-tuple-element.31.refs_1_, f32[27,32,32]{2,1,0:T(8,128)S(1)} %get-tuple-element.32.refs_2_), custom_call_target="tpu_custom_call" | custom-call | flops 20000000 | bytes 4000000 | tf_op jit(solution)/shard_map/weights/pallas_call | solution.py:471
  4.4 0.0 collective-permute-done.sibling.refs_1_
  4.4 0.1 pack_rows.1
  4.5 2.8 %collective-permute-start.1 = (f32[512,128]{1,0:T(8,128)S(1)}, f32[512,128]{1,0:T(8,128)S(1)}, u32[]{:S(2)}, u32[]{:S(2)}) collective-permute-start(f32[512,128]{1,0:T(8,128)S(1)} %pack_rows.1), channel_id=1, source_target_pairs={{0,4},{2,0},{4,8},{6,2},{8,12},{10,6},{12,16},{14,10},{16,20},{18,... | collective-permute-start | bytes 786440 | tf_op jit(solution)/shard_map/ppermute | solution.py:503
  7.3 0.3 pack_strips.1
  7.6 1.6 %collective-permute-start.2 = (f32[128,128]{1,0:T(8,128)S(1)}, f32[128,128]{1,0:T(8,128)S(1)}, u32[]{:S(2)}, u32[]{:S(2)}) collective-permute-start(f32[128,128]{1,0:T(8,128)S(1)} %get-tuple-element.36), channel_id=1, source_target_pairs={{0,1},{1,0},{2,3},{3,2},{4,5},{5,4},{6,7},{7,6},{8,9},{9,8},{10,11... | collective-permute-start | bytes 196616 | tf_op jit(solution)/shard_map/ppermute | solution.py:505
  9.2 1.5 %collective-permute-start.3 = (f32[64,128]{1,0:T(8,128)S(1)}, f32[64,128]{1,0:T(8,128)S(1)}, u32[]{:S(2)}, u32[]{:S(2)}) collective-permute-start(f32[64,128]{1,0:T(8,128)S(1)} %get-tuple-element.37), channel_id=1, source_target_pairs={{0,5},{1,4},{2,1},{3,0},{4,9},{5,8},{6,3},{7,2},{8,13},{9,12},{10,... | collective-permute-start | bytes 98312 | tf_op jit(solution)/shard_map/ppermute | solution.py:504
  10.7 1.3 %collective-permute-done.2.refs_2_.refs_3_ = f32[128,128]{1,0:T(8,128)S(1)} collective-permute-done((f32[128,128]{1,0:T(8,128)S(1)}, f32[128,128]{1,0:T(8,128)S(1)}, u32[]{:S(2)}, u32[]{:S(2)}) %collective-permute-start.2) | collective-permute-done | bytes 65568 | tf_op jit(solution)/shard_map/ppermute | solution.py:505
  12.0 1.7 %early.1 = (bf16[384,1536]{1,0:T(8,128)(2,1)S(1)}, bf16[384,1536]{1,0:T(8,128)(2,1)S(1)}, bf16[384,1536]{1,0:T(8,128)(2,1)S(1)}, f32[64,128]{1,0:T(8,128)S(1)}, ...) custom-call(f32[1024,128]{1,0:T(8,128)S(1)} %get-tuple-element.29.local.refs_0_, ...), custom_call_target="tpu_custom_call" | custom-call | flops 20000000 | bytes 6000000 | tf_op jit(solution)/shard_map/early/pallas_call | solution.py:510
  13.7 0.0 collective-permute-done.3.refs_4_
  13.7 1.0 %collective-permute-done.1.refs_2_ = f32[512,128]{1,0:T(8,128)S(1)} collective-permute-done((f32[512,128]{1,0:T(8,128)S(1)}, f32[512,128]{1,0:T(8,128)S(1)}, u32[]{:S(2)}, u32[]{:S(2)}) %collective-permute-start.1) | collective-permute-done | bytes 262176 | tf_op jit(solution)/shard_map/ppermute | solution.py:503
  14.7 4.2 %layers.1 = (f32[320,128]{1,0:T(8,128)S(1)}, f32[352,128]{1,0:T(8,128)S(1)}, f32[544,128]{1,0:T(8,128)S(1)}, bf16[384,1536]{1,0:T(8,128)(2,1)S(1)}, bf16[384,153...) custom-call(f32[1024,128]{1,0:T(8,128)S(1)} %get-tuple-element.29.lo, ...), custom_call_target="tpu_custom_call", output_to_operand_aliasing={{3}: (10, {}), {4}: (11, {}), {5}: (12, {})} | custom-call | tf_op jit(solution)/shard_map/layers/pallas_call | solution.py:521
  18.9 0.1 collective-permute-start.4
  19.0 1.5 %collective-permute-done.4 = f32[544,128]{1,0:T(8,128)S(1)} collective-permute-done((f32[544,128]{1,0:T(8,128)S(1)}, f32[544,128]{1,0:T(8,128)S(1)}, u32[]{:S(2)}, u32[]{:S(2)}) %collective-permute-start.4) | collective-permute-done | bytes 278560 | tf_op jit(solution)/shard_map/ppermute | solution.py:421
  20.6 3.5 %collective-permute-start.7 = (f32[88,128]{1,0:T(8,128)S(1)}, f32[88,128]{1,0:T(8,128)S(1)}, u32[]{:S(2)}, u32[]{:S(2)}) collective-permute-start(f32[88,128]{1,0:T(8,128)S(1)} %get-tuple-element.54), channel_id=1, source_target_pairs={{0,5},{1,4},{2,7},{3,6},{4,1},{5,0},{6,3},{7,2},{8,13},{9,12},{10,... | collective-permute-start | bytes 135176 | tf_op jit(solution)/shard_map/ppermute | solution.py:421
  24.1 0.0 collective-permute-start.6
  24.1 0.6 %collective-permute-start.5 = (f32[88,128]{1,0:T(8,128)S(1)}, f32[88,128]{1,0:T(8,128)S(1)}, u32[]{:S(2)}, u32[]{:S(2)}) collective-permute-start(f32[88,128]{1,0:T(8,128)S(1)} %get-tuple-element.56), channel_id=1, source_target_pairs={{0,1},{1,0},{2,3},{3,2},{4,5},{5,4},{6,7},{7,6},{8,9},{9,8},{10,11... | collective-permute-start | bytes 135176 | tf_op jit(solution)/shard_map/ppermute | solution.py:421
  24.7 1.9 %collective-permute-start.11 = (f32[128,128]{1,0:T(8,128)S(1)}, f32[128,128]{1,0:T(8,128)S(1)}, u32[]{:S(2)}, u32[]{:S(2)}) collective-permute-start(f32[128,128]{1,0:T(8,128)S(1)} %slice.35), channel_id=1, source_target_pairs={{0,4},{2,0},{4,8},{6,2},{8,12},{10,6},{12,16},{14,10},{16,20},{18,... | collective-permute-start | bytes 196616 | tf_op jit(solution)/shard_map/ppermute | solution.py:538
  26.6 0.0 collective-permute-done.7
  26.6 1.5 %collective-permute-done.6 = f32[88,128]{1,0:T(8,128)S(1)} collective-permute-done((f32[88,128]{1,0:T(8,128)S(1)}, f32[88,128]{1,0:T(8,128)S(1)}, u32[]{:S(2)}, u32[]{:S(2)}) %collective-permute-start.6) | collective-permute-done | bytes 45088 | tf_op jit(solution)/shard_map/ppermute | solution.py:421
  28.2 0.0 collective-permute-done.5
  28.2 2.8 %collective-permute-start.10 = (f32[88,128]{1,0:T(8,128)S(1)}, f32[88,128]{1,0:T(8,128)S(1)}, u32[]{:S(2)}, u32[]{:S(2)}) collective-permute-start(f32[88,128]{1,0:T(8,128)S(1)} %fusion), channel_id=1, source_target_pairs={{0,24},{1,25},{2,26},{3,27},{4,28},{5,29},{6,30},{7,31},{8,16},{9,... | collective-permute-start | bytes 135176 | tf_op jit(solution)/shard_map/ppermute | solution.py:421
  31.0 0.3 collective-permute-start.9
  31.3 1.4 %collective-permute-start.8 = (f32[88,128]{1,0:T(8,128)S(1)}, f32[88,128]{1,0:T(8,128)S(1)}, u32[]{:S(2)}, u32[]{:S(2)}) collective-permute-start(f32[88,128]{1,0:T(8,128)S(1)} %fusion), channel_id=1, source_target_pairs={{0,8},{1,9},{2,10},{3,11},{4,12},{5,13},{6,14},{7,15},{8,0},{9,1},... | collective-permute-start | bytes 135176 | tf_op jit(solution)/shard_map/ppermute | solution.py:421
  32.7 0.0 collective-permute-done.11.ringed
  32.7 1.3 %grad_input.1 = f32[256,128]{1,0:T(8,128)} custom-call(f32[320,128]{1,0:T(8,128)S(1)} %get-tuple-element.48.own, f32[192,128]{1,0:T(8,128)S(1)} %slice.34.swapped, f32[128,128]{1,0:T(8,128)S(1)} %collective-permute-done.11.ringed, bf16[384,1152]{1,0:T(8,128)(2,1)S(1)} %get-tuple-element.39.refs_6_.backward), custom_call_target="tpu_custom_call" | custom-call | flops 600000000 | bytes 1000000 | tf_op jit(solution)/shard_map/grad_input/pallas_call | solution.py:539
  34.0 0.2 collective-permute-done.10
  34.1 2.2 %collective-permute-done.9 = f32[88,128]{1,0:T(8,128)S(1)} collective-permute-done((f32[88,128]{1,0:T(8,128)S(1)}, f32[88,128]{1,0:T(8,128)S(1)}, u32[]{:S(2)}, u32[]{:S(2)}) %collective-permute-start.9) | collective-permute-done | bytes 45088 | tf_op jit(solution)/shard_map/ppermute | solution.py:421
  36.3 0.0 collective-permute-done.8
  36.3 1.1 %collective-permute-start.14 = (f32[88,128]{1,0:T(8,128)S(1)}, f32[88,128]{1,0:T(8,128)S(1)}, u32[]{:S(2)}, u32[]{:S(2)}) collective-permute-start(f32[88,128]{1,0:T(8,128)S(1)} %add_add_fusion), channel_id=1, source_target_pairs={{0,5},{1,4},{2,7},{3,6},{4,1},{5,0},{6,3},{7,2},{8,13},{9,12},{10,... | collective-permute-start | bytes 135176 | tf_op jit(solution)/shard_map/ppermute | solution.py:421
  37.4 1.3 %collective-permute-start.13 = (f32[88,128]{1,0:T(8,128)S(1)}, f32[88,128]{1,0:T(8,128)S(1)}, u32[]{:S(2)}, u32[]{:S(2)}) collective-permute-start(f32[88,128]{1,0:T(8,128)S(1)} %add_add_fusion), channel_id=1, source_target_pairs={{0,4},{1,5},{2,6},{3,7},{4,0},{5,1},{6,2},{7,3},{8,12},{9,13},{10,... | collective-permute-start | bytes 135176 | tf_op jit(solution)/shard_map/ppermute | solution.py:421
  38.7 1.2 %collective-permute-start.12 = (f32[88,128]{1,0:T(8,128)S(1)}, f32[88,128]{1,0:T(8,128)S(1)}, u32[]{:S(2)}, u32[]{:S(2)}) collective-permute-start(f32[88,128]{1,0:T(8,128)S(1)} %add_add_fusion), channel_id=1, source_target_pairs={{0,1},{1,0},{2,3},{3,2},{4,5},{5,4},{6,7},{7,6},{8,9},{9,8},{10,11... | collective-permute-start | bytes 135176 | tf_op jit(solution)/shard_map/ppermute | solution.py:421
  39.9 2.9 %collective-permute-done.12 = f32[88,128]{1,0:T(8,128)S(1)} collective-permute-done((f32[88,128]{1,0:T(8,128)S(1)}, f32[88,128]{1,0:T(8,128)S(1)}, u32[]{:S(2)}, u32[]{:S(2)}) %collective-permute-start.12) | collective-permute-done | bytes 45088 | tf_op jit(solution)/shard_map/ppermute | solution.py:421
  42.7 0.0 collective-permute-done.13
  42.7 0.0 collective-permute-done.14
  42.8 0.1 collective-permute-start.15
  42.9 1.4 %collective-permute-done.15.other = f32[352,128]{1,0:T(8,128)S(1)} collective-permute-done((f32[352,128]{1,0:T(8,128)S(1)}, f32[352,128]{1,0:T(8,128)S(1)}, u32[]{:S(2)}, u32[]{:S(2)}) %collective-permute-start.15) | collective-permute-done | bytes 180256 | tf_op jit(solution)/shard_map/ppermute | solution.py:421
  44.3 1.2 %unpack.1 = (f32[27,32,32]{2,1,0:T(8,128)}, f32[27,32,32]{2,1,0:T(8,128)}, f32[27,32,32]{2,1,0:T(8,128)}) custom-call(f32[352,128]{1,0:T(8,128)S(1)} %constant_dynamic-update-slice_fusion.mine, f32[352,128]{1,0:T(8,128)S(1)} %collective-permute-done.15.other), custom_call_target="tpu_custom_call" | custom-call | tf_op jit(solution)/shard_map/unpack/pallas_call | solution.py:551
  (10 shorter events, 0.1 us)
Async XLA Ops:
  2.2 2.2 %collective-permute-start = (f32[1024,128]{1,0:T(8,128)S(1)}, f32[1024,128]{1,0:T(8,128)S(1)}, u32[]{:S(2)}, u32[]{:S(2)}) collective-permute-start(f32[1024,128]{1,0:T(8,128)S(1)} %get-tuple-element.29.local.refs_0_), channel_id=1, source_target_pairs={{0,2},{2,0},{4,6},{6,4},{8,10},{10,8},{12,14},{14,12},{16,18},{18,... | collective-permute-start | bytes 1572872 | tf_op jit(solution)/shard_map/ppermute | solution.py:466
  4.5 10.2 %collective-permute-start.1 = (f32[512,128]{1,0:T(8,128)S(1)}, f32[512,128]{1,0:T(8,128)S(1)}, u32[]{:S(2)}, u32[]{:S(2)}) collective-permute-start(f32[512,128]{1,0:T(8,128)S(1)} %pack_rows.1), channel_id=1, source_target_pairs={{0,4},{2,0},{4,8},{6,2},{8,12},{10,6},{12,16},{14,10},{16,20},{18,... | collective-permute-start | bytes 786440 | tf_op jit(solution)/shard_map/ppermute | solution.py:503
  7.6 4.3 %collective-permute-start.2 = (f32[128,128]{1,0:T(8,128)S(1)}, f32[128,128]{1,0:T(8,128)S(1)}, u32[]{:S(2)}, u32[]{:S(2)}) collective-permute-start(f32[128,128]{1,0:T(8,128)S(1)} %get-tuple-element.36), channel_id=1, source_target_pairs={{0,1},{1,0},{2,3},{3,2},{4,5},{5,4},{6,7},{7,6},{8,9},{9,8},{10,11... | collective-permute-start | bytes 196616 | tf_op jit(solution)/shard_map/ppermute | solution.py:505
  9.2 4.5 %collective-permute-start.3 = (f32[64,128]{1,0:T(8,128)S(1)}, f32[64,128]{1,0:T(8,128)S(1)}, u32[]{:S(2)}, u32[]{:S(2)}) collective-permute-start(f32[64,128]{1,0:T(8,128)S(1)} %get-tuple-element.37), channel_id=1, source_target_pairs={{0,5},{1,4},{2,1},{3,0},{4,9},{5,8},{6,3},{7,2},{8,13},{9,12},{10,... | collective-permute-start | bytes 98312 | tf_op jit(solution)/shard_map/ppermute | solution.py:504
  18.9 1.6 %collective-permute-start.4 = (f32[544,128]{1,0:T(8,128)S(1)}, f32[544,128]{1,0:T(8,128)S(1)}, u32[]{:S(2)}, u32[]{:S(2)}) collective-permute-start(f32[544,128]{1,0:T(8,128)S(1)} %get-tuple-element.47), channel_id=1, source_target_pairs={{0,2},{1,3},{2,0},{3,1},{4,6},{5,7},{6,4},{7,5},{8,10},{9,11},{10,... | collective-permute-start | bytes 835592 | tf_op jit(solution)/shard_map/ppermute | solution.py:421
  20.6 6.1 %collective-permute-start.7 = (f32[88,128]{1,0:T(8,128)S(1)}, f32[88,128]{1,0:T(8,128)S(1)}, u32[]{:S(2)}, u32[]{:S(2)}) collective-permute-start(f32[88,128]{1,0:T(8,128)S(1)} %get-tuple-element.54), channel_id=1, source_target_pairs={{0,5},{1,4},{2,7},{3,6},{4,1},{5,0},{6,3},{7,2},{8,13},{9,12},{10,... | collective-permute-start | bytes 135176 | tf_op jit(solution)/shard_map/ppermute | solution.py:421
  24.1 4.1 %collective-permute-start.6 = (f32[88,128]{1,0:T(8,128)S(1)}, f32[88,128]{1,0:T(8,128)S(1)}, u32[]{:S(2)}, u32[]{:S(2)}) collective-permute-start(f32[88,128]{1,0:T(8,128)S(1)} %get-tuple-element.55), channel_id=1, source_target_pairs={{0,4},{1,5},{2,6},{3,7},{4,0},{5,1},{6,2},{7,3},{8,12},{9,13},{10,... | collective-permute-start | bytes 135176 | tf_op jit(solution)/shard_map/ppermute | solution.py:421
  24.1 4.1 %collective-permute-start.5 = (f32[88,128]{1,0:T(8,128)S(1)}, f32[88,128]{1,0:T(8,128)S(1)}, u32[]{:S(2)}, u32[]{:S(2)}) collective-permute-start(f32[88,128]{1,0:T(8,128)S(1)} %get-tuple-element.56), channel_id=1, source_target_pairs={{0,1},{1,0},{2,3},{3,2},{4,5},{5,4},{6,7},{7,6},{8,9},{9,8},{10,11... | collective-permute-start | bytes 135176 | tf_op jit(solution)/shard_map/ppermute | solution.py:421
  24.7 7.9 %collective-permute-start.11 = (f32[128,128]{1,0:T(8,128)S(1)}, f32[128,128]{1,0:T(8,128)S(1)}, u32[]{:S(2)}, u32[]{:S(2)}) collective-permute-start(f32[128,128]{1,0:T(8,128)S(1)} %slice.35), channel_id=1, source_target_pairs={{0,4},{2,0},{4,8},{6,2},{8,12},{10,6},{12,16},{14,10},{16,20},{18,... | collective-permute-start | bytes 196616 | tf_op jit(solution)/shard_map/ppermute | solution.py:538
  28.2 5.9 %collective-permute-start.10 = (f32[88,128]{1,0:T(8,128)S(1)}, f32[88,128]{1,0:T(8,128)S(1)}, u32[]{:S(2)}, u32[]{:S(2)}) collective-permute-start(f32[88,128]{1,0:T(8,128)S(1)} %fusion), channel_id=1, source_target_pairs={{0,24},{1,25},{2,26},{3,27},{4,28},{5,29},{6,30},{7,31},{8,16},{9,... | collective-permute-start | bytes 135176 | tf_op jit(solution)/shard_map/ppermute | solution.py:421
  31.0 5.2 %collective-permute-start.9 = (f32[88,128]{1,0:T(8,128)S(1)}, f32[88,128]{1,0:T(8,128)S(1)}, u32[]{:S(2)}, u32[]{:S(2)}) collective-permute-start(f32[88,128]{1,0:T(8,128)S(1)} %fusion), channel_id=1, source_target_pairs={{0,16},{1,17},{2,18},{3,19},{4,20},{5,21},{6,22},{7,23},{8,24},{9,... | collective-permute-start | bytes 135176 | tf_op jit(solution)/shard_map/ppermute | solution.py:421
  31.3 5.0 %collective-permute-start.8 = (f32[88,128]{1,0:T(8,128)S(1)}, f32[88,128]{1,0:T(8,128)S(1)}, u32[]{:S(2)}, u32[]{:S(2)}) collective-permute-start(f32[88,128]{1,0:T(8,128)S(1)} %fusion), channel_id=1, source_target_pairs={{0,8},{1,9},{2,10},{3,11},{4,12},{5,13},{6,14},{7,15},{8,0},{9,1},... | collective-permute-start | bytes 135176 | tf_op jit(solution)/shard_map/ppermute | solution.py:421
  36.3 6.4 %collective-permute-start.14 = (f32[88,128]{1,0:T(8,128)S(1)}, f32[88,128]{1,0:T(8,128)S(1)}, u32[]{:S(2)}, u32[]{:S(2)}) collective-permute-start(f32[88,128]{1,0:T(8,128)S(1)} %add_add_fusion), channel_id=1, source_target_pairs={{0,5},{1,4},{2,7},{3,6},{4,1},{5,0},{6,3},{7,2},{8,13},{9,12},{10,... | collective-permute-start | bytes 135176 | tf_op jit(solution)/shard_map/ppermute | solution.py:421
  37.4 5.4 %collective-permute-start.13 = (f32[88,128]{1,0:T(8,128)S(1)}, f32[88,128]{1,0:T(8,128)S(1)}, u32[]{:S(2)}, u32[]{:S(2)}) collective-permute-start(f32[88,128]{1,0:T(8,128)S(1)} %add_add_fusion), channel_id=1, source_target_pairs={{0,4},{1,5},{2,6},{3,7},{4,0},{5,1},{6,2},{7,3},{8,12},{9,13},{10,... | collective-permute-start | bytes 135176 | tf_op jit(solution)/shard_map/ppermute | solution.py:421
  38.7 4.0 %collective-permute-start.12 = (f32[88,128]{1,0:T(8,128)S(1)}, f32[88,128]{1,0:T(8,128)S(1)}, u32[]{:S(2)}, u32[]{:S(2)}) collective-permute-start(f32[88,128]{1,0:T(8,128)S(1)} %add_add_fusion), channel_id=1, source_target_pairs={{0,1},{1,0},{2,3},{3,2},{4,5},{5,4},{6,7},{7,6},{8,9},{9,8},{10,11... | collective-permute-start | bytes 135176 | tf_op jit(solution)/shard_map/ppermute | solution.py:421
  42.8 1.5 %collective-permute-start.15 = (f32[352,128]{1,0:T(8,128)S(1)}, f32[352,128]{1,0:T(8,128)S(1)}, u32[]{:S(2)}, u32[]{:S(2)}) collective-permute-start(f32[352,128]{1,0:T(8,128)S(1)} %constant_dynamic-update-slice_fusion.mine), channel_id=1, source_target_pairs={{0,2},{1,3},{2,0},{3,1},{4,6},{5,7},{6,4},{7,5},{8,10},{9,11},{10,... | collective-permute-start | bytes 540680 | tf_op jit(solution)/shard_map/ppermute | solution.py:421

commit v7 on v6

--- a/solution.py
+++ b/solution.py
@@ -73,11 +73,7 @@
     return high, low
 
 
-def fetch_kernel(*refs):
-    count = 4 + LAYERS
-    sources, (local, *kernels), semaphores = refs[:count], refs[count : count + 1 + LAYERS], refs[-1]
-    size = sources[0].shape[0]
-    targets = [local.at[pl.ds(f * size, size), :] for f in range(4)] + kernels
+def run_copies(sources, targets, semaphores):
     copies = [
         pltpu.make_async_copy(source, target, semaphores.at[k])
         for k, (source, target) in enumerate(zip(sources, targets))
@@ -86,6 +82,16 @@
         copy.start()
     for copy in copies:
         copy.wait()
+
+
+def fetch_fields(*refs):
+    sources, local, semaphores = refs[:4], refs[4], refs[5]
+    size = sources[0].shape[0]
+    run_copies(sources, [local.at[pl.ds(f * size, size), :] for f in range(4)], semaphores)
+
+
+def fetch_kernels(*refs):
+    run_copies(refs[:LAYERS], refs[LAYERS:-1], refs[-1])
 
 
 def pack_rows(depth, rows, sibling, out):
@@ -453,32 +459,31 @@
 
     kernels = [kernel_three, kernel_two, kernel_one]
     size = planes * rows
-    local, *kernels = pl.pallas_call(
-        fetch_kernel,
-        out_shape=[pltpu.VMEM((4 * size, cols), F32)] + [pltpu.VMEM(v.shape, F32) for v in kernels],
-        in_specs=[pl.BlockSpec(memory_space=pltpu.HBM)] * (4 + LAYERS),
-        out_specs=vmem(1 + LAYERS),
-        scratch_shapes=[pltpu.SemaphoreType.DMA((4 + LAYERS,))],
+    local = pl.pallas_call(
+        fetch_fields,
+        out_shape=pltpu.VMEM((4 * size, cols), F32),
+        in_specs=[pl.BlockSpec(memory_space=pltpu.HBM)] * 4,
+        out_specs=vmem(1)[0],
+        scratch_shapes=[pltpu.SemaphoreType.DMA((4,))],
         compiler_params=room(8),
         name="fetch",
-    )(*(far(v) for v in fields + kernels))
+    )(*(far(v) for v in fields))
 
     sibling = lax.ppermute(local, "gx", [(i, i ^ 1) for i in range(gx_size)])
+    kernels = pl.pallas_call(
+        fetch_kernels,
+        out_shape=[pltpu.VMEM(v.shape, F32) for v in kernels],
+        in_specs=[pl.BlockSpec(memory_space=pltpu.HBM)] * LAYERS,
+        out_specs=vmem(LAYERS),
+        scratch_shapes=[pltpu.SemaphoreType.DMA((LAYERS,))],
+        compiler_params=room(8),
+        cost_estimate=pl.CostEstimate(flops=0, bytes_accessed=4_000_000, transcendentals=0),
+        name="fetch_kernels",
+    )(*(far(v) for v in kernels))
+    sibling, *kernels = lax.optimization_barrier((sibling, *kernels))
     across = [(i, i - 2) if i % 2 else (i, i + 2) for i in range(gx_size)]
     across = [(i, j) if 0 <= j < gx_size else (i, i ^ 1) for i, j in across]
     y_rounds = pair_rounds(gy_size)
-    weight_shape = pltpu.VMEM((LAYERS * 2 * planes, 9 * LANES), BF16)
-    forward, backward = pl.pallas_call(
-        functools.partial(weight_kernel, channels, depth),
-        out_shape=[weight_shape, weight_shape],
-        in_specs=vmem(LAYERS),
-        out_specs=vmem(2),
-        cost_estimate=pl.CostEstimate(flops=20_000_000, bytes_accessed=4_000_000, transcendentals=0),
-        compiler_params=room(12),
-        name="weights",
-    )(*(near(v) for v in kernels))
-
-    sibling, forward, backward = lax.optimization_barrier((sibling, forward, backward))
     outer = pl.pallas_call(
         functools.partial(pack_rows, depth, rows),
         out_shape=pltpu.VMEM((SLABS * planes, cols), F32),
@@ -496,6 +501,18 @@
         cost_estimate=pl.CostEstimate(flops=5_000_000, bytes_accessed=2_000_000, transcendentals=0),
         name="pack_strips",
     )(near(local), near(sibling))
+
+    strips, *kernels = lax.optimization_barrier((strips, *kernels))
+    weight_shape = pltpu.VMEM((LAYERS * 2 * planes, 9 * LANES), BF16)
+    forward, backward = pl.pallas_call(
+        functools.partial(weight_kernel, channels, depth),
+        out_shape=[weight_shape, weight_shape],
+        in_specs=vmem(LAYERS),
+        out_specs=vmem(2),
+        cost_estimate=pl.CostEstimate(flops=20_000_000, bytes_accessed=4_000_000, transcendentals=0),
+        compiler_params=room(12),
+        name="weights",
+    )(*(near(v) for v in kernels))
 
     def diagonal(x_pairs, y_pairs):
         return [(i * gy_size + k, j * gy_size + m) for i, j in x_pairs for k, m in y_pairs]

time: 45.6 us -> 45.2 us (level)
  waiting for transfers between devices: 12 us -> 10.6 us
  Pallas kernels: 12.1 us -> 12.9 us
    ppermute x1, waiting for transfers between devices: 1.28 us -> 0.01 us  [per_device(): strips = [lax.ppermute(strips, 'gy', pairs) for pairs in y_rounds]]
    pallas_call x1 -> x2, Pallas kernels: 1.6 us -> 2.43 us  [the longest x1 1.3 us: per_device(): pl.pallas_call(fetch_kernels, out_shape=[pltpu.VMEM(v.shape, F32) for v i...]
  transfers between devices with their start and end apart: 16 -> 16, of which waited for: 8 -> 8; matrix products, arithmetic and copies ran while one was open for 0% -> 0% of each run, Pallas kernels for 11% -> 14%
where the time goes in v7:
time: 45.2 us; the launch traced here: 45 us
  starting transfers between devices  20.7 us (46%)
  Pallas kernels  12.9 us (29%)
  waiting for transfers between devices  10.6 us (23%)
  between operations  0.77 us (2%)
    ppermute x11, starting transfers between devices, swap(): return lax.ppermute(value, axes, [(i, i ^ bits) for i in range(total)])  12.3 us
    ppermute x11, waiting for transfers between devices, swap(): return lax.ppermute(value, axes, [(i, i ^ bits) for i in range(total)])  9.67 us
    pallas_call x1, Pallas kernels, per_device(): pl.pallas_call(functools.partial(layers_kernel, depth, rows, channels, le...  4.21 us
    ppermute x1, starting transfers between devices, per_device(): outer = lax.ppermute(outer, 'gx', across)  2.94 us
    ppermute x1, starting transfers between devices, input_gradient(): ringed = lax.ppermute(swapped[planes:], 'gx', across)  1.92 us
    pallas_call x1, Pallas kernels, per_device(): pl.pallas_call(functools.partial(early_kernel, depth, rows), out_shape=[s...  1.69 us
    pallas_call x1, Pallas kernels, per_device(): pl.pallas_call(functools.partial(weight_kernel, channels, depth), out_sha...  1.63 us
    ppermute x1, starting transfers between devices, per_device(): strips = [lax.ppermute(strips, 'gy', pairs) for pairs in y_rounds]  1.56 us
  transfers between devices with their start and end apart: 16, of which 8 were waited for; matrix products, arithmetic and copies ran while one was open for 0% of the time, Pallas kernels for 14%

profile of v7, /device:TPU:0, one launch (start us, length us, event | category | flops | bytes accessed | tf_op | source)
XLA Modules:
  0.0 45.0 jit_solution(13386668755603083250)
XLA Ops:
  0.6 1.1 %fetch.1.local.refs_0_ = f32[1024,128]{1,0:T(8,128)S(1)} custom-call(f32[256,128]{1,0:T(8,128)} %bitcast.5, f32[256,128]{1,0:T(8,128)} %bitcast.6, f32[256,128]{1,0:T(8,128)} %bitcast.7, f32[256,128]{1,0:T(8,128)} %bitcast.8), custom_call_target="tpu_custom_call" | custom-call | tf_op jit(solution)/shard_map/fetch/pallas_call | solution.py:462
  1.8 0.5 %collective-permute-start = (f32[1024,128]{1,0:T(8,128)S(1)}, f32[1024,128]{1,0:T(8,128)S(1)}, u32[]{:S(2)}, u32[]{:S(2)}) collective-permute-start(f32[1024,128]{1,0:T(8,128)S(1)} %fetch.1.local.refs_0_), channel_id=1, source_target_pairs={{0,2},{2,0},{4,6},{6,4},{8,10},{10,8},{12,14},{14,12},{16,18},{18,... | collective-permute-start | bytes 1572872 | tf_op jit(solution)/shard_map/ppermute | solution.py:472
  2.3 1.3 %fetch_kernels.1 = (f32[27,32,32]{2,1,0:T(8,128)S(1)}, f32[27,32,32]{2,1,0:T(8,128)S(1)}, f32[27,32,32]{2,1,0:T(8,128)S(1)}) custom-call(f32[27,32,32]{2,1,0:T(8,128)} %refs_0_.1, f32[27,32,32]{2,1,0:T(8,128)} %refs_1_.1, f32[27,32,32]{2,1,0:T(8,128)} %refs_2_.1), custom_call_target="tpu_custom_call" | custom-call | bytes 4000000 | tf_op jit(solution)/shard_map/fetch_kernels/pallas_call | solution.py:473
  3.6 0.2 collective-permute-done.sibling.refs_1_
  3.8 0.1 pack_rows.1
  3.9 2.9 %collective-permute-start.1 = (f32[512,128]{1,0:T(8,128)S(1)}, f32[512,128]{1,0:T(8,128)S(1)}, u32[]{:S(2)}, u32[]{:S(2)}) collective-permute-start(f32[512,128]{1,0:T(8,128)S(1)} %pack_rows.1), channel_id=1, source_target_pairs={{0,4},{2,0},{4,8},{6,2},{8,12},{10,6},{12,16},{14,10},{16,20},{18,... | collective-permute-start | bytes 786440 | tf_op jit(solution)/shard_map/ppermute | solution.py:520
  6.8 0.3 pack_strips.1
  7.2 1.6 %collective-permute-start.2 = (f32[128,128]{1,0:T(8,128)S(1)}, f32[128,128]{1,0:T(8,128)S(1)}, u32[]{:S(2)}, u32[]{:S(2)}) collective-permute-start(f32[128,128]{1,0:T(8,128)S(1)} %get-tuple-element.41), channel_id=1, source_target_pairs={{0,1},{1,0},{2,3},{3,2},{4,5},{5,4},{6,7},{7,6},{8,9},{9,8},{10,11... | collective-permute-start | bytes 196616 | tf_op jit(solution)/shard_map/ppermute | solution.py:522
  8.7 1.5 %collective-permute-start.3 = (f32[64,128]{1,0:T(8,128)S(1)}, f32[64,128]{1,0:T(8,128)S(1)}, u32[]{:S(2)}, u32[]{:S(2)}) collective-permute-start(f32[64,128]{1,0:T(8,128)S(1)} %get-tuple-element.42), channel_id=1, source_target_pairs={{0,5},{1,4},{2,1},{3,0},{4,9},{5,8},{6,3},{7,2},{8,13},{9,12},{10,... | collective-permute-start | bytes 98312 | tf_op jit(solution)/shard_map/ppermute | solution.py:521
  10.2 1.6 %weights.1 = (bf16[384,1152]{1,0:T(8,128)(2,1)S(1)}, bf16[384,1152]{1,0:T(8,128)(2,1)S(1)}) custom-call(f32[27,32,32]{2,1,0:T(8,128)S(1)} %get-tuple-element.43.refs_0_, f32[27,32,32]{2,1,0:T(8,128)S(1)} %get-tuple-element.44.refs_1_, f32[27,32,32]{2,1,0:T(8,128)S(1)} %get-tuple-element.45.refs_2_), custom_call_target="tpu_custom_call" | custom-call | flops 20000000 | bytes 4000000 | tf_op jit(solution)/shard_map/weights/pallas_call | solution.py:507
  11.9 0.0 collective-permute-done.2.refs_2_.refs_3_
  11.9 1.7 %early.1 = (bf16[384,1536]{1,0:T(8,128)(2,1)S(1)}, bf16[384,1536]{1,0:T(8,128)(2,1)S(1)}, bf16[384,1536]{1,0:T(8,128)(2,1)S(1)}, f32[64,128]{1,0:T(8,128)S(1)}, ...) custom-call(f32[1024,128]{1,0:T(8,128)S(1)} %fetch.1.local.refs_0_, f32[1024,128]{1,0:T(8,128)S(1)} %collective-permute-done.sibling.refs_1_, ...), custom_call_target="tpu_custom_call" | custom-call | flops 20000000 | bytes 6000000 | tf_op jit(solution)/shard_map/early/pallas_call | solution.py:527
  13.6 0.0 collective-permute-done.3.refs_4_
  13.6 0.7 %collective-permute-done.1.refs_2_ = f32[512,128]{1,0:T(8,128)S(1)} collective-permute-done((f32[512,128]{1,0:T(8,128)S(1)}, f32[512,128]{1,0:T(8,128)S(1)}, u32[]{:S(2)}, u32[]{:S(2)}) %collective-permute-start.1) | collective-permute-done | bytes 262176 | tf_op jit(solution)/shard_map/ppermute | solution.py:520
  14.2 4.2 %layers.1 = (f32[320,128]{1,0:T(8,128)S(1)}, f32[352,128]{1,0:T(8,128)S(1)}, f32[544,128]{1,0:T(8,128)S(1)}, bf16[384,1536]{1,0:T(8,128)(2,1)S(1)}, bf16[384,153...) custom-call(f32[1024,128]{1,0:T(8,128)S(1)} %fetch.1.local.refs_0_, ...), custom_call_target="tpu_custom_call", output_to_operand_aliasing={{3}: (10, {}), {4}: (11, {}), {5}: (12, {})} | custom-call | tf_op jit(solution)/shard_map/layers/pallas_call | solution.py:538
  18.4 0.1 collective-permute-start.4
  18.5 1.5 %collective-permute-done.4 = f32[544,128]{1,0:T(8,128)S(1)} collective-permute-done((f32[544,128]{1,0:T(8,128)S(1)}, f32[544,128]{1,0:T(8,128)S(1)}, u32[]{:S(2)}, u32[]{:S(2)}) %collective-permute-start.4) | collective-permute-done | bytes 278560 | tf_op jit(solution)/shard_map/ppermute | solution.py:427
  20.1 3.5 %collective-permute-start.7 = (f32[88,128]{1,0:T(8,128)S(1)}, f32[88,128]{1,0:T(8,128)S(1)}, u32[]{:S(2)}, u32[]{:S(2)}) collective-permute-start(f32[88,128]{1,0:T(8,128)S(1)} %get-tuple-element.62), channel_id=1, source_target_pairs={{0,5},{1,4},{2,7},{3,6},{4,1},{5,0},{6,3},{7,2},{8,13},{9,12},{10,... | collective-permute-start | bytes 135176 | tf_op jit(solution)/shard_map/ppermute | solution.py:427
  23.6 0.0 collective-permute-start.6
  23.6 0.6 %collective-permute-start.5 = (f32[88,128]{1,0:T(8,128)S(1)}, f32[88,128]{1,0:T(8,128)S(1)}, u32[]{:S(2)}, u32[]{:S(2)}) collective-permute-start(f32[88,128]{1,0:T(8,128)S(1)} %get-tuple-element.64), channel_id=1, source_target_pairs={{0,1},{1,0},{2,3},{3,2},{4,5},{5,4},{6,7},{7,6},{8,9},{9,8},{10,11... | collective-permute-start | bytes 135176 | tf_op jit(solution)/shard_map/ppermute | solution.py:427
  24.2 1.9 %collective-permute-start.11 = (f32[128,128]{1,0:T(8,128)S(1)}, f32[128,128]{1,0:T(8,128)S(1)}, u32[]{:S(2)}, u32[]{:S(2)}) collective-permute-start(f32[128,128]{1,0:T(8,128)S(1)} %slice.35), channel_id=1, source_target_pairs={{0,4},{2,0},{4,8},{6,2},{8,12},{10,6},{12,16},{14,10},{16,20},{18,... | collective-permute-start | bytes 196616 | tf_op jit(solution)/shard_map/ppermute | solution.py:555
  26.2 0.0 collective-permute-done.7
  26.2 1.5 %collective-permute-done.6 = f32[88,128]{1,0:T(8,128)S(1)} collective-permute-done((f32[88,128]{1,0:T(8,128)S(1)}, f32[88,128]{1,0:T(8,128)S(1)}, u32[]{:S(2)}, u32[]{:S(2)}) %collective-permute-start.6) | collective-permute-done | bytes 45088 | tf_op jit(solution)/shard_map/ppermute | solution.py:427
  27.7 0.0 collective-permute-done.5
  27.7 2.7 %collective-permute-start.10 = (f32[88,128]{1,0:T(8,128)S(1)}, f32[88,128]{1,0:T(8,128)S(1)}, u32[]{:S(2)}, u32[]{:S(2)}) collective-permute-start(f32[88,128]{1,0:T(8,128)S(1)} %fusion), channel_id=1, source_target_pairs={{0,24},{1,25},{2,26},{3,27},{4,28},{5,29},{6,30},{7,31},{8,16},{9,... | collective-permute-start | bytes 135176 | tf_op jit(solution)/shard_map/ppermute | solution.py:427
  30.4 0.4 collective-permute-start.9
  30.8 1.3 %collective-permute-start.8 = (f32[88,128]{1,0:T(8,128)S(1)}, f32[88,128]{1,0:T(8,128)S(1)}, u32[]{:S(2)}, u32[]{:S(2)}) collective-permute-start(f32[88,128]{1,0:T(8,128)S(1)} %fusion), channel_id=1, source_target_pairs={{0,8},{1,9},{2,10},{3,11},{4,12},{5,13},{6,14},{7,15},{8,0},{9,1},... | collective-permute-start | bytes 135176 | tf_op jit(solution)/shard_map/ppermute | solution.py:427
  32.2 0.0 collective-permute-done.11.ringed
  32.2 1.3 %grad_input.1 = f32[256,128]{1,0:T(8,128)} custom-call(f32[320,128]{1,0:T(8,128)S(1)} %get-tuple-element.56.own, f32[192,128]{1,0:T(8,128)S(1)} %slice.34.swapped, f32[128,128]{1,0:T(8,128)S(1)} %collective-permute-done.11.ringed, bf16[384,1152]{1,0:T(8,128)(2,1)S(1)} %get-tuple-element.47.refs_6_.backward), custom_call_target="tpu_custom_call" | custom-call | flops 600000000 | bytes 1000000 | tf_op jit(solution)/shard_map/grad_input/pallas_call | solution.py:556
  33.5 0.2 collective-permute-done.10
  33.6 2.2 %collective-permute-done.9 = f32[88,128]{1,0:T(8,128)S(1)} collective-permute-done((f32[88,128]{1,0:T(8,128)S(1)}, f32[88,128]{1,0:T(8,128)S(1)}, u32[]{:S(2)}, u32[]{:S(2)}) %collective-permute-start.9) | collective-permute-done | bytes 45088 | tf_op jit(solution)/shard_map/ppermute | solution.py:427
  35.8 0.0 collective-permute-done.8
  35.8 1.1 %collective-permute-start.14 = (f32[88,128]{1,0:T(8,128)S(1)}, f32[88,128]{1,0:T(8,128)S(1)}, u32[]{:S(2)}, u32[]{:S(2)}) collective-permute-start(f32[88,128]{1,0:T(8,128)S(1)} %add_add_fusion), channel_id=1, source_target_pairs={{0,5},{1,4},{2,7},{3,6},{4,1},{5,0},{6,3},{7,2},{8,13},{9,12},{10,... | collective-permute-start | bytes 135176 | tf_op jit(solution)/shard_map/ppermute | solution.py:427
  36.9 1.3 %collective-permute-start.13 = (f32[88,128]{1,0:T(8,128)S(1)}, f32[88,128]{1,0:T(8,128)S(1)}, u32[]{:S(2)}, u32[]{:S(2)}) collective-permute-start(f32[88,128]{1,0:T(8,128)S(1)} %add_add_fusion), channel_id=1, source_target_pairs={{0,4},{1,5},{2,6},{3,7},{4,0},{5,1},{6,2},{7,3},{8,12},{9,13},{10,... | collective-permute-start | bytes 135176 | tf_op jit(solution)/shard_map/ppermute | solution.py:427
  38.2 1.2 %collective-permute-start.12 = (f32[88,128]{1,0:T(8,128)S(1)}, f32[88,128]{1,0:T(8,128)S(1)}, u32[]{:S(2)}, u32[]{:S(2)}) collective-permute-start(f32[88,128]{1,0:T(8,128)S(1)} %add_add_fusion), channel_id=1, source_target_pairs={{0,1},{1,0},{2,3},{3,2},{4,5},{5,4},{6,7},{7,6},{8,9},{9,8},{10,11... | collective-permute-start | bytes 135176 | tf_op jit(solution)/shard_map/ppermute | solution.py:427
  39.4 2.8 %collective-permute-done.12 = f32[88,128]{1,0:T(8,128)S(1)} collective-permute-done((f32[88,128]{1,0:T(8,128)S(1)}, f32[88,128]{1,0:T(8,128)S(1)}, u32[]{:S(2)}, u32[]{:S(2)}) %collective-permute-start.12) | collective-permute-done | bytes 45088 | tf_op jit(solution)/shard_map/ppermute | solution.py:427
  42.2 0.0 collective-permute-done.13
  42.3 0.0 collective-permute-done.14
  42.3 0.1 collective-permute-start.15
  42.4 1.4 %collective-permute-done.15.other = f32[352,128]{1,0:T(8,128)S(1)} collective-permute-done((f32[352,128]{1,0:T(8,128)S(1)}, f32[352,128]{1,0:T(8,128)S(1)}, u32[]{:S(2)}, u32[]{:S(2)}) %collective-permute-start.15) | collective-permute-done | bytes 180256 | tf_op jit(solution)/shard_map/ppermute | solution.py:427
  43.8 1.2 %unpack.1 = (f32[27,32,32]{2,1,0:T(8,128)}, f32[27,32,32]{2,1,0:T(8,128)}, f32[27,32,32]{2,1,0:T(8,128)}) custom-call(f32[352,128]{1,0:T(8,128)S(1)} %constant_dynamic-update-slice_fusion.mine, f32[352,128]{1,0:T(8,128)S(1)} %collective-permute-done.15.other), custom_call_target="tpu_custom_call" | custom-call | tf_op jit(solution)/shard_map/unpack/pallas_call | solution.py:568
  (10 shorter events, 0.1 us)
Async XLA Ops:
  1.8 2.1 %collective-permute-start = (f32[1024,128]{1,0:T(8,128)S(1)}, f32[1024,128]{1,0:T(8,128)S(1)}, u32[]{:S(2)}, u32[]{:S(2)}) collective-permute-start(f32[1024,128]{1,0:T(8,128)S(1)} %fetch.1.local.refs_0_), channel_id=1, source_target_pairs={{0,2},{2,0},{4,6},{6,4},{8,10},{10,8},{12,14},{14,12},{16,18},{18,... | collective-permute-start | bytes 1572872 | tf_op jit(solution)/shard_map/ppermute | solution.py:472
  3.9 10.3 %collective-permute-start.1 = (f32[512,128]{1,0:T(8,128)S(1)}, f32[512,128]{1,0:T(8,128)S(1)}, u32[]{:S(2)}, u32[]{:S(2)}) collective-permute-start(f32[512,128]{1,0:T(8,128)S(1)} %pack_rows.1), channel_id=1, source_target_pairs={{0,4},{2,0},{4,8},{6,2},{8,12},{10,6},{12,16},{14,10},{16,20},{18,... | collective-permute-start | bytes 786440 | tf_op jit(solution)/shard_map/ppermute | solution.py:520
  7.2 4.7 %collective-permute-start.2 = (f32[128,128]{1,0:T(8,128)S(1)}, f32[128,128]{1,0:T(8,128)S(1)}, u32[]{:S(2)}, u32[]{:S(2)}) collective-permute-start(f32[128,128]{1,0:T(8,128)S(1)} %get-tuple-element.41), channel_id=1, source_target_pairs={{0,1},{1,0},{2,3},{3,2},{4,5},{5,4},{6,7},{7,6},{8,9},{9,8},{10,11... | collective-permute-start | bytes 196616 | tf_op jit(solution)/shard_map/ppermute | solution.py:522
  8.7 4.8 %collective-permute-start.3 = (f32[64,128]{1,0:T(8,128)S(1)}, f32[64,128]{1,0:T(8,128)S(1)}, u32[]{:S(2)}, u32[]{:S(2)}) collective-permute-start(f32[64,128]{1,0:T(8,128)S(1)} %get-tuple-element.42), channel_id=1, source_target_pairs={{0,5},{1,4},{2,1},{3,0},{4,9},{5,8},{6,3},{7,2},{8,13},{9,12},{10,... | collective-permute-start | bytes 98312 | tf_op jit(solution)/shard_map/ppermute | solution.py:521
  18.4 1.6 %collective-permute-start.4 = (f32[544,128]{1,0:T(8,128)S(1)}, f32[544,128]{1,0:T(8,128)S(1)}, u32[]{:S(2)}, u32[]{:S(2)}) collective-permute-start(f32[544,128]{1,0:T(8,128)S(1)} %get-tuple-element.55), channel_id=1, source_target_pairs={{0,2},{1,3},{2,0},{3,1},{4,6},{5,7},{6,4},{7,5},{8,10},{9,11},{10,... | collective-permute-start | bytes 835592 | tf_op jit(solution)/shard_map/ppermute | solution.py:427
  20.1 6.1 %collective-permute-start.7 = (f32[88,128]{1,0:T(8,128)S(1)}, f32[88,128]{1,0:T(8,128)S(1)}, u32[]{:S(2)}, u32[]{:S(2)}) collective-permute-start(f32[88,128]{1,0:T(8,128)S(1)} %get-tuple-element.62), channel_id=1, source_target_pairs={{0,5},{1,4},{2,7},{3,6},{4,1},{5,0},{6,3},{7,2},{8,13},{9,12},{10,... | collective-permute-start | bytes 135176 | tf_op jit(solution)/shard_map/ppermute | solution.py:427
  23.6 4.1 %collective-permute-start.6 = (f32[88,128]{1,0:T(8,128)S(1)}, f32[88,128]{1,0:T(8,128)S(1)}, u32[]{:S(2)}, u32[]{:S(2)}) collective-permute-start(f32[88,128]{1,0:T(8,128)S(1)} %get-tuple-element.63), channel_id=1, source_target_pairs={{0,4},{1,5},{2,6},{3,7},{4,0},{5,1},{6,2},{7,3},{8,12},{9,13},{10,... | collective-permute-start | bytes 135176 | tf_op jit(solution)/shard_map/ppermute | solution.py:427
  23.6 4.1 %collective-permute-start.5 = (f32[88,128]{1,0:T(8,128)S(1)}, f32[88,128]{1,0:T(8,128)S(1)}, u32[]{:S(2)}, u32[]{:S(2)}) collective-permute-start(f32[88,128]{1,0:T(8,128)S(1)} %get-tuple-element.64), channel_id=1, source_target_pairs={{0,1},{1,0},{2,3},{3,2},{4,5},{5,4},{6,7},{7,6},{8,9},{9,8},{10,11... | collective-permute-start | bytes 135176 | tf_op jit(solution)/shard_map/ppermute | solution.py:427
  24.2 7.9 %collective-permute-start.11 = (f32[128,128]{1,0:T(8,128)S(1)}, f32[128,128]{1,0:T(8,128)S(1)}, u32[]{:S(2)}, u32[]{:S(2)}) collective-permute-start(f32[128,128]{1,0:T(8,128)S(1)} %slice.35), channel_id=1, source_target_pairs={{0,4},{2,0},{4,8},{6,2},{8,12},{10,6},{12,16},{14,10},{16,20},{18,... | collective-permute-start | bytes 196616 | tf_op jit(solution)/shard_map/ppermute | solution.py:555
  27.7 5.9 %collective-permute-start.10 = (f32[88,128]{1,0:T(8,128)S(1)}, f32[88,128]{1,0:T(8,128)S(1)}, u32[]{:S(2)}, u32[]{:S(2)}) collective-permute-start(f32[88,128]{1,0:T(8,128)S(1)} %fusion), channel_id=1, source_target_pairs={{0,24},{1,25},{2,26},{3,27},{4,28},{5,29},{6,30},{7,31},{8,16},{9,... | collective-permute-start | bytes 135176 | tf_op jit(solution)/shard_map/ppermute | solution.py:427
  30.4 5.4 %collective-permute-start.9 = (f32[88,128]{1,0:T(8,128)S(1)}, f32[88,128]{1,0:T(8,128)S(1)}, u32[]{:S(2)}, u32[]{:S(2)}) collective-permute-start(f32[88,128]{1,0:T(8,128)S(1)} %fusion), channel_id=1, source_target_pairs={{0,16},{1,17},{2,18},{3,19},{4,20},{5,21},{6,22},{7,23},{8,24},{9,... | collective-permute-start | bytes 135176 | tf_op jit(solution)/shard_map/ppermute | solution.py:427
  30.8 5.0 %collective-permute-start.8 = (f32[88,128]{1,0:T(8,128)S(1)}, f32[88,128]{1,0:T(8,128)S(1)}, u32[]{:S(2)}, u32[]{:S(2)}) collective-permute-start(f32[88,128]{1,0:T(8,128)S(1)} %fusion), channel_id=1, source_target_pairs={{0,8},{1,9},{2,10},{3,11},{4,12},{5,13},{6,14},{7,15},{8,0},{9,1},... | collective-permute-start | bytes 135176 | tf_op jit(solution)/shard_map/ppermute | solution.py:427
  35.8 6.4 %collective-permute-start.14 = (f32[88,128]{1,0:T(8,128)S(1)}, f32[88,128]{1,0:T(8,128)S(1)}, u32[]{:S(2)}, u32[]{:S(2)}) collective-permute-start(f32[88,128]{1,0:T(8,128)S(1)} %add_add_fusion), channel_id=1, source_target_pairs={{0,5},{1,4},{2,7},{3,6},{4,1},{5,0},{6,3},{7,2},{8,13},{9,12},{10,... | collective-permute-start | bytes 135176 | tf_op jit(solution)/shard_map/ppermute | solution.py:427
  36.9 5.4 %collective-permute-start.13 = (f32[88,128]{1,0:T(8,128)S(1)}, f32[88,128]{1,0:T(8,128)S(1)}, u32[]{:S(2)}, u32[]{:S(2)}) collective-permute-start(f32[88,128]{1,0:T(8,128)S(1)} %add_add_fusion), channel_id=1, source_target_pairs={{0,4},{1,5},{2,6},{3,7},{4,0},{5,1},{6,2},{7,3},{8,12},{9,13},{10,... | collective-permute-start | bytes 135176 | tf_op jit(solution)/shard_map/ppermute | solution.py:427
  38.2 4.0 %collective-permute-start.12 = (f32[88,128]{1,0:T(8,128)S(1)}, f32[88,128]{1,0:T(8,128)S(1)}, u32[]{:S(2)}, u32[]{:S(2)}) collective-permute-start(f32[88,128]{1,0:T(8,128)S(1)} %add_add_fusion), channel_id=1, source_target_pairs={{0,1},{1,0},{2,3},{3,2},{4,5},{5,4},{6,7},{7,6},{8,9},{9,8},{10,11... | collective-permute-start | bytes 135176 | tf_op jit(solution)/shard_map/ppermute | solution.py:427
  42.3 1.5 %collective-permute-start.15 = (f32[352,128]{1,0:T(8,128)S(1)}, f32[352,128]{1,0:T(8,128)S(1)}, u32[]{:S(2)}, u32[]{:S(2)}) collective-permute-start(f32[352,128]{1,0:T(8,128)S(1)} %constant_dynamic-update-slice_fusion.mine), channel_id=1, source_target_pairs={{0,2},{1,3},{2,0},{3,1},{4,6},{5,7},{6,4},{7,5},{8,10},{9,11},{10,... | collective-permute-start | bytes 540680 | tf_op jit(solution)/shard_map/ppermute | solution.py:427

commit v8 on v7

--- a/solution.py
+++ b/solution.py
@@ -149,8 +149,8 @@
 
 def conv_rows(weights, layer, source, low, high):
     out = {}
-    for e in range(low, high, 2):
-        count = min(2, high - e)
+    for e in range(low, high, 4):
+        count = min(4, high - e)
         window = [source[:, pl.ds((e + b - 1) * LANES, count * LANES)] for b in range(3)]
         value = conv(weights, layer, jnp.concatenate(window, axis=0))
         for k in range(count):

time: 45.2 us -> 45.2 us (level)
  no operation moved by 1% of the time
where the time goes in v8:
time: 45.2 us; the launch traced here: 45 us
  starting transfers between devices  20.7 us (46%)
  Pallas kernels  12.9 us (29%)
  waiting for transfers between devices  10.6 us (23%)
  between operations  0.77 us (2%)
    ppermute x11, starting transfers between devices, swap(): return lax.ppermute(value, axes, [(i, i ^ bits) for i in range(total)])  12.3 us
    ppermute x11, waiting for transfers between devices, swap(): return lax.ppermute(value, axes, [(i, i ^ bits) for i in range(total)])  9.67 us
    pallas_call x1, Pallas kernels, per_device(): pl.pallas_call(functools.partial(layers_kernel, depth, rows, channels, le...  4.21 us
    ppermute x1, starting transfers between devices, per_device(): outer = lax.ppermute(outer, 'gx', across)  2.94 us
    ppermute x1, starting transfers between devices, input_gradient(): ringed = lax.ppermute(swapped[planes:], 'gx', across)  1.92 us
    pallas_call x1, Pallas kernels, per_device(): pl.pallas_call(functools.partial(early_kernel, depth, rows), out_shape=[s...  1.69 us
    pallas_call x1, Pallas kernels, per_device(): pl.pallas_call(functools.partial(weight_kernel, channels, depth), out_sha...  1.63 us
    ppermute x1, starting transfers between devices, per_device(): strips = [lax.ppermute(strips, 'gy', pairs) for pairs in y_rounds]  1.56 us
  transfers between devices with their start and end apart: 16, of which 8 were waited for; matrix products, arithmetic and copies ran while one was open for 0% of the time, Pallas kernels for 14%

profile of v8, /device:TPU:0, one launch (start us, length us, event | category | flops | bytes accessed | tf_op | source)
XLA Modules:
  0.0 45.0 jit_solution(2472665501998288948)
XLA Ops:
  0.6 1.1 %fetch.1.local.refs_0_ = f32[1024,128]{1,0:T(8,128)S(1)} custom-call(f32[256,128]{1,0:T(8,128)} %bitcast.5, f32[256,128]{1,0:T(8,128)} %bitcast.6, f32[256,128]{1,0:T(8,128)} %bitcast.7, f32[256,128]{1,0:T(8,128)} %bitcast.8), custom_call_target="tpu_custom_call" | custom-call | tf_op jit(solution)/shard_map/fetch/pallas_call | solution.py:462
  1.8 0.5 %collective-permute-start = (f32[1024,128]{1,0:T(8,128)S(1)}, f32[1024,128]{1,0:T(8,128)S(1)}, u32[]{:S(2)}, u32[]{:S(2)}) collective-permute-start(f32[1024,128]{1,0:T(8,128)S(1)} %fetch.1.local.refs_0_), channel_id=1, source_target_pairs={{0,2},{2,0},{4,6},{6,4},{8,10},{10,8},{12,14},{14,12},{16,18},{18,... | collective-permute-start | bytes 1572872 | tf_op jit(solution)/shard_map/ppermute | solution.py:472
  2.3 1.3 %fetch_kernels.1 = (f32[27,32,32]{2,1,0:T(8,128)S(1)}, f32[27,32,32]{2,1,0:T(8,128)S(1)}, f32[27,32,32]{2,1,0:T(8,128)S(1)}) custom-call(f32[27,32,32]{2,1,0:T(8,128)} %refs_0_.1, f32[27,32,32]{2,1,0:T(8,128)} %refs_1_.1, f32[27,32,32]{2,1,0:T(8,128)} %refs_2_.1), custom_call_target="tpu_custom_call" | custom-call | bytes 4000000 | tf_op jit(solution)/shard_map/fetch_kernels/pallas_call | solution.py:473
  3.6 0.2 collective-permute-done.sibling.refs_1_
  3.8 0.1 pack_rows.1
  3.9 2.9 %collective-permute-start.1 = (f32[512,128]{1,0:T(8,128)S(1)}, f32[512,128]{1,0:T(8,128)S(1)}, u32[]{:S(2)}, u32[]{:S(2)}) collective-permute-start(f32[512,128]{1,0:T(8,128)S(1)} %pack_rows.1), channel_id=1, source_target_pairs={{0,4},{2,0},{4,8},{6,2},{8,12},{10,6},{12,16},{14,10},{16,20},{18,... | collective-permute-start | bytes 786440 | tf_op jit(solution)/shard_map/ppermute | solution.py:520
  6.8 0.3 pack_strips.1
  7.2 1.6 %collective-permute-start.2 = (f32[128,128]{1,0:T(8,128)S(1)}, f32[128,128]{1,0:T(8,128)S(1)}, u32[]{:S(2)}, u32[]{:S(2)}) collective-permute-start(f32[128,128]{1,0:T(8,128)S(1)} %get-tuple-element.41), channel_id=1, source_target_pairs={{0,1},{1,0},{2,3},{3,2},{4,5},{5,4},{6,7},{7,6},{8,9},{9,8},{10,11... | collective-permute-start | bytes 196616 | tf_op jit(solution)/shard_map/ppermute | solution.py:522
  8.7 1.5 %collective-permute-start.3 = (f32[64,128]{1,0:T(8,128)S(1)}, f32[64,128]{1,0:T(8,128)S(1)}, u32[]{:S(2)}, u32[]{:S(2)}) collective-permute-start(f32[64,128]{1,0:T(8,128)S(1)} %get-tuple-element.42), channel_id=1, source_target_pairs={{0,5},{1,4},{2,1},{3,0},{4,9},{5,8},{6,3},{7,2},{8,13},{9,12},{10,... | collective-permute-start | bytes 98312 | tf_op jit(solution)/shard_map/ppermute | solution.py:521
  10.2 1.6 %weights.1 = (bf16[384,1152]{1,0:T(8,128)(2,1)S(1)}, bf16[384,1152]{1,0:T(8,128)(2,1)S(1)}) custom-call(f32[27,32,32]{2,1,0:T(8,128)S(1)} %get-tuple-element.43.refs_0_, f32[27,32,32]{2,1,0:T(8,128)S(1)} %get-tuple-element.44.refs_1_, f32[27,32,32]{2,1,0:T(8,128)S(1)} %get-tuple-element.45.refs_2_), custom_call_target="tpu_custom_call" | custom-call | flops 20000000 | bytes 4000000 | tf_op jit(solution)/shard_map/weights/pallas_call | solution.py:507
  11.9 0.0 collective-permute-done.2.refs_2_.refs_3_
  11.9 1.7 %early.1 = (bf16[384,1536]{1,0:T(8,128)(2,1)S(1)}, bf16[384,1536]{1,0:T(8,128)(2,1)S(1)}, bf16[384,1536]{1,0:T(8,128)(2,1)S(1)}, f32[64,128]{1,0:T(8,128)S(1)}, ...) custom-call(f32[1024,128]{1,0:T(8,128)S(1)} %fetch.1.local.refs_0_, f32[1024,128]{1,0:T(8,128)S(1)} %collective-permute-done.sibling.refs_1_, ...), custom_call_target="tpu_custom_call" | custom-call | flops 20000000 | bytes 6000000 | tf_op jit(solution)/shard_map/early/pallas_call | solution.py:527
  13.6 0.0 collective-permute-done.3.refs_4_
  13.6 0.7 %collective-permute-done.1.refs_2_ = f32[512,128]{1,0:T(8,128)S(1)} collective-permute-done((f32[512,128]{1,0:T(8,128)S(1)}, f32[512,128]{1,0:T(8,128)S(1)}, u32[]{:S(2)}, u32[]{:S(2)}) %collective-permute-start.1) | collective-permute-done | bytes 262176 | tf_op jit(solution)/shard_map/ppermute | solution.py:520
  14.2 4.2 %layers.1 = (f32[320,128]{1,0:T(8,128)S(1)}, f32[352,128]{1,0:T(8,128)S(1)}, f32[544,128]{1,0:T(8,128)S(1)}, bf16[384,1536]{1,0:T(8,128)(2,1)S(1)}, bf16[384,153...) custom-call(f32[1024,128]{1,0:T(8,128)S(1)} %fetch.1.local.refs_0_, ...), custom_call_target="tpu_custom_call", output_to_operand_aliasing={{3}: (10, {}), {4}: (11, {}), {5}: (12, {})} | custom-call | tf_op jit(solution)/shard_map/layers/pallas_call | solution.py:538
  18.4 0.1 collective-permute-start.4
  18.5 1.5 %collective-permute-done.4 = f32[544,128]{1,0:T(8,128)S(1)} collective-permute-done((f32[544,128]{1,0:T(8,128)S(1)}, f32[544,128]{1,0:T(8,128)S(1)}, u32[]{:S(2)}, u32[]{:S(2)}) %collective-permute-start.4) | collective-permute-done | bytes 278560 | tf_op jit(solution)/shard_map/ppermute | solution.py:427
  20.1 3.5 %collective-permute-start.7 = (f32[88,128]{1,0:T(8,128)S(1)}, f32[88,128]{1,0:T(8,128)S(1)}, u32[]{:S(2)}, u32[]{:S(2)}) collective-permute-start(f32[88,128]{1,0:T(8,128)S(1)} %get-tuple-element.62), channel_id=1, source_target_pairs={{0,5},{1,4},{2,7},{3,6},{4,1},{5,0},{6,3},{7,2},{8,13},{9,12},{10,... | collective-permute-start | bytes 135176 | tf_op jit(solution)/shard_map/ppermute | solution.py:427
  23.6 0.0 collective-permute-start.6
  23.6 0.6 %collective-permute-start.5 = (f32[88,128]{1,0:T(8,128)S(1)}, f32[88,128]{1,0:T(8,128)S(1)}, u32[]{:S(2)}, u32[]{:S(2)}) collective-permute-start(f32[88,128]{1,0:T(8,128)S(1)} %get-tuple-element.64), channel_id=1, source_target_pairs={{0,1},{1,0},{2,3},{3,2},{4,5},{5,4},{6,7},{7,6},{8,9},{9,8},{10,11... | collective-permute-start | bytes 135176 | tf_op jit(solution)/shard_map/ppermute | solution.py:427
  24.2 1.9 %collective-permute-start.11 = (f32[128,128]{1,0:T(8,128)S(1)}, f32[128,128]{1,0:T(8,128)S(1)}, u32[]{:S(2)}, u32[]{:S(2)}) collective-permute-start(f32[128,128]{1,0:T(8,128)S(1)} %slice.35), channel_id=1, source_target_pairs={{0,4},{2,0},{4,8},{6,2},{8,12},{10,6},{12,16},{14,10},{16,20},{18,... | collective-permute-start | bytes 196616 | tf_op jit(solution)/shard_map/ppermute | solution.py:555
  26.2 0.0 collective-permute-done.7
  26.2 1.5 %collective-permute-done.6 = f32[88,128]{1,0:T(8,128)S(1)} collective-permute-done((f32[88,128]{1,0:T(8,128)S(1)}, f32[88,128]{1,0:T(8,128)S(1)}, u32[]{:S(2)}, u32[]{:S(2)}) %collective-permute-start.6) | collective-permute-done | bytes 45088 | tf_op jit(solution)/shard_map/ppermute | solution.py:427
  27.7 0.0 collective-permute-done.5
  27.7 2.7 %collective-permute-start.10 = (f32[88,128]{1,0:T(8,128)S(1)}, f32[88,128]{1,0:T(8,128)S(1)}, u32[]{:S(2)}, u32[]{:S(2)}) collective-permute-start(f32[88,128]{1,0:T(8,128)S(1)} %fusion), channel_id=1, source_target_pairs={{0,24},{1,25},{2,26},{3,27},{4,28},{5,29},{6,30},{7,31},{8,16},{9,... | collective-permute-start | bytes 135176 | tf_op jit(solution)/shard_map/ppermute | solution.py:427
  30.4 0.4 collective-permute-start.9
  30.8 1.3 %collective-permute-start.8 = (f32[88,128]{1,0:T(8,128)S(1)}, f32[88,128]{1,0:T(8,128)S(1)}, u32[]{:S(2)}, u32[]{:S(2)}) collective-permute-start(f32[88,128]{1,0:T(8,128)S(1)} %fusion), channel_id=1, source_target_pairs={{0,8},{1,9},{2,10},{3,11},{4,12},{5,13},{6,14},{7,15},{8,0},{9,1},... | collective-permute-start | bytes 135176 | tf_op jit(solution)/shard_map/ppermute | solution.py:427
  32.2 0.0 collective-permute-done.11.ringed
  32.2 1.3 %grad_input.1 = f32[256,128]{1,0:T(8,128)} custom-call(f32[320,128]{1,0:T(8,128)S(1)} %get-tuple-element.56.own, f32[192,128]{1,0:T(8,128)S(1)} %slice.34.swapped, f32[128,128]{1,0:T(8,128)S(1)} %collective-permute-done.11.ringed, bf16[384,1152]{1,0:T(8,128)(2,1)S(1)} %get-tuple-element.47.refs_6_.backward), custom_call_target="tpu_custom_call" | custom-call | flops 600000000 | bytes 1000000 | tf_op jit(solution)/shard_map/grad_input/pallas_call | solution.py:556
  33.5 0.2 collective-permute-done.10
  33.6 2.2 %collective-permute-done.9 = f32[88,128]{1,0:T(8,128)S(1)} collective-permute-done((f32[88,128]{1,0:T(8,128)S(1)}, f32[88,128]{1,0:T(8,128)S(1)}, u32[]{:S(2)}, u32[]{:S(2)}) %collective-permute-start.9) | collective-permute-done | bytes 45088 | tf_op jit(solution)/shard_map/ppermute | solution.py:427
  35.8 0.0 collective-permute-done.8
  35.8 1.1 %collective-permute-start.14 = (f32[88,128]{1,0:T(8,128)S(1)}, f32[88,128]{1,0:T(8,128)S(1)}, u32[]{:S(2)}, u32[]{:S(2)}) collective-permute-start(f32[88,128]{1,0:T(8,128)S(1)} %add_add_fusion), channel_id=1, source_target_pairs={{0,5},{1,4},{2,7},{3,6},{4,1},{5,0},{6,3},{7,2},{8,13},{9,12},{10,... | collective-permute-start | bytes 135176 | tf_op jit(solution)/shard_map/ppermute | solution.py:427
  36.9 1.3 %collective-permute-start.13 = (f32[88,128]{1,0:T(8,128)S(1)}, f32[88,128]{1,0:T(8,128)S(1)}, u32[]{:S(2)}, u32[]{:S(2)}) collective-permute-start(f32[88,128]{1,0:T(8,128)S(1)} %add_add_fusion), channel_id=1, source_target_pairs={{0,4},{1,5},{2,6},{3,7},{4,0},{5,1},{6,2},{7,3},{8,12},{9,13},{10,... | collective-permute-start | bytes 135176 | tf_op jit(solution)/shard_map/ppermute | solution.py:427
  38.2 1.2 %collective-permute-start.12 = (f32[88,128]{1,0:T(8,128)S(1)}, f32[88,128]{1,0:T(8,128)S(1)}, u32[]{:S(2)}, u32[]{:S(2)}) collective-permute-start(f32[88,128]{1,0:T(8,128)S(1)} %add_add_fusion), channel_id=1, source_target_pairs={{0,1},{1,0},{2,3},{3,2},{4,5},{5,4},{6,7},{7,6},{8,9},{9,8},{10,11... | collective-permute-start | bytes 135176 | tf_op jit(solution)/shard_map/ppermute | solution.py:427
  39.4 2.8 %collective-permute-done.12 = f32[88,128]{1,0:T(8,128)S(1)} collective-permute-done((f32[88,128]{1,0:T(8,128)S(1)}, f32[88,128]{1,0:T(8,128)S(1)}, u32[]{:S(2)}, u32[]{:S(2)}) %collective-permute-start.12) | collective-permute-done | bytes 45088 | tf_op jit(solution)/shard_map/ppermute | solution.py:427
  42.2 0.0 collective-permute-done.13
  42.3 0.0 collective-permute-done.14
  42.3 0.1 collective-permute-start.15
  42.4 1.4 %collective-permute-done.15.other = f32[352,128]{1,0:T(8,128)S(1)} collective-permute-done((f32[352,128]{1,0:T(8,128)S(1)}, f32[352,128]{1,0:T(8,128)S(1)}, u32[]{:S(2)}, u32[]{:S(2)}) %collective-permute-start.15) | collective-permute-done | bytes 180256 | tf_op jit(solution)/shard_map/ppermute | solution.py:427
  43.8 1.2 %unpack.1 = (f32[27,32,32]{2,1,0:T(8,128)}, f32[27,32,32]{2,1,0:T(8,128)}, f32[27,32,32]{2,1,0:T(8,128)}) custom-call(f32[352,128]{1,0:T(8,128)S(1)} %constant_dynamic-update-slice_fusion.mine, f32[352,128]{1,0:T(8,128)S(1)} %collective-permute-done.15.other), custom_call_target="tpu_custom_call" | custom-call | tf_op jit(solution)/shard_map/unpack/pallas_call | solution.py:568
  (10 shorter events, 0.1 us)
Async XLA Ops:
  1.8 2.1 %collective-permute-start = (f32[1024,128]{1,0:T(8,128)S(1)}, f32[1024,128]{1,0:T(8,128)S(1)}, u32[]{:S(2)}, u32[]{:S(2)}) collective-permute-start(f32[1024,128]{1,0:T(8,128)S(1)} %fetch.1.local.refs_0_), channel_id=1, source_target_pairs={{0,2},{2,0},{4,6},{6,4},{8,10},{10,8},{12,14},{14,12},{16,18},{18,... | collective-permute-start | bytes 1572872 | tf_op jit(solution)/shard_map/ppermute | solution.py:472
  3.9 10.3 %collective-permute-start.1 = (f32[512,128]{1,0:T(8,128)S(1)}, f32[512,128]{1,0:T(8,128)S(1)}, u32[]{:S(2)}, u32[]{:S(2)}) collective-permute-start(f32[512,128]{1,0:T(8,128)S(1)} %pack_rows.1), channel_id=1, source_target_pairs={{0,4},{2,0},{4,8},{6,2},{8,12},{10,6},{12,16},{14,10},{16,20},{18,... | collective-permute-start | bytes 786440 | tf_op jit(solution)/shard_map/ppermute | solution.py:520
  7.2 4.7 %collective-permute-start.2 = (f32[128,128]{1,0:T(8,128)S(1)}, f32[128,128]{1,0:T(8,128)S(1)}, u32[]{:S(2)}, u32[]{:S(2)}) collective-permute-start(f32[128,128]{1,0:T(8,128)S(1)} %get-tuple-element.41), channel_id=1, source_target_pairs={{0,1},{1,0},{2,3},{3,2},{4,5},{5,4},{6,7},{7,6},{8,9},{9,8},{10,11... | collective-permute-start | bytes 196616 | tf_op jit(solution)/shard_map/ppermute | solution.py:522
  8.7 4.8 %collective-permute-start.3 = (f32[64,128]{1,0:T(8,128)S(1)}, f32[64,128]{1,0:T(8,128)S(1)}, u32[]{:S(2)}, u32[]{:S(2)}) collective-permute-start(f32[64,128]{1,0:T(8,128)S(1)} %get-tuple-element.42), channel_id=1, source_target_pairs={{0,5},{1,4},{2,1},{3,0},{4,9},{5,8},{6,3},{7,2},{8,13},{9,12},{10,... | collective-permute-start | bytes 98312 | tf_op jit(solution)/shard_map/ppermute | solution.py:521
  18.4 1.6 %collective-permute-start.4 = (f32[544,128]{1,0:T(8,128)S(1)}, f32[544,128]{1,0:T(8,128)S(1)}, u32[]{:S(2)}, u32[]{:S(2)}) collective-permute-start(f32[544,128]{1,0:T(8,128)S(1)} %get-tuple-element.55), channel_id=1, source_target_pairs={{0,2},{1,3},{2,0},{3,1},{4,6},{5,7},{6,4},{7,5},{8,10},{9,11},{10,... | collective-permute-start | bytes 835592 | tf_op jit(solution)/shard_map/ppermute | solution.py:427
  20.1 6.1 %collective-permute-start.7 = (f32[88,128]{1,0:T(8,128)S(1)}, f32[88,128]{1,0:T(8,128)S(1)}, u32[]{:S(2)}, u32[]{:S(2)}) collective-permute-start(f32[88,128]{1,0:T(8,128)S(1)} %get-tuple-element.62), channel_id=1, source_target_pairs={{0,5},{1,4},{2,7},{3,6},{4,1},{5,0},{6,3},{7,2},{8,13},{9,12},{10,... | collective-permute-start | bytes 135176 | tf_op jit(solution)/shard_map/ppermute | solution.py:427
  23.6 4.1 %collective-permute-start.6 = (f32[88,128]{1,0:T(8,128)S(1)}, f32[88,128]{1,0:T(8,128)S(1)}, u32[]{:S(2)}, u32[]{:S(2)}) collective-permute-start(f32[88,128]{1,0:T(8,128)S(1)} %get-tuple-element.63), channel_id=1, source_target_pairs={{0,4},{1,5},{2,6},{3,7},{4,0},{5,1},{6,2},{7,3},{8,12},{9,13},{10,... | collective-permute-start | bytes 135176 | tf_op jit(solution)/shard_map/ppermute | solution.py:427
  23.6 4.1 %collective-permute-start.5 = (f32[88,128]{1,0:T(8,128)S(1)}, f32[88,128]{1,0:T(8,128)S(1)}, u32[]{:S(2)}, u32[]{:S(2)}) collective-permute-start(f32[88,128]{1,0:T(8,128)S(1)} %get-tuple-element.64), channel_id=1, source_target_pairs={{0,1},{1,0},{2,3},{3,2},{4,5},{5,4},{6,7},{7,6},{8,9},{9,8},{10,11... | collective-permute-start | bytes 135176 | tf_op jit(solution)/shard_map/ppermute | solution.py:427
  24.2 7.9 %collective-permute-start.11 = (f32[128,128]{1,0:T(8,128)S(1)}, f32[128,128]{1,0:T(8,128)S(1)}, u32[]{:S(2)}, u32[]{:S(2)}) collective-permute-start(f32[128,128]{1,0:T(8,128)S(1)} %slice.35), channel_id=1, source_target_pairs={{0,4},{2,0},{4,8},{6,2},{8,12},{10,6},{12,16},{14,10},{16,20},{18,... | collective-permute-start | bytes 196616 | tf_op jit(solution)/shard_map/ppermute | solution.py:555
  27.7 5.9 %collective-permute-start.10 = (f32[88,128]{1,0:T(8,128)S(1)}, f32[88,128]{1,0:T(8,128)S(1)}, u32[]{:S(2)}, u32[]{:S(2)}) collective-permute-start(f32[88,128]{1,0:T(8,128)S(1)} %fusion), channel_id=1, source_target_pairs={{0,24},{1,25},{2,26},{3,27},{4,28},{5,29},{6,30},{7,31},{8,16},{9,... | collective-permute-start | bytes 135176 | tf_op jit(solution)/shard_map/ppermute | solution.py:427
  30.4 5.4 %collective-permute-start.9 = (f32[88,128]{1,0:T(8,128)S(1)}, f32[88,128]{1,0:T(8,128)S(1)}, u32[]{:S(2)}, u32[]{:S(2)}) collective-permute-start(f32[88,128]{1,0:T(8,128)S(1)} %fusion), channel_id=1, source_target_pairs={{0,16},{1,17},{2,18},{3,19},{4,20},{5,21},{6,22},{7,23},{8,24},{9,... | collective-permute-start | bytes 135176 | tf_op jit(solution)/shard_map/ppermute | solution.py:427
  30.8 5.0 %collective-permute-start.8 = (f32[88,128]{1,0:T(8,128)S(1)}, f32[88,128]{1,0:T(8,128)S(1)}, u32[]{:S(2)}, u32[]{:S(2)}) collective-permute-start(f32[88,128]{1,0:T(8,128)S(1)} %fusion), channel_id=1, source_target_pairs={{0,8},{1,9},{2,10},{3,11},{4,12},{5,13},{6,14},{7,15},{8,0},{9,1},... | collective-permute-start | bytes 135176 | tf_op jit(solution)/shard_map/ppermute | solution.py:427
  35.8 6.4 %collective-permute-start.14 = (f32[88,128]{1,0:T(8,128)S(1)}, f32[88,128]{1,0:T(8,128)S(1)}, u32[]{:S(2)}, u32[]{:S(2)}) collective-permute-start(f32[88,128]{1,0:T(8,128)S(1)} %add_add_fusion), channel_id=1, source_target_pairs={{0,5},{1,4},{2,7},{3,6},{4,1},{5,0},{6,3},{7,2},{8,13},{9,12},{10,... | collective-permute-start | bytes 135176 | tf_op jit(solution)/shard_map/ppermute | solution.py:427
  36.9 5.4 %collective-permute-start.13 = (f32[88,128]{1,0:T(8,128)S(1)}, f32[88,128]{1,0:T(8,128)S(1)}, u32[]{:S(2)}, u32[]{:S(2)}) collective-permute-start(f32[88,128]{1,0:T(8,128)S(1)} %add_add_fusion), channel_id=1, source_target_pairs={{0,4},{1,5},{2,6},{3,7},{4,0},{5,1},{6,2},{7,3},{8,12},{9,13},{10,... | collective-permute-start | bytes 135176 | tf_op jit(solution)/shard_map/ppermute | solution.py:427
  38.2 4.0 %collective-permute-start.12 = (f32[88,128]{1,0:T(8,128)S(1)}, f32[88,128]{1,0:T(8,128)S(1)}, u32[]{:S(2)}, u32[]{:S(2)}) collective-permute-start(f32[88,128]{1,0:T(8,128)S(1)} %add_add_fusion), channel_id=1, source_target_pairs={{0,1},{1,0},{2,3},{3,2},{4,5},{5,4},{6,7},{7,6},{8,9},{9,8},{10,11... | collective-permute-start | bytes 135176 | tf_op jit(solution)/shard_map/ppermute | solution.py:427
  42.3 1.5 %collective-permute-start.15 = (f32[352,128]{1,0:T(8,128)S(1)}, f32[352,128]{1,0:T(8,128)S(1)}, u32[]{:S(2)}, u32[]{:S(2)}) collective-permute-start(f32[352,128]{1,0:T(8,128)S(1)} %constant_dynamic-update-slice_fusion.mine), channel_id=1, source_target_pairs={{0,2},{1,3},{2,0},{3,1},{4,6},{5,7},{6,4},{7,5},{8,10},{9,11},{10,... | collective-permute-start | bytes 540680 | tf_op jit(solution)/shard_map/ppermute | solution.py:427
